TPU v7x, 32 devices: a whole 2x2x4 slice. The times are simulated.
32 devices in a mesh: dp: 16 (over z, y, core), rows: 2 (over x).
Axes of the slice: x: 2, y: 2, z: 4, core: 2. Of those that a mesh axis runs over, the one named last changes fastest.
Arguments:
- latents: bfloat16 [16, 32, 32, 640], P('dp', 'rows'), may hold values from -6 to 6
- target: bfloat16 [16, 32, 32, 640], P('dp', 'rows'), may hold values from -6 to 6
- weight: float32 [9, 640, 640], P(None, 'rows', 'dp'), may hold values from -0.078125 to 0.078125
- moment1: float32 [9, 640, 640], P(None, 'rows', 'dp'), may hold values from -6 to 6
- moment2: float32 [9, 640, 640], P(None, 'rows', 'dp'), may hold values from 0.5 to 4
Outputs:
- student: bfloat16 [16, 32, 32, 640], P('dp', 'rows')
- input_grad: bfloat16 [16, 32, 32, 640], P('dp', 'rows')
- new_weight: float32 [9, 640, 640], P(None, 'rows', 'dp')
- new_moment1: float32 [9, 640, 640], P(None, 'rows', 'dp')
- new_moment2: float32 [9, 640, 640], P(None, 'rows', 'dp')
All inputs are finite; a program needn't handle non-finite values.
Results may differ from a plain program's by a relative error of at most 0.009.
Values may be sent and summed in bfloat16 or wider, within the bound.
No kernel may reach another device: no remote copies, remote signals or barrier semaphores. Data moves between devices by JAX's collectives and lax.ppermute only.
A program may use at most 128 MiB of HBM per device.

v0:
```python
import jax
import jax.numpy as jnp
from jax import lax
from jax.sharding import PartitionSpec as P


def padded_2(cells, sides, width):
    for axis, dim in sides:
        count = lax.axis_size(axis)
        ends = count - 1
        head = lax.slice_in_dim(cells, 0, width, axis=dim)
        tail = lax.slice_in_dim(cells, cells.shape[dim] - width, cells.shape[dim], axis=dim)
        cells = jnp.concatenate(
            [
                lax.ppermute(tail, axis, [(i, (i + 1) % count) for i in range(ends)]),
                cells,
                lax.ppermute(head, axis, [((i + 1) % count, i) for i in range(ends)]),
            ],
            axis=dim,
        )
    return cells


def forward_cells(padded, kernel, band, width):
    total = None
    for tap in range(9):
        a, c = divmod(tap, 3)
        term = jnp.einsum(
            "bhwc,cn->bhwn",
            padded[:, a : a + band, c : c + width],
            kernel[tap],
            preferred_element_type=jnp.float32,
        )
        total = term if total is None else total + term
    return total


def backward_cells(error_pad, kernel, band, width):
    total = None
    for tap in range(9):
        a, c = divmod(tap, 3)
        window = error_pad[:, 2 - a : 2 - a + band, 2 - c : 2 - c + width]
        term = jnp.einsum("bhwn,cn->bhwc", window, kernel[tap], preferred_element_type=jnp.float32)
        total = term if total is None else total + term
    return total


def band_partial(padded, error, band, width):
    pieces = []
    for tap in range(9):
        a, c = divmod(tap, 3)
        window = padded[:, a : a + band, c : c + width]
        pieces.append(
            jnp.einsum("bhwc,bhwn->cn", window, error, preferred_element_type=jnp.float32)
        )
    return lax.optimization_barrier(jnp.stack(pieces).astype(jnp.bfloat16)).astype(jnp.float32)


def per_device(latents, target, weight, moment1, moment2):
    band = latents.shape[1]
    width = latents.shape[2]
    channels = latents.shape[3]
    side_pad = ((0, 0), (0, 0), (1, 1), (0, 0))
    kernel_part = lax.all_gather(weight.astype(jnp.bfloat16), "rows", axis=1, tiled=True)
    padded = padded_2(latents, (("rows", 1),), 1)
    padded = jnp.pad(padded, side_pad)
    kernel = lax.all_gather(kernel_part, "dp", axis=2, tiled=True)
    student = forward_cells(padded, kernel, band, width).astype(jnp.bfloat16)
    error = (student.astype(jnp.float32) - target.astype(jnp.float32)).astype(jnp.bfloat16)
    error_pad = padded_2(error, (("rows", 1),), 1)
    error_pad = jnp.pad(error_pad, side_pad)
    input_grad = backward_cells(error_pad, kernel, band, width).astype(jnp.bfloat16)
    band_count = lax.axis_size("rows")
    narrow = channels // band_count
    spread = lax.all_to_all(padded, "rows", split_axis=3, concat_axis=1, tiled=True)
    errors_all = lax.all_gather(error, "rows", axis=1, tiled=True)

    def band_step(index, running):
        rows_input = lax.dynamic_slice_in_dim(spread, index * (band + 2), band + 2, 1)
        rows_error = lax.dynamic_slice_in_dim(errors_all, index * band, band, 1)
        return running + band_partial(rows_input, rows_error, band, width)

    banded = lax.fori_loop(0, band_count, band_step, jnp.zeros((9, narrow, channels), jnp.float32))
    summed = lax.psum_scatter(banded, "dp", scatter_dimension=2, tiled=True)
    grad = summed / jnp.float32(latents.shape[0] * lax.axis_size("dp"))
    new_moment1 = 0.9 * moment1 + 0.1 * grad
    new_moment2 = 0.999 * moment2 + 0.001 * grad * grad
    new_weight = weight - 0.01 * new_moment1 / (jnp.sqrt(new_moment2) + 1e-08)
    return (student, input_grad, new_weight, new_moment1, new_moment2)


def solution(mesh):
    in_specs = (
        P("dp", "rows", None, None),
        P("dp", "rows", None, None),
        P(None, "rows", "dp"),
        P(None, "rows", "dp"),
        P(None, "rows", "dp"),
    )
    out_specs = (
        P("dp", "rows", None, None),
        P("dp", "rows", None, None),
        P(None, "rows", "dp"),
        P(None, "rows", "dp"),
        P(None, "rows", "dp"),
    )
    return jax.shard_map(
        per_device, mesh=mesh, in_specs=in_specs, out_specs=out_specs, check_vma=False
    )
```

profile of v0, /device:TPU:0, one launch (start us, length us, event | category | flops | bytes accessed | tf_op | source)
XLA Modules:
  0.0 324.5 jit_solution(6088130988909758059)
XLA Ops:
  7.2 1.1 convert_element_type.40
  8.3 1.2 copy.43
  9.5 32.5 %all_gather.9 = bf16[9,640,40]{2,0,1:T(8,128)(2,1)} all-gather(bf16[9,320,40]{2,0,1:T(8,128)(2,1)S(1)} %copy.43), channel_id=1, replica_groups=mesh['dp'=16,'rows'=2] {'rows'}, dimensions={1}, use_global_device_ids=true | all-gather | bytes 691200 | tf_op jit(solution)/shard_map/all_gather | solution.py:64
  41.9 4.0 %copy.44 = bf16[9,640,40]{1,2,0:T(8,128)(2,1)} copy(bf16[9,640,40]{2,0,1:T(8,128)(2,1)} %all_gather.9) | data formatting | bytes 921600 | tf_op jit(solution)/shard_map/all_gather | solution.py:64
  46.1 3.7 %collective-permute-start = (bf16[1,1,32,640]{3,2,1,0:T(8,128)(2,1)S(1)}, bf16[1,1,32,640]{3,2,1,0:T(8,128)(2,1)S(1)}, u32[]{:S(2)}, u32[]{:S(2)}) collective-permute-start(bf16[1,1,32,640]{3,2,1,0:T(8,128)(2,1)S(1)} %get-tuple-element.125), channel_id=1, source_target_pairs={{0,1},{2,3},{4,5},{6,7},{8,9},{10,11},{12,13},{14,15},{16,17},{18,... | collective-permute-start | bytes 122888 | tf_op jit(solution)/shard_map/ppermute | solution.py:15
  49.8 1.3 collective-permute-start.1
  51.4 4.2 %collective-permute-done.1 = bf16[1,1,32,640]{3,2,1,0:T(8,128)(2,1)S(1)} collective-permute-done((bf16[1,1,32,640]{3,2,1,0:T(8,128)(2,1)S(1)}, bf16[1,1,32,640]{3,2,1,0:T(8,128)(2,1)S(1)}, u32[]{:S(2)}, u32[]{:S(2)}) %collective-permute-start.1) | collective-permute-done | bytes 40992 | tf_op jit(solution)/shard_map/ppermute | solution.py:17
  56.0 60.1 %all-gather.3.cloned.1.call-done = bf16[9,640,640]{1,2,0:T(8,128)(2,1)} async-done(((bf16[9,640,40]{1,2,0:T(8,128)(2,1)}), bf16[9,640,640]{1,2,0:T(8,128)(2,1)}) %all-gather.3.cloned.1.call-update) | async-done | bytes 7372816 | tf_op jit(solution)/shard_map/all_gather | solution.py:67
  116.1 1.9 fusion.63
  118.1 2.1 fusion.65
  120.2 2.2 convolution_add_fusion.13
  122.4 0.8 convolution_add_fusion.12
  123.2 0.8 convolution_add_fusion.11
  124.0 0.8 convolution_add_fusion.10
  124.9 0.8 convolution_add_fusion.9
  125.7 0.8 convolution_add_fusion.8
  126.8 1.9 subtract_convert_fusion
  128.7 4.0 %copy.54 = bf16[1,18,34,640]{2,1,0,3:T(8,128)(2,1)} copy(bf16[1,18,34,640]{3,2,1,0:T(8,128)(2,1)S(1)} %select_maximum_fusion.2) | data formatting | bytes 1566720 | tf_op jit(solution)/shard_map/jit(_pad)/pad | solution.py:66
  132.7 6.9 %reshape.222 = bf16[2,2,97920]{2,1,0:T(2,128)(2,1)} reshape(bf16[640,1,18,34]{3,2,1,0:T(8,128)(2,1)} %bitcast.364) | data formatting | bytes 1566720
  139.6 3.5 %all-to-all-start = ((bf16[2,2,97920]{2,1,0:T(2,128)(2,1)}), bf16[2,2,97920]{2,1,0:T(2,128)(2,1)S(1)}, u32[]{:S(2)}, u32[]{:S(2)}) async-start(bf16[2,2,97920]{2,1,0:T(2,128)(2,1)} %reshape.222), calls=%async_computation | async-start | bytes 1566720 | tf_op jit(solution)/shard_map/all_to_all | solution.py:75
  143.4 16.3 %all-to-all-done = bf16[2,2,97920]{2,1,0:T(2,128)(2,1)S(1)} async-done(((bf16[2,2,97920]{2,1,0:T(2,128)(2,1)}), bf16[2,2,97920]{2,1,0:T(2,128)(2,1)S(1)}, u32[]{:S(2)}, u32[]{:S(2)}) %all-to-all-start) | async-done | bytes 783392 | tf_op jit(solution)/shard_map/all_to_all | solution.py:75
  159.7 6.1 %reshape.223 = bf16[640,1,18,34]{3,2,1,0:T(8,128)(2,1)} reshape(bf16[2,2,97920]{2,1,0:T(2,128)(2,1)S(1)} %all-to-all-done) | data formatting | bytes 1566720
  165.8 6.0 %copy.55 = bf16[1,2,18,34,320]{4,3,2,1,0:T(8,128)(2,1)S(1)} copy(bf16[1,2,18,34,320]{3,2,4,1,0:T(8,128)(2,1)} %bitcast.365) | data formatting | bytes 1566720 | tf_op jit(solution)/shard_map/all_to_all | solution.py:75
  171.9 25.7 %while.14 = (s32[]{:T(128)}, f32[9,320,640]{2,1,0:T(8,128)}, bf16[1,36,34,320]{3,2,1,0:T(8,128)(2,1)S(1)}, bf16[1,32,32,640]{3,2,1,0:T(8,128)(2,1)}, s32[]{:T(12...) while((s32[]{:T(128)}, f32[9,320,640]{2,1,0:T(8,128)}, ...), condition=%wide.region_1.2_spmd.clone, body=%wide.region_0.1_spmd.clone.sunk | while | flops 1894809600 | bytes 88408528 | solution.py:83
  171.9 1.6 fusion.113
  178.3 1.1 slice-done.1
  179.4 2.3 select_add_fusion.2
  181.8 3.0 copy-done
  184.7 1.6 fusion.113
  191.1 1.1 slice-done.1
  192.2 2.3 select_add_fusion.2
  194.6 3.0 copy-done
  197.5 10.8 %copy.58 = f32[9,320,640]{1,2,0:T(8,128)} copy(f32[9,320,640]{2,1,0:T(8,128)} %get-tuple-element.84) | data formatting | bytes 14745600 | tf_op jit(solution)/shard_map/while | solution.py:83
  208.4 1.1 copy-done.1
  209.4 2.2 collective-permute-start.2
  211.7 1.5 collective-permute-start.3
  213.3 4.2 %collective-permute-done.3 = bf16[1,1,32,640]{3,2,1,0:T(8,128)(2,1)S(1)} collective-permute-done((bf16[1,1,32,640]{3,2,1,0:T(8,128)(2,1)S(1)}, bf16[1,1,32,640]{3,2,1,0:T(8,128)(2,1)S(1)}, u32[]{:S(2)}, u32[]{:S(2)}) %collective-permute-start.3) | collective-permute-done | bytes 40992 | tf_op jit(solution)/shard_map/ppermute | solution.py:17
  217.9 2.3 fusion.62
  220.2 2.0 fusion.64
  222.3 2.2 convolution_add_fusion.6
  224.4 2.1 convolution_add_fusion.5
  226.5 0.8 convolution_add_fusion.4
  227.3 0.8 convolution_add_fusion.3
  228.1 0.8 convolution_add_fusion.2
  228.9 0.8 convolution_add_fusion.1
  229.7 1.6 fusion.59
  231.3 84.2 %reduce-scatter.2.cloned.1.call-done = f32[9,320,40]{1,2,0:T(8,128)} async-done(((f32[9,320,640]{1,2,0:T(8,128)}), f32[9,320,40]{1,2,0:T(8,128)}) %reduce-scatter.2.cloned.1.call-update) | async-done | bytes 460816 | tf_op jit(solution)/shard_map/reduce_scatter | solution.py:84
  315.5 2.4 divide_subtract_fusion
  (62 shorter events, 11.2 us)
Async XLA Ops:
  7.2 109.0 %all-gather.3.cloned.1.call-start = ((), (), s32[]{:S(2)}) async-start(), calls=%async_computation.2 | async-start | bytes 7833600 | tf_op jit(solution)/shard_map/all_gather | solution.py:67
  41.9 4.1 %copy-start.3 = (bf16[1,16,32,640]{3,2,1,0:T(8,128)(2,1)S(1)}, bf16[1,16,32,640]{3,2,1,0:T(8,128)(2,1)}, u32[]{:S(2)}) copy-start(bf16[1,16,32,640]{3,2,1,0:T(8,128)(2,1)} %param.7) | copy-start | bytes 1966084
  46.0 125.9 %all-gather.5.cloned.1.call-start = ((), (), s32[]{:S(2)}) async-start(), calls=%async_computation.3 | async-start | bytes 1966080 | tf_op jit(solution)/shard_map/all_gather | solution.py:76
  46.1 5.3 %collective-permute-start = (bf16[1,1,32,640]{3,2,1,0:T(8,128)(2,1)S(1)}, bf16[1,1,32,640]{3,2,1,0:T(8,128)(2,1)S(1)}, u32[]{:S(2)}, u32[]{:S(2)}) collective-permute-start(bf16[1,1,32,640]{3,2,1,0:T(8,128)(2,1)S(1)} %get-tuple-element.125), channel_id=1, source_target_pairs={{0,1},{2,3},{4,5},{6,7},{8,9},{10,11},{12,13},{14,15},{16,17},{18,... | collective-permute-start | bytes 122888 | tf_op jit(solution)/shard_map/ppermute | solution.py:15
  49.8 5.9 %collective-permute-start.1 = (bf16[1,1,32,640]{3,2,1,0:T(8,128)(2,1)S(1)}, bf16[1,1,32,640]{3,2,1,0:T(8,128)(2,1)S(1)}, u32[]{:S(2)}, u32[]{:S(2)}) collective-permute-start(bf16[1,1,32,640]{3,2,1,0:T(8,128)(2,1)S(1)} %get-tuple-element.126), channel_id=1, source_target_pairs={{1,0},{3,2},{5,4},{7,6},{9,8},{11,10},{13,12},{15,14},{17,16},{19,... | collective-permute-start | bytes 122888 | tf_op jit(solution)/shard_map/ppermute | solution.py:17
  118.1 4.3 %copy-start.2 = (bf16[9,640,640]{1,2,0:T(8,128)(2,1)S(1)}, bf16[9,640,640]{1,2,0:T(8,128)(2,1)}, u32[]{:S(2)}) copy-start(bf16[9,640,640]{1,2,0:T(8,128)(2,1)} %all-gather.3.cloned.1.call-done) | copy-start | bytes 22118404
  125.7 1.1 copy-start.5
  139.6 20.1 %all-to-all-start = ((bf16[2,2,97920]{2,1,0:T(2,128)(2,1)}), bf16[2,2,97920]{2,1,0:T(2,128)(2,1)S(1)}, u32[]{:S(2)}, u32[]{:S(2)}) async-start(bf16[2,2,97920]{2,1,0:T(2,128)(2,1)} %reshape.222), calls=%async_computation | async-start | bytes 1566720 | tf_op jit(solution)/shard_map/all_to_all | solution.py:75
  143.1 172.4 %reduce-scatter.2.cloned.1.call-start = ((), (), s32[]{:S(2)}) async-start(), calls=%async_computation.4 | async-start | bytes 9400320 | tf_op jit(solution)/shard_map/reduce_scatter | solution.py:84
  171.9 1.7 copy-start.8
  176.1 2.2 slice-start
  176.6 2.8 slice-start.1
  181.7 3.0 copy-start
  184.7 1.7 copy-start.8
  188.9 2.2 slice-start
  189.4 2.8 slice-start.1
  194.6 3.0 copy-start
  208.3 1.1 copy-start.1
  209.4 3.9 %collective-permute-start.2 = (bf16[1,1,32,640]{3,2,1,0:T(8,128)(2,1)S(1)}, bf16[1,1,32,640]{3,2,1,0:T(8,128)(2,1)S(1)}, u32[]{:S(2)}, u32[]{:S(2)}) collective-permute-start(bf16[1,1,32,640]{3,2,1,0:T(8,128)(2,1)S(1)} %get-tuple-element.123), channel_id=1, source_target_pairs={{0,1},{2,3},{4,5},{6,7},{8,9},{10,11},{12,13},{14,15},{16,17},{18,... | collective-permute-start | bytes 122888 | tf_op jit(solution)/shard_map/ppermute | solution.py:15
  211.7 5.9 %collective-permute-start.3 = (bf16[1,1,32,640]{3,2,1,0:T(8,128)(2,1)S(1)}, bf16[1,1,32,640]{3,2,1,0:T(8,128)(2,1)S(1)}, u32[]{:S(2)}, u32[]{:S(2)}) collective-permute-start(bf16[1,1,32,640]{3,2,1,0:T(8,128)(2,1)S(1)} %get-tuple-element.124), channel_id=1, source_target_pairs={{1,0},{3,2},{5,4},{7,6},{9,8},{11,10},{13,12},{15,14},{17,16},{19,... | collective-permute-start | bytes 122888 | tf_op jit(solution)/shard_map/ppermute | solution.py:17
  217.6 9.0 %slice-start.2 = ((s8[7372800]{0:T(1024)(128)(4,1)}), s8[4194304]{0:T(1024)(128)(4,1)S(1)}, s32[]{:S(2)}) async-start(s8[7372800]{0:T(1024)(128)(4,1)} %bitcast.362), calls=%async_computation.7 | async-start | bytes 8388608
  222.3 4.3 %slice-start.3 = ((s8[7372800]{0:T(1024)(128)(4,1)}), s8[3178496]{0:T(1024)(128)(4,1)S(1)}, s32[]{:S(2)}) async-start(s8[7372800]{0:T(1024)(128)(4,1)} %bitcast.362), calls=%async_computation.8 | async-start | bytes 6356992
  229.6 85.9 %copy-start.4 = (f32[9,320,40]{1,2,0:T(8,128)S(1)}, f32[9,320,40]{1,2,0:T(8,128)}, u32[]{:S(2)}) copy-start(f32[9,320,40]{1,2,0:T(8,128)} %param.9) | copy-start | bytes 1382404
  229.6 85.9 %copy-start.6 = (f32[9,320,40]{1,2,0:T(8,128)S(1)}, f32[9,320,40]{1,2,0:T(8,128)}, u32[]{:S(2)}) copy-start(f32[9,320,40]{1,2,0:T(8,128)} %param.10) | copy-start | bytes 1382404
  229.7 85.9 %copy-start.7 = (f32[9,320,40]{1,2,0:T(8,128)S(1)}, f32[9,320,40]{1,2,0:T(8,128)}, u32[]{:S(2)}) copy-start(f32[9,320,40]{1,2,0:T(8,128)} %param.11) | copy-start | bytes 1382404
Sparse Core Ops, SparseCore 0:
  46.1 69.9 all-gather.2
  128.8 27.8 all-gather.4
  208.5 107.0 reduce-scatter.1
where the time goes:
time: 325 us; the launch traced here: 324 us
  waiting for transfers between devices  170 us (52%)
  local copies, waits for them, and re-layouts  49.9 us (15%)
  matrix products  36.8 us (11%)
  blocking collectives  32.5 us (10%)
  between operations  14.1 us (4%)
  starting transfers between devices  12.5 us (4%)
  other arithmetic  8.82 us (3%)
    reduce_scatter x1, waiting for transfers between devices, per_device(): summed = lax.psum_scatter(banded, 'dp', scatter_dimension=2, tiled=True)  84.2 us
    all_gather x1, waiting for transfers between devices, per_device(): kernel = lax.all_gather(kernel_part, 'dp', axis=2, tiled=True)  60.1 us
    all_gather x1, blocking collectives, per_device(): lax.all_gather(weight.astype(jnp.bfloat16), 'rows', axis=1, tiled=True)  32.5 us
    all_to_all x1, waiting for transfers between devices, per_device(): lax.all_to_all(padded, 'rows', split_axis=3, concat_axis=1, tiled=True)  16.3 us
    unnamed x20, local copies, waits for them, and re-layouts  14.4 us
    dot_general x9, matrix products, backward_cells(): jnp.einsum('bhwn,cn->bhwc', window, kernel[tap], preferred_element_type=j...  13.3 us
    dot_general x9, matrix products, forward_cells(): jnp.einsum('bhwc,cn->bhwn', padded[:, a:a + band, c:c + width], kernel[ta...  12.2 us
    dot_general x18, matrix products, band_partial(): jnp.einsum('bhwc,bhwn->cn', window, error, preferred_element_type=jnp.flo...  11.4 us
  transfers between devices with their start and end apart: 8, of which 7 were waited for; matrix products, arithmetic and copies ran while one was open for 11% of the time, Pallas kernels for 0%

commit v1 on v0

v1 whole, which is shorter than its diff:
```python
import functools

import jax
import jax.numpy as jnp
import numpy as np
from jax import lax
from jax.experimental import pallas as pl
from jax.experimental.pallas import tpu as pltpu
from jax.sharding import PartitionSpec as P

BF = jnp.bfloat16
F32 = jnp.float32
NT = (((1,), (1,)), ((), ()))
NN = (((1,), (0,)), ((), ()))
VMEM_LIMIT = 48 << 20
TAPS = 9
ROUTES = (8, 16, 16)


def mm(a, b, dims):
    return lax.dot_general(a, b, dims, preferred_element_type=F32)


def conv_student(kernel_ref, x_ref, t_ref, s_ref, e_ref, width):
    wide = x_ref.shape[2]
    cells = x_ref.shape[1] - 2 * width
    for l in range(x_ref.shape[0]):
        at = slice(l * cells, (l + 1) * cells)
        total = None
        for a in range(3):
            term = mm(
                kernel_ref[:, a * wide : (a + 1) * wide],
                x_ref[l, a * width : a * width + cells, :],
                NT,
            )
            total = term if total is None else total + term
        student = total.astype(BF)
        s_ref[:, at] = student
        e_ref[:, at] = (student.astype(F32) - t_ref[:, at].astype(F32)).astype(BF)


def tap_grad(x_ref, e_ref, tap, width):
    a, c = divmod(tap, 3)
    channels = x_ref.shape[2] // 3
    cells = x_ref.shape[1] - 2 * width
    total = None
    for l in range(x_ref.shape[0]):
        term = mm(
            e_ref[:, l * cells : (l + 1) * cells],
            x_ref[l, a * width : a * width + cells, c * channels : (c + 1) * channels],
            NN,
        )
        total = term if total is None else total + term
    return total


def plain_kernel(width, kernel_ref, x_ref, t_ref, s_ref, e_ref, g_ref):
    channels = x_ref.shape[2] // 3
    conv_student(kernel_ref, x_ref, t_ref, s_ref, e_ref, width)
    for tap in range(TAPS):
        g_ref[:, tap * channels : (tap + 1) * channels] = tap_grad(
            x_ref, e_ref, tap, width
        ).astype(BF)


def routed_kernel(width, half_ref, w_ref, x_ref, t_ref, k_ref, s_ref, e_ref, *outs):
    a_refs, (b0_ref, b1_ref, c0_ref, c1_ref, mid_ref) = outs[:4], outs[4:]
    first = half_ref[0]
    second = 1 - first
    low = lax.broadcasted_iota(jnp.int32, (w_ref.shape[1], 128), 1) < 64
    spare = TAPS * 256
    for tap in range(TAPS):
        k_ref[:, tap * 640 : tap * 640 + 256] = w_ref[first, :, tap * 256 : (tap + 1) * 256]
        k_ref[:, tap * 640 + 384 : (tap + 1) * 640] = w_ref[second, :, tap * 256 : (tap + 1) * 256]
    for pair in range(5):
        at = slice(spare + pair * 128, spare + (pair + 1) * 128)
        left = w_ref[first, :, at].astype(F32)
        right = w_ref[second, :, at].astype(F32)
        k_ref[:, 2 * pair * 640 + 256 : 2 * pair * 640 + 384] = jnp.where(
            low, left, pltpu.roll(right, 64, 1)
        ).astype(BF)
        if 2 * pair + 1 < TAPS:
            k_ref[:, (2 * pair + 1) * 640 + 256 : (2 * pair + 1) * 640 + 384] = jnp.where(
                low, pltpu.roll(left, 64, 1), right
            ).astype(BF)
    conv_student(k_ref, x_ref, t_ref, s_ref, e_ref, width)

    is_first = first == 0

    def put(at, lo, hi):
        own = jnp.where(is_first, lo, hi).astype(BF)
        other = jnp.where(is_first, hi, lo).astype(BF)
        for s in range(4):
            a_refs[s][0, :, at] = own[s * 16 : (s + 1) * 16]
            a_refs[s][1, :, at] = other[s * 16 : (s + 1) * 16]
        b0_ref[0, :, at] = own[64:128]
        b0_ref[1, :, at] = other[64:128]
        b1_ref[0, :, at] = own[128:192]
        b1_ref[1, :, at] = other[128:192]
        c0_ref[:, at] = own[192:]
        c1_ref[:, at] = other[192:]

    for tap in range(TAPS):
        grad = tap_grad(x_ref, e_ref, tap, width)
        put(slice(tap * 256, (tap + 1) * 256), grad[:, :256], grad[:, 384:])
        mid_ref[tap] = grad[:, 256:384]
    for pair in range(5):
        even = mid_ref[2 * pair]
        odd = mid_ref[2 * pair + 1] if 2 * pair + 1 < TAPS else jnp.zeros_like(even)
        put(
            slice(spare + pair * 128, spare + (pair + 1) * 128),
            jnp.where(low, even, pltpu.roll(odd, 64, 1)),
            jnp.where(low, pltpu.roll(even, 64, 1), odd),
        )


def back_kernel(width, kernel_ref, e_ref, out_ref):
    channels = kernel_ref.shape[1] // TAPS
    cells = e_ref.shape[2] - 2 * width
    for l in range(e_ref.shape[1]):
        total = None
        for tap in range(TAPS):
            a, c = divmod(tap, 3)
            term = mm(
                e_ref[c, l, (2 - a) * width : (2 - a) * width + cells, :],
                kernel_ref[:, tap * channels : (tap + 1) * channels],
                NN,
            )
            total = term if total is None else total + term
        out_ref[l] = total


def vmem_call(kernel, outs, scalars, *args, scratch=()):
    flops = 2 * 1024 * 320 * 5760
    return pl.pallas_call(
        kernel,
        out_shape=outs,
        in_specs=[pl.BlockSpec(memory_space=pltpu.SMEM)] * scalars
        + [pl.BlockSpec(memory_space=pltpu.VMEM)] * (len(args) - scalars),
        out_specs=jax.tree.map(lambda _: pl.BlockSpec(memory_space=pltpu.VMEM), outs),
        scratch_shapes=scratch,
        cost_estimate=pl.CostEstimate(flops=flops, bytes_accessed=8 << 20, transcendentals=0),
        compiler_params=pltpu.CompilerParams(vmem_limit_bytes=VMEM_LIMIT),
    )(*args)


def shape(*dims, dtype=BF):
    return jax.ShapeDtypeStruct(dims, dtype)


def column_shift(cells, by):
    if by == 0:
        return cells
    zero = jnp.zeros_like(cells[:, :, :1])
    if by > 0:
        return jnp.concatenate([cells[:, :, 1:], zero], axis=2)
    return jnp.concatenate([zero, cells[:, :, :-1]], axis=2)


def adam(weight, moment1, moment2, grad):
    new_moment1 = 0.9 * moment1 + 0.1 * grad
    new_moment2 = 0.999 * moment2 + 0.001 * grad * grad
    new_weight = weight - 0.01 * new_moment1 / (jnp.sqrt(new_moment2) + 1e-08)
    return new_weight, new_moment1, new_moment2


def with_halo(cells):
    count = lax.axis_size("rows")
    if count == 2:
        at_top = lax.axis_index("rows") == 0
        edge = jnp.where(at_top, cells[:, -1:], cells[:, :1])
        got = lax.ppermute(edge, "rows", [(0, 1), (1, 0)])
        zero = jnp.zeros_like(got)
        return jnp.concatenate(
            [jnp.where(at_top, zero, got), cells, jnp.where(at_top, got, zero)], axis=1
        )
    up = lax.ppermute(cells[:, -1:], "rows", [(i, i + 1) for i in range(count - 1)])
    down = lax.ppermute(cells[:, :1], "rows", [(i + 1, i) for i in range(count - 1)])
    return jnp.concatenate([up, cells, down], axis=1)


def wide_cells(cells):
    b, h, w, c = cells.shape
    return jnp.concatenate([column_shift(cells, k - 1) for k in range(3)], axis=3).reshape(
        b, h * w, 3 * c
    )


def back_cells(error):
    b, h, w, n = error.shape
    return jnp.stack([column_shift(error, 1 - k) for k in range(3)]).reshape(3, b, h * w, n)


def general_device(latents, target, weight, moment1, moment2):
    b, band, width, channels = latents.shape
    cells = b * band * width
    part, outs = weight.shape[1], weight.shape[2]
    row_count = lax.axis_size("rows")
    packed = weight.astype(BF).transpose(2, 0, 1)
    gathered = lax.all_gather(packed, "dp", axis=0, tiled=True)
    kernel = lax.all_gather(gathered, "rows", axis=2, tiled=True)
    total_out = kernel.shape[0]
    kernel = kernel.reshape(total_out, TAPS * channels)
    x = wide_cells(with_halo(latents))
    t = target.reshape(cells, total_out).T
    student, error, grad = vmem_call(
        functools.partial(plain_kernel, width),
        (shape(total_out, cells), shape(total_out, cells), shape(total_out, TAPS * channels)),
        0,
        kernel,
        x,
        t,
    )
    error = error.T.reshape(b, band, width, total_out)
    back = vmem_call(
        functools.partial(back_kernel, width),
        shape(b, band * width, channels, dtype=F32),
        0,
        kernel,
        back_cells(with_halo(error)),
    )
    grad = grad.astype(F32).reshape(total_out, TAPS, row_count, part).transpose(2, 0, 1, 3)
    grad = lax.psum_scatter(grad, "rows", scatter_dimension=0, tiled=True)[0]
    grad = lax.psum_scatter(grad, "dp", scatter_dimension=0, tiled=True)
    grad = grad.transpose(1, 2, 0) / F32(b * lax.axis_size("dp"))
    return (
        student.T.reshape(latents.shape),
        back.astype(BF).reshape(latents.shape),
        *adam(weight, moment1, moment2, grad),
    )


def routed_device(latents, target, weight, moment1, moment2):
    b, band, width, channels = latents.shape
    cells = band * width
    index = lax.axis_index("dp")
    core, y, z = index % 2, (index // 2) % 2, index // 4
    half = lax.axis_index("rows")
    along_core = lambda v: lax.ppermute(v, "dp", [(i, i ^ 1) for i in range(16)])
    along_y = lambda v: lax.ppermute(v, "dp", [(i, i ^ 2) for i in range(16)])
    along_z = lambda v, s: lax.ppermute(v, "dp", [(i, (i + 4 * s) % 16) for i in range(16)])
    along_x = lambda v: lax.ppermute(v, "rows", [(0, 1), (1, 0)])
    ra, rb, rc = ROUTES
    lanes = TAPS * 256 + 640

    piece = weight.transpose(2, 0, 1)
    piece = jnp.where(half == 0, piece, jnp.roll(piece, -64, axis=2)).astype(BF)
    piece = jnp.concatenate(
        [
            piece[:, :, :256].reshape(-1, TAPS * 256),
            piece[:, :, 256:].reshape(-1, TAPS * 64),
            jnp.zeros((piece.shape[0], 64), BF),
        ],
        axis=1,
    )

    pa, pbc = piece[:ra], piece[ra:]
    zbc = jnp.stack([pbc] + [along_z(pbc, s) for s in (1, 2, 3)])
    pa = jnp.stack([pa, along_x(pa)])
    pa = jnp.stack([pa, along_y(pa)], axis=1)
    pb, pc = zbc[:, :rb], zbc[:, rb:]
    pb = jnp.stack([pb, along_x(pb)])
    pc = jnp.stack([pc, along_y(pc)])
    pa = jnp.stack([pa] + [along_z(pa, s) for s in (1, 2, 3)], axis=1)
    pb = jnp.stack([pb, along_y(pb)], axis=1)
    pc = jnp.stack([pc, along_x(pc)])
    pieces = jnp.concatenate(
        [pa.reshape(2, 8 * ra, lanes), pb.reshape(2, 8 * rb, lanes), pc.reshape(2, 8 * rc, lanes)],
        axis=1,
    )

    order = []
    for r, (off, count, axes) in enumerate(((0, ra, "sy"), (ra, rb, "ys"), (ra + rb, rc, "ys"))):
        grid = np.indices((4, 2, count) if axes == "sy" else (2, 4, count)).reshape(3, -1)
        s, yr = (grid[0], grid[1]) if axes == "sy" else (grid[1], grid[0])
        order.append(np.stack([s, yr, off + grid[2]]))
    order = np.concatenate(order, axis=1).astype(np.int32)
    block = ((z - order[0]) % 4) * 4 + (y ^ order[1]) * 2
    per = weight.shape[2]
    everything = jnp.arange(channels, dtype=jnp.int32)
    pick_own = ((block + core) * per + order[2])[:, None] == everything[None, :]
    pick_other = ((block + 1 - core) * per + order[2])[:, None] == everything[None, :]
    pick = jnp.concatenate([pick_own, pick_other]).astype(BF)
    rows = order.shape[1]

    banded = with_halo(latents)
    x = wide_cells(jnp.concatenate([banded, along_core(banded)]))
    t = mm(pick, target.reshape(cells, channels), NT).astype(BF)
    t = jnp.concatenate([t[:rows], along_core(t[rows:])], axis=1)

    kernel, student, error, a0, a1, a2, a3, b0, b1, c0, c1 = vmem_call(
        functools.partial(routed_kernel, width),
        (shape(rows, TAPS * channels), shape(rows, 2 * cells), shape(rows, 2 * cells))
        + (shape(2, 2 * ra, lanes),) * 4
        + (shape(2, 4 * rb, lanes),) * 2
        + (shape(8 * rc, lanes),) * 2,
        1,
        half.astype(jnp.int32).reshape(1),
        pieces,
        x,
        t,
        scratch=[pltpu.VMEM((TAPS, rows, 128), F32)],
    )

    def plus(*terms):
        total = terms[0].astype(F32)
        for term in terms[1:]:
            total = total + term.astype(F32)
        return total

    gb = along_y(b1)
    gc = along_x(c1)
    az = [along_z(v, -s) for s, v in ((1, a1), (2, a2), (3, a3))]
    gb_out = plus(b0[1], gb[1]).astype(BF)
    gc = gc.reshape(2, 4 * rc, lanes)
    c0 = c0.reshape(2, 4 * rc, lanes)
    gc_out = plus(c0[1], gc[1]).astype(BF)
    gb2 = along_x(gb_out)
    gc2 = along_y(gc_out)
    gb = plus(b0[0], gb[0], gb2).astype(BF).reshape(4, rb, lanes)
    gc = plus(c0[0], gc[0], gc2).astype(BF).reshape(4, rc, lanes)
    gbc = jnp.concatenate([gb, gc], axis=1)
    bcz = [along_z(gbc[s], -s) for s in (1, 2, 3)]
    ga = plus(a0, *az).reshape(2, 2, ra, lanes)
    ga_in = along_y(ga[:, 1].astype(BF))
    ga = plus(ga[:, 0], ga_in)
    ga_in = along_x(ga[1].astype(BF))
    ga = plus(ga[0], ga_in)
    grad = jnp.concatenate([ga, plus(gbc[0], *bcz)], axis=0) / F32(b * lax.axis_size("dp"))
    grad = jnp.concatenate(
        [
            grad[:, : TAPS * 256].reshape(-1, TAPS, 256),
            grad[:, TAPS * 256 : TAPS * 320].reshape(-1, TAPS, 64),
        ],
        axis=2,
    )
    grad = jnp.where(half == 0, grad, jnp.roll(grad, 64, axis=2)).transpose(1, 2, 0)

    both = jnp.concatenate([student[:, :cells], along_core(student[:, cells:])])
    out = mm(both, pick, (((0,), (0,)), ((), ()))).astype(BF).reshape(latents.shape)

    error = error.T.reshape(2, band, width, rows)
    back = vmem_call(
        functools.partial(back_kernel, width),
        shape(2, cells, channels, dtype=F32),
        0,
        kernel,
        back_cells(with_halo(error)),
    )
    input_grad = (back[0] + along_core(back[1])).astype(BF).reshape(latents.shape)
    return (out, input_grad, *adam(weight, moment1, moment2, grad))


def solution(mesh):
    def per_device(latents, target, weight, moment1, moment2):
        routed = (
            mesh.shape["dp"] == 16
            and mesh.shape["rows"] == 2
            and latents.shape[0] == 1
            and weight.shape == (TAPS, 320, 40)
        )
        return (routed_device if routed else general_device)(
            latents, target, weight, moment1, moment2
        )

    cells = P("dp", "rows", None, None)
    weights = P(None, "rows", "dp")
    return jax.shard_map(
        per_device,
        mesh=mesh,
        in_specs=(cells, cells, weights, weights, weights),
        out_specs=(cells, cells, weights, weights, weights),
        check_vma=False,
    )
```

time: 325 us -> 159 us (0.49)
  waiting for transfers between devices: 170 us -> 66.8 us
  local copies, waits for them, and re-layouts: 49.9 us -> 9.86 us
  matrix products: 36.8 us -> 2.34 us
  blocking collectives: 32.5 us -> 0 us
  starting transfers between devices: 12.5 us -> 37.7 us
  Pallas kernels: 0 us -> 23.9 us
  between operations: 14.1 us -> 1.17 us
  other arithmetic: 8.82 us -> 16.7 us
    reduce_scatter x1 -> x0, waiting for transfers between devices: 84.2 us -> none  [per_device(): summed = lax.psum_scatter(banded, 'dp', scatter_dimension=2, tiled=True)]
    all_gather x2 -> x0, waiting for transfers between devices: 60.2 us -> none  [the longest x1 60.1 us: per_device(): kernel = lax.all_gather(kernel_part, 'dp', axis=2, tiled=True)]
    ppermute x4 -> x30, waiting for transfers between devices: 8.97 us -> 66.8 us  [the longest x6 24.8 us: routed_device(): along_y = lambda v: lax.ppermute(v, 'dp', [(i, i ^ 2) for i in range(16)])]
    dot_general x36 -> x2, matrix products: 36.8 us -> 2.34 us  [mm(): return lax.dot_general(a, b, dims, preferred_element_type=F32)]
    all_gather x1 -> x0, blocking collectives: 32.5 us -> none  [per_device(): lax.all_gather(weight.astype(jnp.bfloat16), 'rows', axis=1, tiled=True)]
    ppermute x4 -> x30, starting transfers between devices: 8.7 us -> 37.7 us  [the longest x12 22.5 us: routed_device(): lax.ppermute(v, 'dp', [(i, (i + 4 * s) % 16) for i in range(16)])]
    pallas_call x0 -> x2, Pallas kernels: none -> 23.9 us  [vmem_call(): pl.pallas_call(kernel, out_shape=outs, in_specs=[pl.BlockSpec(memory_spac...]
    while x17 -> x0, local copies, waits for them, and re-layouts: 20.3 us -> none  [the longest x1 10.8 us: per_device(): lax.fori_loop(0, band_count, band_step, jnp.zeros((9, narrow, channels),...]
  transfers between devices with their start and end apart: 8 -> 30, of which waited for: 7 -> 16; matrix products, arithmetic and copies ran while one was open for 11% -> 10% of each run, Pallas kernels for 0% -> 6%
where the time goes in v1:
time: 159 us; the launch traced here: 158 us
  waiting for transfers between devices  66.8 us (42%)
  starting transfers between devices  37.7 us (24%)
  Pallas kernels  23.9 us (15%)
  other arithmetic  16.7 us (11%)
  local copies, waits for them, and re-layouts  9.86 us (6%)
  matrix products  2.34 us (1%)
    ppermute x6, waiting for transfers between devices, routed_device(): along_y = lambda v: lax.ppermute(v, 'dp', [(i, i ^ 2) for i in range(16)])  24.8 us
    pallas_call x2, Pallas kernels, vmem_call(): pl.pallas_call(kernel, out_shape=outs, in_specs=[pl.BlockSpec(memory_spac...  23.9 us
    ppermute x12, starting transfers between devices, routed_device(): lax.ppermute(v, 'dp', [(i, (i + 4 * s) % 16) for i in range(16)])  22.5 us
    ppermute x12, waiting for transfers between devices, routed_device(): lax.ppermute(v, 'dp', [(i, (i + 4 * s) % 16) for i in range(16)])  22 us
    ppermute x6, waiting for transfers between devices, routed_device(): along_x = lambda v: lax.ppermute(v, 'rows', [(0, 1), (1, 0)])  17.6 us
    ppermute x6, starting transfers between devices, routed_device(): along_y = lambda v: lax.ppermute(v, 'dp', [(i, i ^ 2) for i in range(16)])  7.35 us
    ppermute x6, starting transfers between devices, routed_device(): along_x = lambda v: lax.ppermute(v, 'rows', [(0, 1), (1, 0)])  5.83 us
    concatenate x1, other arithmetic, routed_device(): jnp.concatenate([pa.reshape(2, 8 * ra, lanes), pb.reshape(2, 8 * rb, lane...  4.02 us
  transfers between devices with their start and end apart: 30, of which 16 were waited for; matrix products, arithmetic and copies ran while one was open for 10% of the time, Pallas kernels for 6%

profile of v1, /device:TPU:0, one launch (start us, length us, event | category | flops | bytes accessed | tf_op | source)
XLA Modules:
  0.0 158.3 jit_solution(6128375979019196581)
XLA Ops:
  0.7 1.0 slice.173
  1.7 1.2 slice.172
  2.9 1.1 fusion.11
  4.4 4.1 %collective-permute-start.6 = (bf16[32,2944]{1,0:T(8,128)(2,1)S(1)}, bf16[32,2944]{1,0:T(8,128)(2,1)S(1)}, u32[]{:S(2)}, u32[]{:S(2)}) collective-permute-start(bf16[32,2944]{1,0:T(8,128)(2,1)S(1)} %get-tuple-element.55), channel_id=1, source_target_pairs={{0,16},{2,18},{4,20},{6,22},{8,24},{10,26},{12,28},{14,30},{16,0},... | collective-permute-start | bytes 565256 | tf_op jit(solution)/shard_map/ppermute | solution.py:241
  8.6 1.6 collective-permute-start.5
  10.1 2.2 %collective-permute-start.7 = (bf16[32,2944]{1,0:T(8,128)(2,1)S(1)}, bf16[32,2944]{1,0:T(8,128)(2,1)S(1)}, u32[]{:S(2)}, u32[]{:S(2)}) collective-permute-start(bf16[32,2944]{1,0:T(8,128)(2,1)S(1)} %get-tuple-element.55), channel_id=1, source_target_pairs={{0,24},{2,26},{4,28},{6,30},{8,0},{10,2},{12,4},{14,6},{16,8},{18,... | collective-permute-start | bytes 565256 | tf_op jit(solution)/shard_map/ppermute | solution.py:241
  12.4 1.6 collective-permute-start.12
  14.9 0.7 convolution_convert_fusion.1
  15.7 0.8 collective-permute-done.12
  16.5 1.6 %collective-permute-done = bf16[8,2944]{1,0:T(8,128)(2,1)S(1)} collective-permute-done((bf16[8,2944]{1,0:T(8,128)(2,1)S(1)}, bf16[8,2944]{1,0:T(8,128)(2,1)S(1)}, u32[]{:S(2)}, u32[]{:S(2)}) %collective-permute-start) | collective-permute-done | bytes 47136 | tf_op jit(solution)/shard_map/ppermute | solution.py:242
  18.1 1.6 %collective-permute-start.1 = (bf16[2,8,2944]{2,1,0:T(8,128)(2,1)S(1)}, bf16[2,8,2944]{2,1,0:T(8,128)(2,1)S(1)}, u32[]{:S(2)}, u32[]{:S(2)}) collective-permute-start(bf16[2,8,2944]{2,1,0:T(8,128)(2,1)S(1)} %get-tuple-element.59), channel_id=1, source_target_pairs={{0,4},{2,6},{4,0},{6,2},{8,12},{10,14},{12,8},{14,10},{16,20},{18,... | collective-permute-start | bytes 282632 | tf_op jit(solution)/shard_map/ppermute | solution.py:240
  19.8 2.9 %collective-permute-done.1 = bf16[2,8,2944]{2,1,0:T(8,128)(2,1)S(1)} collective-permute-done((bf16[2,8,2944]{2,1,0:T(8,128)(2,1)S(1)}, bf16[2,8,2944]{2,1,0:T(8,128)(2,1)S(1)}, u32[]{:S(2)}, u32[]{:S(2)}) %collective-permute-start.1) | collective-permute-done | bytes 94240 | tf_op jit(solution)/shard_map/ppermute | solution.py:240
  22.9 7.4 %collective-permute-start.2 = (bf16[2,2,8,2944]{3,2,0,1:T(8,128)(2,1)S(1)}, bf16[2,2,8,2944]{3,2,0,1:T(8,128)(2,1)S(1)}, u32[]{:S(2)}, u32[]{:S(2)}) collective-permute-start(bf16[2,2,8,2944]{3,2,0,1:T(8,128)(2,1)S(1)} %get-tuple-element.57), channel_id=1, source_target_pairs={{0,8},{2,10},{4,12},{6,14},{8,16},{10,18},{12,20},{14,22},{16,24},... | collective-permute-start | bytes 565256 | tf_op jit(solution)/shard_map/ppermute | solution.py:241
  30.5 1.6 collective-permute-start.8
  32.1 6.2 %collective-permute-done.3 = bf16[2,2,8,2944]{3,2,0,1:T(8,128)(2,1)S(1)} collective-permute-done((bf16[2,2,8,2944]{3,2,0,1:T(8,128)(2,1)S(1)}, bf16[2,2,8,2944]{3,2,0,1:T(8,128)(2,1)S(1)}, u32[]{:S(2)}, u32[]{:S(2)}) %collective-permute-start.3) | collective-permute-done | bytes 188448 | tf_op jit(solution)/shard_map/ppermute | solution.py:241
  38.3 1.5 collective-permute-start.10
  39.8 2.4 %collective-permute-done.4 = bf16[2,2,8,2944]{3,2,0,1:T(8,128)(2,1)S(1)} collective-permute-done((bf16[2,2,8,2944]{3,2,0,1:T(8,128)(2,1)S(1)}, bf16[2,2,8,2944]{3,2,0,1:T(8,128)(2,1)S(1)}, u32[]{:S(2)}, u32[]{:S(2)}) %collective-permute-start.4) | collective-permute-done | bytes 188448 | tf_op jit(solution)/shard_map/ppermute | solution.py:241
  42.5 1.6 %collective-permute-start.9 = (bf16[2,4,16,2944]{3,2,1,0:T(8,128)(2,1)S(1)}, bf16[2,4,16,2944]{3,2,1,0:T(8,128)(2,1)S(1)}, u32[]{:S(2)}, u32[]{:S(2)}) collective-permute-start(bf16[2,4,16,2944]{3,2,1,0:T(8,128)(2,1)S(1)} %get-tuple-element.43), channel_id=1, source_target_pairs={{0,4},{2,6},{4,0},{6,2},{8,12},{10,14},{12,8},{14,10},{16,20},{18,... | collective-permute-start | bytes 2261000 | tf_op jit(solution)/shard_map/ppermute | solution.py:240
  44.1 5.8 %collective-permute-done.10 = bf16[4,16,2944]{2,1,0:T(8,128)(2,1)S(1)} collective-permute-done((bf16[4,16,2944]{2,1,0:T(8,128)(2,1)S(1)}, bf16[4,16,2944]{2,1,0:T(8,128)(2,1)S(1)}, u32[]{:S(2)}, u32[]{:S(2)}) %collective-permute-start.10) | collective-permute-done | bytes 376864 | tf_op jit(solution)/shard_map/ppermute | solution.py:240
  50.0 1.1 collective-permute-start.11
  51.3 0.8 fusion.37
  52.1 3.1 %fusion.2 = bf16[2,18,32,1920]{3,2,1,0:T(8,128)(2,1)} fusion(bf16[2,18,31,640]{3,2,1,0:T(8,128)(2,1)S(1)} %get-tuple-element.36, bf16[2,18,31,640]{3,2,1,0:T(8,128)(2,1)S(1)} %get-tuple-element.35, bf16[1,18,32,640]{3,2,1,0:T(8,128)(2,1)S(1)} %collective-permute-done.13, bf16[1,1,32,640]{3,2,1,0:T(8,128)(2,1)S(1)} %get-tuple-element.63, ...), kind=kLoop, calls=%fused_computation.4 | loop fusion | flops 35389440 | bytes 8755200 | tf_op jit(solution)/shard_map/concatenate | solution.py:184
  55.3 9.9 %collective-permute-done.9 = bf16[2,4,16,2944]{3,2,1,0:T(8,128)(2,1)S(1)} collective-permute-done((bf16[2,4,16,2944]{3,2,1,0:T(8,128)(2,1)S(1)}, bf16[2,4,16,2944]{3,2,1,0:T(8,128)(2,1)S(1)}, u32[]{:S(2)}, u32[]{:S(2)}) %collective-permute-start.9) | collective-permute-done | bytes 753696 | tf_op jit(solution)/shard_map/ppermute | solution.py:240
  65.4 1.6 %collective-permute-done.11 = bf16[2,4,16,2944]{3,2,1,0:T(8,128)(2,1)S(1)} collective-permute-done((bf16[2,4,16,2944]{3,2,1,0:T(8,128)(2,1)S(1)}, bf16[2,4,16,2944]{3,2,1,0:T(8,128)(2,1)S(1)}, u32[]{:S(2)}, u32[]{:S(2)}) %collective-permute-start.11) | collective-permute-done | bytes 753696 | tf_op jit(solution)/shard_map/ppermute | solution.py:242
  67.0 4.0 %maximum_maximum_fusion.w_ref = bf16[2,320,2944]{2,1,0:T(8,128)(2,1)} fusion(bf16[1,128,2944]{2,1,0:T(8,128)(2,1)S(1)} %bitcast.118, bf16[1,128,2944]{2,1,0:T(8,128)(2,1)S(1)} %bitcast.114, bf16[2,128,2944]{2,1,0:T(8,128)(2,1)S(1)} %bitcast.101, bf16[2,64,2944]{2,1,0:T(8,128)(2,1)S(1)} %bitcast.113), kind=kLoop, calls=%fused_computation.6 | loop fusion | flops 15073280 | bytes 7536640 | tf_op jit(solution)/shard_map/concatenate | solution.py:267
  71.0 14.9 %shard_map.128 = (bf16[320,5760]{1,0:T(8,128)(2,1)}, bf16[320,1024]{1,0:T(8,128)(2,1)S(1)}, bf16[320,1024]{1,0:T(8,128)(2,1)S(1)}, bf16[2,16,2944]{2,1,0:T(8,128...) custom-call(s32[1]{0:T(128)} %bitcast.half_ref, ...), custom_call_target="tpu_custom_call" | custom-call | flops 3774873600 | bytes 8388608 | tf_op jit(solution)/shard_map/pallas_call | solution.py:135
  85.9 0.9 copy-done.2
  86.8 0.9 copy-done.4
  87.6 0.9 copy-done.6
  89.5 1.9 %collective-permute-start.20 = (bf16[2,16,2944]{2,1,0:T(8,128)(2,1)}, bf16[2,16,2944]{2,1,0:T(8,128)(2,1)S(1)}, u32[]{:S(2)}, u32[]{:S(2)}) collective-permute-start(bf16[2,16,2944]{2,1,0:T(8,128)(2,1)} %get-tuple-element.22), channel_id=1, source_target_pairs={{0,8},{2,10},{4,12},{6,14},{8,16},{10,18},{12,20},{14,22},{16,24},... | collective-permute-start | bytes 565256 | tf_op jit(solution)/shard_map/ppermute | solution.py:241
  91.5 1.6 %collective-permute-done.16 = bf16[2,1,32,320]{3,2,1,0:T(8,128)(2,1)S(1)} collective-permute-done((bf16[2,1,32,320]{3,2,1,0:T(8,128)(2,1)S(1)}, bf16[2,1,32,320]{3,2,1,0:T(8,128)(2,1)S(1)}, u32[]{:S(2)}, u32[]{:S(2)}) %collective-permute-start.16) | collective-permute-done | bytes 40992 | tf_op jit(solution)/shard_map/ppermute | solution.py:172
  93.1 1.5 collective-permute-start.23
  96.3 9.0 %shard_map.129 = f32[2,512,640]{2,1,0:T(8,128)S(1)} custom-call(bf16[320,5760]{1,0:T(8,128)(2,1)} %get-tuple-element.17.kernel_ref, bf16[3,2,576,320]{3,2,1,0:T(8,128)(2,1)S(1)} %pad_maximum_fusion.e_ref), custom_call_target="tpu_custom_call" | custom-call | flops 3774873600 | bytes 8388608 | tf_op jit(solution)/shard_map/pallas_call | solution.py:135
  106.5 1.2 slice_bitcast_fusion
  107.7 5.3 %collective-permute-done.21 = bf16[2,8,2944]{2,1,0:T(8,128)(2,1)S(1)} collective-permute-done((bf16[2,8,2944]{2,1,0:T(8,128)(2,1)S(1)}, bf16[2,8,2944]{2,1,0:T(8,128)(2,1)S(1)}, u32[]{:S(2)}, u32[]{:S(2)}) %collective-permute-start.21) | collective-permute-done | bytes 94240 | tf_op jit(solution)/shard_map/ppermute | solution.py:240
  113.0 1.7 %collective-permute-start.22 = (bf16[8,2944]{1,0:T(8,128)(2,1)S(1)}, bf16[8,2944]{1,0:T(8,128)(2,1)S(1)}, u32[]{:S(2)}, u32[]{:S(2)}) collective-permute-start(bf16[8,2944]{1,0:T(8,128)(2,1)S(1)} %fusion.26), channel_id=1, source_target_pairs={{0,1},{1,0},{2,3},{3,2},{4,5},{5,4},{6,7},{7,6},{8,9},{9,8},{10,11... | collective-permute-start | bytes 141320 | tf_op jit(solution)/shard_map/ppermute | solution.py:242
  114.8 1.6 %convolution_convert_fusion = bf16[512,640]{1,0:T(8,128)(2,1)} fusion(bf16[320,512]{1,0:T(8,128)(2,1)S(1)} %collective-permute-done.15, bf16[320,512]{1,0:T(8,128)(2,1)S(1)} %get-tuple-element.48, pred[320,640]{1,0:T(32,128)(4,1)S(1)} %copy-done.10, pred[320,640]{1,0:T(32,128)(4,1)S(1)} %copy-done.12), kind=kOutput, calls=%fused_computation.11 | convolution fusion | flops 421478400 | bytes 1720320 | tf_op jit(solution)/shard_map/dot_general | solution.py:21
  116.9 8.3 %collective-permute-done.25 = bf16[128,2944]{1,0:T(8,128)(2,1)S(1)} collective-permute-done((bf16[128,2944]{1,0:T(8,128)(2,1)S(1)}, bf16[128,2944]{1,0:T(8,128)(2,1)S(1)}, u32[]{:S(2)}, u32[]{:S(2)}) %collective-permute-start.25) | collective-permute-done | bytes 753696 | tf_op jit(solution)/shard_map/ppermute | solution.py:242
  125.9 6.0 %collective-permute-done.24 = bf16[64,2944]{1,0:T(8,128)(2,1)S(1)} collective-permute-done((bf16[64,2944]{1,0:T(8,128)(2,1)S(1)}, bf16[64,2944]{1,0:T(8,128)(2,1)S(1)}, u32[]{:S(2)}, u32[]{:S(2)}) %collective-permute-start.24) | collective-permute-done | bytes 376864 | tf_op jit(solution)/shard_map/ppermute | solution.py:242
  132.1 0.9 collective-permute-done.26
  133.2 2.4 %collective-permute-start.27 = (bf16[32,2944]{1,0:T(8,128)(2,1)S(1)}, bf16[32,2944]{1,0:T(8,128)(2,1)S(1)}, u32[]{:S(2)}, u32[]{:S(2)}) collective-permute-start(bf16[32,2944]{1,0:T(8,128)(2,1)S(1)} %get-tuple-element.39), channel_id=1, source_target_pairs={{0,24},{2,26},{4,28},{6,30},{8,0},{10,2},{12,4},{14,6},{16,8},{18,... | collective-permute-start | bytes 565256 | tf_op jit(solution)/shard_map/ppermute | solution.py:241
  135.6 2.7 %collective-permute-start.28 = (bf16[32,2944]{1,0:T(8,128)(2,1)S(1)}, bf16[32,2944]{1,0:T(8,128)(2,1)S(1)}, u32[]{:S(2)}, u32[]{:S(2)}) collective-permute-start(bf16[32,2944]{1,0:T(8,128)(2,1)S(1)} %get-tuple-element.41), channel_id=1, source_target_pairs={{0,16},{2,18},{4,20},{6,22},{8,24},{10,26},{12,28},{14,30},{16,0},... | collective-permute-start | bytes 565256 | tf_op jit(solution)/shard_map/ppermute | solution.py:241
  138.3 4.1 %collective-permute-done.27 = bf16[32,2944]{1,0:T(8,128)(2,1)S(1)} collective-permute-done((bf16[32,2944]{1,0:T(8,128)(2,1)S(1)}, bf16[32,2944]{1,0:T(8,128)(2,1)S(1)}, u32[]{:S(2)}, u32[]{:S(2)}) %collective-permute-start.27) | collective-permute-done | bytes 188448 | tf_op jit(solution)/shard_map/ppermute | solution.py:241
  142.4 4.4 %collective-permute-done.29 = bf16[32,2944]{1,0:T(8,128)(2,1)S(1)} collective-permute-done((bf16[32,2944]{1,0:T(8,128)(2,1)S(1)}, bf16[32,2944]{1,0:T(8,128)(2,1)S(1)}, u32[]{:S(2)}, u32[]{:S(2)}) %collective-permute-start.29) | collective-permute-done | bytes 188448 | tf_op jit(solution)/shard_map/ppermute | solution.py:241
  146.8 4.9 %collective-permute-done.28 = bf16[32,2944]{1,0:T(8,128)(2,1)S(1)} collective-permute-done((bf16[32,2944]{1,0:T(8,128)(2,1)S(1)}, bf16[32,2944]{1,0:T(8,128)(2,1)S(1)}, u32[]{:S(2)}, u32[]{:S(2)}) %collective-permute-start.28) | collective-permute-done | bytes 188448 | tf_op jit(solution)/shard_map/ppermute | solution.py:241
  151.8 0.8 copy.55
  152.8 3.3 %divide_subtract_fusion = (f32[9,320,40]{1,2,0:T(8,128)}, f32[9,320,40]{1,2,0:T(8,128)}, f32[9,320,40]{1,2,0:T(8,128)}) fusion(f32[9,320,40]{1,2,0:T(8,128)} %param.11, f32[40,9,256]{2,0,1:T(8,128)} %bitcast.115, f32[40,9,64]{2,0,1:T(8,128)S(1)} %copy.41, pred[]{:T(512)S(6)} %eq.19, f32[9,320,40]{1,2,0:T(8,128)} %param.12, f32[9,320,40]{1,2,0:T(8,128)} %param.13), kind=kLoop, calls=%fused_computation.46 | loop fusion | flops 1612800 | bytes 3225601 | tf_op jit(solution)/shard_map/sub | solution.py:163
  156.1 2.3 %fusion.5 = bf16[512,640]{1,0:T(8,128)(2,1)} fusion(f32[512,640]{1,0:T(8,128)} %collective-permute-done.17, f32[2,512,640]{2,1,0:T(8,128)S(1)} %shard_map.129), kind=kLoop, calls=%fused_computation.16 | loop fusion | flops 655360 | bytes 3276800 | tf_op jit(solution)/shard_map/convert_element_type | solution.py:350
  (110 shorter events, 8.4 us)
Async XLA Ops:
  0.6 14.3 %copy-start = (bf16[1,16,32,640]{3,2,1,0:T(8,128)(2,1)S(1)}, bf16[1,16,32,640]{3,2,1,0:T(8,128)(2,1)}, u32[]{:S(2)}) copy-start(bf16[1,16,32,640]{3,2,1,0:T(8,128)(2,1)} %param.10) | copy-start | bytes 1966084
  0.6 13.9 %copy-start.13 = (s32[320]{0:T(512)S(1)}, s32[320]{0:T(512)}, u32[]{:S(2)}) copy-start(s32[320]{0:T(512)} %constant.107) | copy-start | bytes 3844
  0.7 13.9 %copy-start.14 = (s32[320]{0:T(512)S(1)}, s32[320]{0:T(512)}, u32[]{:S(2)}) copy-start(s32[320]{0:T(512)} %constant.93.clone) | copy-start | bytes 3844
  0.7 13.9 %copy-start.15 = (s32[320]{0:T(512)S(1)}, s32[320]{0:T(512)}, u32[]{:S(2)}) copy-start(s32[320]{0:T(512)} %constant.92.clone) | copy-start | bytes 3844
  0.7 11.7 %copy-start.8 = (bf16[1,16,32,640]{3,2,1,0:T(8,128)(2,1)S(1)}, bf16[1,16,32,640]{3,2,1,0:T(8,128)(2,1)}, u32[]{:S(2)}) copy-start(bf16[1,16,32,640]{3,2,1,0:T(8,128)(2,1)} %param.9) | copy-start | bytes 1966084
  4.4 18.3 %collective-permute-start.6 = (bf16[32,2944]{1,0:T(8,128)(2,1)S(1)}, bf16[32,2944]{1,0:T(8,128)(2,1)S(1)}, u32[]{:S(2)}, u32[]{:S(2)}) collective-permute-start(bf16[32,2944]{1,0:T(8,128)(2,1)S(1)} %get-tuple-element.55), channel_id=1, source_target_pairs={{0,16},{2,18},{4,20},{6,22},{8,24},{10,26},{12,28},{14,30},{16,0},... | collective-permute-start | bytes 565256 | tf_op jit(solution)/shard_map/ppermute | solution.py:241
  8.6 14.3 %collective-permute-start.5 = (bf16[32,2944]{1,0:T(8,128)(2,1)S(1)}, bf16[32,2944]{1,0:T(8,128)(2,1)S(1)}, u32[]{:S(2)}, u32[]{:S(2)}) collective-permute-start(bf16[32,2944]{1,0:T(8,128)(2,1)S(1)} %get-tuple-element.55), channel_id=1, source_target_pairs={{0,8},{2,10},{4,12},{6,14},{8,16},{10,18},{12,20},{14,22},{16,24},... | collective-permute-start | bytes 565256 | tf_op jit(solution)/shard_map/ppermute | solution.py:241
  10.1 20.1 %collective-permute-start.7 = (bf16[32,2944]{1,0:T(8,128)(2,1)S(1)}, bf16[32,2944]{1,0:T(8,128)(2,1)S(1)}, u32[]{:S(2)}, u32[]{:S(2)}) collective-permute-start(bf16[32,2944]{1,0:T(8,128)(2,1)S(1)} %get-tuple-element.55), channel_id=1, source_target_pairs={{0,24},{2,26},{4,28},{6,30},{8,0},{10,2},{12,4},{14,6},{16,8},{18,... | collective-permute-start | bytes 565256 | tf_op jit(solution)/shard_map/ppermute | solution.py:241
  12.4 4.1 %collective-permute-start.12 = (bf16[1,1,32,640]{3,2,1,0:T(8,128)(2,1)S(1)}, bf16[1,1,32,640]{3,2,1,0:T(8,128)(2,1)S(1)}, u32[]{:S(2)}, u32[]{:S(2)}) collective-permute-start(bf16[1,1,32,640]{3,2,1,0:T(8,128)(2,1)S(1)} %slice_select_fusion.1), channel_id=1, source_target_pairs={{0,1},{1,0},{2,3},{3,2},{4,5},{5,4},{6,7},{7,6},{8,9},{9,8},{10,11... | collective-permute-start | bytes 122888 | tf_op jit(solution)/shard_map/ppermute | solution.py:172
  14.0 4.1 %collective-permute-start = (bf16[8,2944]{1,0:T(8,128)(2,1)S(1)}, bf16[8,2944]{1,0:T(8,128)(2,1)S(1)}, u32[]{:S(2)}, u32[]{:S(2)}) collective-permute-start(bf16[8,2944]{1,0:T(8,128)(2,1)S(1)} %get-tuple-element.53), channel_id=1, source_target_pairs={{0,1},{1,0},{2,3},{3,2},{4,5},{5,4},{6,7},{7,6},{8,9},{9,8},{10,11... | collective-permute-start | bytes 141320 | tf_op jit(solution)/shard_map/ppermute | solution.py:242
  14.9 1.6 copy-start.9
  14.9 3.2 %copy-start.11 = (pred[320,640]{1,0:T(32,128)(4,1)}, pred[320,640]{1,0:T(32,128)(4,1)S(1)}, u32[]{:S(2)}) copy-start(pred[320,640]{1,0:T(32,128)(4,1)S(1)} %get-tuple-element.67) | copy-start | bytes 614404
  16.5 14.0 %collective-permute-start.14 = (bf16[320,512]{1,0:T(8,128)(2,1)S(1)}, bf16[320,512]{1,0:T(8,128)(2,1)S(1)}, u32[]{:S(2)}, u32[]{:S(2)}) collective-permute-start(bf16[320,512]{1,0:T(8,128)(2,1)S(1)} %get-tuple-element.51), channel_id=1, source_target_pairs={{0,2},{2,0},{4,6},{6,4},{8,10},{10,8},{12,14},{14,12},{16,18},{18,... | collective-permute-start | bytes 983048 | tf_op jit(solution)/shard_map/ppermute | solution.py:239
  18.1 4.6 %collective-permute-start.1 = (bf16[2,8,2944]{2,1,0:T(8,128)(2,1)S(1)}, bf16[2,8,2944]{2,1,0:T(8,128)(2,1)S(1)}, u32[]{:S(2)}, u32[]{:S(2)}) collective-permute-start(bf16[2,8,2944]{2,1,0:T(8,128)(2,1)S(1)} %get-tuple-element.59), channel_id=1, source_target_pairs={{0,4},{2,6},{4,0},{6,2},{8,12},{10,14},{12,8},{14,10},{16,20},{18,... | collective-permute-start | bytes 282632 | tf_op jit(solution)/shard_map/ppermute | solution.py:240
  22.7 28.4 %collective-permute-start.13 = (bf16[1,18,32,640]{3,2,1,0:T(8,128)(2,1)S(1)}, bf16[1,18,32,640]{3,2,1,0:T(8,128)(2,1)S(1)}, u32[]{:S(2)}, u32[]{:S(2)}) collective-permute-start(bf16[1,18,32,640]{3,2,1,0:T(8,128)(2,1)S(1)} %pad_maximum_fusion.8), channel_id=1, source_target_pairs={{0,2},{2,0},{4,6},{6,4},{8,10},{10,8},{12,14},{14,12},{16,18},{18,... | collective-permute-start | bytes 2211848 | tf_op jit(solution)/shard_map/ppermute | solution.py:239
  22.8 15.5 %collective-permute-start.3 = (bf16[2,2,8,2944]{3,2,0,1:T(8,128)(2,1)S(1)}, bf16[2,2,8,2944]{3,2,0,1:T(8,128)(2,1)S(1)}, u32[]{:S(2)}, u32[]{:S(2)}) collective-permute-start(bf16[2,2,8,2944]{3,2,0,1:T(8,128)(2,1)S(1)} %get-tuple-element.57), channel_id=1, source_target_pairs={{0,16},{2,18},{4,20},{6,22},{8,24},{10,26},{12,28},{14,30},{16,0},... | collective-permute-start | bytes 565256 | tf_op jit(solution)/shard_map/ppermute | solution.py:241
  22.9 16.9 %collective-permute-start.2 = (bf16[2,2,8,2944]{3,2,0,1:T(8,128)(2,1)S(1)}, bf16[2,2,8,2944]{3,2,0,1:T(8,128)(2,1)S(1)}, u32[]{:S(2)}, u32[]{:S(2)}) collective-permute-start(bf16[2,2,8,2944]{3,2,0,1:T(8,128)(2,1)S(1)} %get-tuple-element.57), channel_id=1, source_target_pairs={{0,8},{2,10},{4,12},{6,14},{8,16},{10,18},{12,20},{14,22},{16,24},... | collective-permute-start | bytes 565256 | tf_op jit(solution)/shard_map/ppermute | solution.py:241
  30.2 12.0 %collective-permute-start.4 = (bf16[2,2,8,2944]{3,2,0,1:T(8,128)(2,1)S(1)}, bf16[2,2,8,2944]{3,2,0,1:T(8,128)(2,1)S(1)}, u32[]{:S(2)}, u32[]{:S(2)}) collective-permute-start(bf16[2,2,8,2944]{3,2,0,1:T(8,128)(2,1)S(1)} %get-tuple-element.57), channel_id=1, source_target_pairs={{0,24},{2,26},{4,28},{6,30},{8,0},{10,2},{12,4},{14,6},{16,8},{18,... | collective-permute-start | bytes 565256 | tf_op jit(solution)/shard_map/ppermute | solution.py:241
  30.5 11.9 %collective-permute-start.8 = (bf16[4,16,2944]{2,1,0:T(8,128)(2,1)S(1)}, bf16[4,16,2944]{2,1,0:T(8,128)(2,1)S(1)}, u32[]{:S(2)}, u32[]{:S(2)}) collective-permute-start(bf16[4,16,2944]{2,1,0:T(8,128)(2,1)S(1)} %get-tuple-element.47), channel_id=1, source_target_pairs={{0,1},{1,0},{2,3},{3,2},{4,5},{5,4},{6,7},{7,6},{8,9},{9,8},{10,11... | collective-permute-start | bytes 1130504 | tf_op jit(solution)/shard_map/ppermute | solution.py:242
  38.3 11.6 %collective-permute-start.10 = (bf16[4,16,2944]{2,1,0:T(8,128)(2,1)S(1)}, bf16[4,16,2944]{2,1,0:T(8,128)(2,1)S(1)}, u32[]{:S(2)}, u32[]{:S(2)}) collective-permute-start(bf16[4,16,2944]{2,1,0:T(8,128)(2,1)S(1)} %get-tuple-element.46), channel_id=1, source_target_pairs={{0,4},{2,6},{4,0},{6,2},{8,12},{10,14},{12,8},{14,10},{16,20},{18,... | collective-permute-start | bytes 1130504 | tf_op jit(solution)/shard_map/ppermute | solution.py:240
  42.5 22.6 %collective-permute-start.9 = (bf16[2,4,16,2944]{3,2,1,0:T(8,128)(2,1)S(1)}, bf16[2,4,16,2944]{3,2,1,0:T(8,128)(2,1)S(1)}, u32[]{:S(2)}, u32[]{:S(2)}) collective-permute-start(bf16[2,4,16,2944]{3,2,1,0:T(8,128)(2,1)S(1)} %get-tuple-element.43), channel_id=1, source_target_pairs={{0,4},{2,6},{4,0},{6,2},{8,12},{10,14},{12,8},{14,10},{16,20},{18,... | collective-permute-start | bytes 2261000 | tf_op jit(solution)/shard_map/ppermute | solution.py:240
  50.0 17.0 %collective-permute-start.11 = (bf16[2,4,16,2944]{3,2,1,0:T(8,128)(2,1)S(1)}, bf16[2,4,16,2944]{3,2,1,0:T(8,128)(2,1)S(1)}, u32[]{:S(2)}, u32[]{:S(2)}) collective-permute-start(bf16[2,4,16,2944]{3,2,1,0:T(8,128)(2,1)S(1)} %pad_maximum_fusion.7), channel_id=1, source_target_pairs={{0,1},{1,0},{2,3},{3,2},{4,5},{5,4},{6,7},{7,6},{8,9},{9,8},{10,11... | collective-permute-start | bytes 2261000 | tf_op jit(solution)/shard_map/ppermute | solution.py:242
  85.9 0.9 copy-start.2
  86.8 0.9 copy-start.4
  87.6 0.9 copy-start.6
  88.9 4.2 %collective-permute-start.16 = (bf16[2,1,32,320]{3,2,1,0:T(8,128)(2,1)S(1)}, bf16[2,1,32,320]{3,2,1,0:T(8,128)(2,1)S(1)}, u32[]{:S(2)}, u32[]{:S(2)}) collective-permute-start(bf16[2,1,32,320]{3,2,1,0:T(8,128)(2,1)S(1)} %slice_select_fusion), channel_id=1, source_target_pairs={{0,1},{1,0},{2,3},{3,2},{4,5},{5,4},{6,7},{7,6},{8,9},{9,8},{10,11... | collective-permute-start | bytes 122888 | tf_op jit(solution)/shard_map/ppermute | solution.py:172
  89.4 16.0 %collective-permute-start.18 = (bf16[2,16,2944]{2,1,0:T(8,128)(2,1)}, bf16[2,16,2944]{2,1,0:T(8,128)(2,1)S(1)}, u32[]{:S(2)}, u32[]{:S(2)}) collective-permute-start(bf16[2,16,2944]{2,1,0:T(8,128)(2,1)} %get-tuple-element.20), channel_id=1, source_target_pairs={{0,24},{2,26},{4,28},{6,30},{8,0},{10,2},{12,4},{14,6},{16,8},{18,... | collective-permute-start | bytes 565256 | tf_op jit(solution)/shard_map/ppermute | solution.py:241
  89.5 16.4 %collective-permute-start.19 = (bf16[2,16,2944]{2,1,0:T(8,128)(2,1)}, bf16[2,16,2944]{2,1,0:T(8,128)(2,1)S(1)}, u32[]{:S(2)}, u32[]{:S(2)}) collective-permute-start(bf16[2,16,2944]{2,1,0:T(8,128)(2,1)} %get-tuple-element.21), channel_id=1, source_target_pairs={{0,16},{2,18},{4,20},{6,22},{8,24},{10,26},{12,28},{14,30},{16,0},... | collective-permute-start | bytes 565256 | tf_op jit(solution)/shard_map/ppermute | solution.py:241
  89.5 16.3 %collective-permute-start.20 = (bf16[2,16,2944]{2,1,0:T(8,128)(2,1)}, bf16[2,16,2944]{2,1,0:T(8,128)(2,1)S(1)}, u32[]{:S(2)}, u32[]{:S(2)}) collective-permute-start(bf16[2,16,2944]{2,1,0:T(8,128)(2,1)} %get-tuple-element.22), channel_id=1, source_target_pairs={{0,8},{2,10},{4,12},{6,14},{8,16},{10,18},{12,20},{14,22},{16,24},... | collective-permute-start | bytes 565256 | tf_op jit(solution)/shard_map/ppermute | solution.py:241
  91.5 23.3 %collective-permute-start.15 = (bf16[320,512]{1,0:T(8,128)(2,1)S(1)}, bf16[320,512]{1,0:T(8,128)(2,1)S(1)}, u32[]{:S(2)}, u32[]{:S(2)}) collective-permute-start(bf16[320,512]{1,0:T(8,128)(2,1)S(1)} %get-tuple-element.49), channel_id=1, source_target_pairs={{0,2},{2,0},{4,6},{6,4},{8,10},{10,8},{12,14},{14,12},{16,18},{18,... | collective-permute-start | bytes 983048 | tf_op jit(solution)/shard_map/ppermute | solution.py:239
  93.1 23.3 %collective-permute-start.23 = (bf16[2,64,2944]{2,1,0:T(8,128)(2,1)}, bf16[2,64,2944]{2,1,0:T(8,128)(2,1)S(1)}, u32[]{:S(2)}, u32[]{:S(2)}) collective-permute-start(bf16[2,64,2944]{2,1,0:T(8,128)(2,1)} %get-tuple-element.24), channel_id=1, source_target_pairs={{0,4},{2,6},{4,0},{6,2},{8,12},{10,14},{12,8},{14,10},{16,20},{18,... | collective-permute-start | bytes 2261000 | tf_op jit(solution)/shard_map/ppermute | solution.py:240
  96.3 9.1 %copy-start.7 = (bf16[128,2944]{1,0:T(8,128)(2,1)S(1)}, bf16[128,2944]{1,0:T(8,128)(2,1)}, u32[]{:S(2)}) copy-start(bf16[128,2944]{1,0:T(8,128)(2,1)} %copy-done.6) | copy-start | bytes 2260996
  105.3 9.4 %copy-start.10 = (pred[320,640]{1,0:T(32,128)(4,1)S(1)}, pred[320,640]{1,0:T(32,128)(4,1)}, u32[]{:S(2)}) copy-start(pred[320,640]{1,0:T(32,128)(4,1)} %copy-done.9) | copy-start | bytes 614404
  105.4 9.4 %copy-start.12 = (pred[320,640]{1,0:T(32,128)(4,1)S(1)}, pred[320,640]{1,0:T(32,128)(4,1)}, u32[]{:S(2)}) copy-start(pred[320,640]{1,0:T(32,128)(4,1)} %copy-done.11) | copy-start | bytes 614404
  105.4 19.8 %collective-permute-start.25 = (bf16[128,2944]{1,0:T(8,128)(2,1)S(1)}, bf16[128,2944]{1,0:T(8,128)(2,1)S(1)}, u32[]{:S(2)}, u32[]{:S(2)}) collective-permute-start(bf16[128,2944]{1,0:T(8,128)(2,1)S(1)} %copy-done.7), channel_id=1, source_target_pairs={{0,1},{1,0},{2,3},{3,2},{4,5},{5,4},{6,7},{7,6},{8,9},{9,8},{10,11... | collective-permute-start | bytes 2261000 | tf_op jit(solution)/shard_map/ppermute | solution.py:242
  105.9 7.0 %collective-permute-start.21 = (bf16[2,8,2944]{2,1,0:T(8,128)(2,1)S(1)}, bf16[2,8,2944]{2,1,0:T(8,128)(2,1)S(1)}, u32[]{:S(2)}, u32[]{:S(2)}) collective-permute-start(bf16[2,8,2944]{2,1,0:T(8,128)(2,1)S(1)} %fusion.24), channel_id=1, source_target_pairs={{0,4},{2,6},{4,0},{6,2},{8,12},{10,14},{12,8},{14,10},{16,20},{18,... | collective-permute-start | bytes 282632 | tf_op jit(solution)/shard_map/ppermute | solution.py:240
  107.7 8.7 %copy-start.5 = (bf16[2,64,2944]{2,1,0:T(8,128)(2,1)S(1)}, bf16[2,64,2944]{2,1,0:T(8,128)(2,1)}, u32[]{:S(2)}) copy-start(bf16[2,64,2944]{2,1,0:T(8,128)(2,1)} %copy-done.4) | copy-start | bytes 2260996
  107.7 48.4 %collective-permute-start.17 = (f32[512,640]{1,0:T(8,128)}, f32[512,640]{1,0:T(8,128)}, u32[]{:S(2)}, u32[]{:S(2)}) collective-permute-start(f32[512,640]{1,0:T(8,128)} %slice_bitcast_fusion), channel_id=1, source_target_pairs={{0,2},{2,0},{4,6},{6,4},{8,10},{10,8},{12,14},{14,12},{16,18},{18,... | collective-permute-start | bytes 3932168 | tf_op jit(solution)/shard_map/ppermute | solution.py:239
  113.0 12.3 %copy-start.3 = (bf16[128,2944]{1,0:T(8,128)(2,1)S(1)}, bf16[128,2944]{1,0:T(8,128)(2,1)}, u32[]{:S(2)}) copy-start(bf16[128,2944]{1,0:T(8,128)(2,1)} %copy-done.2) | copy-start | bytes 2260996
  113.0 25.3 %collective-permute-start.22 = (bf16[8,2944]{1,0:T(8,128)(2,1)S(1)}, bf16[8,2944]{1,0:T(8,128)(2,1)S(1)}, u32[]{:S(2)}, u32[]{:S(2)}) collective-permute-start(bf16[8,2944]{1,0:T(8,128)(2,1)S(1)} %fusion.26), channel_id=1, source_target_pairs={{0,1},{1,0},{2,3},{3,2},{4,5},{5,4},{6,7},{7,6},{8,9},{9,8},{10,11... | collective-permute-start | bytes 141320 | tf_op jit(solution)/shard_map/ppermute | solution.py:242
  116.5 15.4 %collective-permute-start.24 = (bf16[64,2944]{1,0:T(8,128)(2,1)S(1)}, bf16[64,2944]{1,0:T(8,128)(2,1)S(1)}, u32[]{:S(2)}, u32[]{:S(2)}) collective-permute-start(bf16[64,2944]{1,0:T(8,128)(2,1)S(1)} %fusion.13), channel_id=1, source_target_pairs={{0,1},{1,0},{2,3},{3,2},{4,5},{5,4},{6,7},{7,6},{8,9},{9,8},{10,11... | collective-permute-start | bytes 1130504 | tf_op jit(solution)/shard_map/ppermute | solution.py:242
  125.3 7.7 %collective-permute-start.26 = (bf16[64,2944]{1,0:T(8,128)(2,1)S(1)}, bf16[64,2944]{1,0:T(8,128)(2,1)S(1)}, u32[]{:S(2)}, u32[]{:S(2)}) collective-permute-start(bf16[64,2944]{1,0:T(8,128)(2,1)S(1)} %add_convert_fusion.1), channel_id=1, source_target_pairs={{0,4},{2,6},{4,0},{6,2},{8,12},{10,14},{12,8},{14,10},{16,20},{18,... | collective-permute-start | bytes 1130504 | tf_op jit(solution)/shard_map/ppermute | solution.py:240
  133.2 9.2 %collective-permute-start.27 = (bf16[32,2944]{1,0:T(8,128)(2,1)S(1)}, bf16[32,2944]{1,0:T(8,128)(2,1)S(1)}, u32[]{:S(2)}, u32[]{:S(2)}) collective-permute-start(bf16[32,2944]{1,0:T(8,128)(2,1)S(1)} %get-tuple-element.39), channel_id=1, source_target_pairs={{0,24},{2,26},{4,28},{6,30},{8,0},{10,2},{12,4},{14,6},{16,8},{18,... | collective-permute-start | bytes 565256 | tf_op jit(solution)/shard_map/ppermute | solution.py:241
  135.6 11.2 %collective-permute-start.29 = (bf16[32,2944]{1,0:T(8,128)(2,1)S(1)}, bf16[32,2944]{1,0:T(8,128)(2,1)S(1)}, u32[]{:S(2)}, u32[]{:S(2)}) collective-permute-start(bf16[32,2944]{1,0:T(8,128)(2,1)S(1)} %get-tuple-element.40), channel_id=1, source_target_pairs={{0,8},{2,10},{4,12},{6,14},{8,16},{10,18},{12,20},{14,22},{16,24},... | collective-permute-start | bytes 565256 | tf_op jit(solution)/shard_map/ppermute | solution.py:241
  135.6 16.1 %collective-permute-start.28 = (bf16[32,2944]{1,0:T(8,128)(2,1)S(1)}, bf16[32,2944]{1,0:T(8,128)(2,1)S(1)}, u32[]{:S(2)}, u32[]{:S(2)}) collective-permute-start(bf16[32,2944]{1,0:T(8,128)(2,1)S(1)} %get-tuple-element.41), channel_id=1, source_target_pairs={{0,16},{2,18},{4,20},{6,22},{8,24},{10,26},{12,28},{14,30},{16,0},... | collective-permute-start | bytes 565256 | tf_op jit(solution)/shard_map/ppermute | solution.py:241
  152.8 5.6 %copy-start.1 = (bf16[1,16,32,640]{3,2,1,0:T(8,128)(2,1)S(1)}, bf16[1,16,32,640]{3,2,1,0:T(8,128)(2,1)}, u32[]{:S(2)}) copy-start(bf16[1,16,32,640]{3,2,1,0:T(8,128)(2,1)} %param.10) | copy-start | bytes 1966084

commit v2 on v1

--- a/solution.py
+++ b/solution.py
@@ -14,7 +14,7 @@
 NN = (((1,), (0,)), ((), ()))
 VMEM_LIMIT = 48 << 20
 TAPS = 9
-ROUTES = (8, 16, 16)
+ROUTES = (8, 32)
 
 
 def mm(a, b, dims):
@@ -63,19 +63,30 @@
         ).astype(BF)
 
 
-def routed_kernel(width, half_ref, w_ref, x_ref, t_ref, k_ref, s_ref, e_ref, *outs):
-    a_refs, (b0_ref, b1_ref, c0_ref, c1_ref, mid_ref) = outs[:4], outs[4:]
-    first = half_ref[0]
-    second = 1 - first
-    low = lax.broadcasted_iota(jnp.int32, (w_ref.shape[1], 128), 1) < 64
+def routed_kernel(
+    width, place_ref, a0, a1, a2, a3, own_ref, near_ref, far_ref, x_ref, t_ref, k_ref, s_ref, e_ref, *outs
+):
+    g_refs, (keep_ref, send_ref, mid_ref) = outs[:4], outs[4:]
+    a_refs = (a0, a1, a2, a3)
+    first, on_core0 = place_ref[0] == 0, place_ref[1] == 0
+    rows = k_ref.shape[0]
+    low = lax.broadcasted_iota(jnp.int32, (rows, 128), 1) < 64
     spare = TAPS * 256
+
+    def load(at):
+        near, far = near_ref[:, at], far_ref[0, :, at]
+        own = [r[0, :, at] for r in a_refs] + [own_ref[:, at], jnp.where(on_core0, far, near)]
+        other = [r[1, :, at] for r in a_refs] + [jnp.where(on_core0, near, far), far_ref[1, :, at]]
+        own, other = jnp.concatenate(own), jnp.concatenate(other)
+        return jnp.where(first, own, other), jnp.where(first, other, own)
+
     for tap in range(TAPS):
-        k_ref[:, tap * 640 : tap * 640 + 256] = w_ref[first, :, tap * 256 : (tap + 1) * 256]
-        k_ref[:, tap * 640 + 384 : (tap + 1) * 640] = w_ref[second, :, tap * 256 : (tap + 1) * 256]
+        left, right = load(slice(tap * 256, (tap + 1) * 256))
+        k_ref[:, tap * 640 : tap * 640 + 256] = left
+        k_ref[:, tap * 640 + 384 : (tap + 1) * 640] = right
     for pair in range(5):
-        at = slice(spare + pair * 128, spare + (pair + 1) * 128)
-        left = w_ref[first, :, at].astype(F32)
-        right = w_ref[second, :, at].astype(F32)
+        left, right = load(slice(spare + pair * 128, spare + (pair + 1) * 128))
+        left, right = left.astype(F32), right.astype(F32)
         k_ref[:, 2 * pair * 640 + 256 : 2 * pair * 640 + 384] = jnp.where(
             low, left, pltpu.roll(right, 64, 1)
         ).astype(BF)
@@ -85,20 +96,17 @@
             ).astype(BF)
     conv_student(k_ref, x_ref, t_ref, s_ref, e_ref, width)
 
-    is_first = first == 0
-
-    def put(at, lo, hi):
-        own = jnp.where(is_first, lo, hi).astype(BF)
-        other = jnp.where(is_first, hi, lo).astype(BF)
+    def put(at, left, right):
+        left, right = left.astype(BF), right.astype(BF)
+        own, other = jnp.where(first, left, right), jnp.where(first, right, left)
         for s in range(4):
-            a_refs[s][0, :, at] = own[s * 16 : (s + 1) * 16]
-            a_refs[s][1, :, at] = other[s * 16 : (s + 1) * 16]
-        b0_ref[0, :, at] = own[64:128]
-        b0_ref[1, :, at] = other[64:128]
-        b1_ref[0, :, at] = own[128:192]
-        b1_ref[1, :, at] = other[128:192]
-        c0_ref[:, at] = own[192:]
-        c1_ref[:, at] = other[192:]
+            g_refs[s][0, :, at] = own[s * 16 : (s + 1) * 16]
+            g_refs[s][1, :, at] = other[s * 16 : (s + 1) * 16]
+        own_far, other_near = own[192:], other[64:192]
+        keep_ref[0, :, at] = own[64:192]
+        send_ref[1, :, at] = other[192:]
+        send_ref[0, :, at] = jnp.where(on_core0, own_far, other_near)
+        keep_ref[1, :, at] = jnp.where(on_core0, other_near, own_far)
 
     for tap in range(TAPS):
         grad = tap_grad(x_ref, e_ref, tap, width)
@@ -114,7 +122,7 @@
         )
 
 
-def back_kernel(width, kernel_ref, e_ref, out_ref):
+def back_kernel(width, kernel_ref, e_ref, *out_refs):
     channels = kernel_ref.shape[1] // TAPS
     cells = e_ref.shape[2] - 2 * width
     for l in range(e_ref.shape[1]):
@@ -127,7 +135,7 @@
                 NN,
             )
             total = term if total is None else total + term
-        out_ref[l] = total
+        out_refs[l][...] = total
 
 
 def vmem_call(kernel, outs, scalars, *args, scratch=()):
@@ -214,7 +222,7 @@
     error = error.T.reshape(b, band, width, total_out)
     back = vmem_call(
         functools.partial(back_kernel, width),
-        shape(b, band * width, channels, dtype=F32),
+        (shape(band * width, channels, dtype=F32),) * b,
         0,
         kernel,
         back_cells(with_halo(error)),
@@ -225,9 +233,18 @@
     grad = grad.transpose(1, 2, 0) / F32(b * lax.axis_size("dp"))
     return (
         student.T.reshape(latents.shape),
-        back.astype(BF).reshape(latents.shape),
+        jnp.stack(back).astype(BF).reshape(latents.shape),
         *adam(weight, moment1, moment2, grad),
     )
+
+
+def hop(pairs_of):
+    pairs = []
+    for i in range(32):
+        z, y, core, x = i // 8, i // 4 % 2, i // 2 % 2, i % 2
+        z, y, core, x = pairs_of(z, y, core, x)
+        pairs.append((i, ((z % 4 * 2 + y) * 2 + core) * 2 + x))
+    return lambda v: lax.ppermute(v, ("dp", "rows"), pairs)
 
 
 def routed_device(latents, target, weight, moment1, moment2):
@@ -236,11 +253,11 @@
     index = lax.axis_index("dp")
     core, y, z = index % 2, (index // 2) % 2, index // 4
     half = lax.axis_index("rows")
-    along_core = lambda v: lax.ppermute(v, "dp", [(i, i ^ 1) for i in range(16)])
-    along_y = lambda v: lax.ppermute(v, "dp", [(i, i ^ 2) for i in range(16)])
-    along_z = lambda v, s: lax.ppermute(v, "dp", [(i, (i + 4 * s) % 16) for i in range(16)])
-    along_x = lambda v: lax.ppermute(v, "rows", [(0, 1), (1, 0)])
-    ra, rb, rc = ROUTES
+    along_core = hop(lambda z, y, core, x: (z, y, 1 - core, x))
+    along_xy = hop(lambda z, y, core, x: (z, y ^ core, core, x ^ 1 ^ core))
+    along_yx = hop(lambda z, y, core, x: (z, y ^ 1 ^ core, core, x ^ core))
+    along_z = lambda v, s: hop(lambda z, y, core, x: (z + s, y, core, x))(v)
+    ra, rb = ROUTES
     lanes = TAPS * 256 + 640
 
     piece = weight.transpose(2, 0, 1)
@@ -254,49 +271,46 @@
         axis=1,
     )
 
-    pa, pbc = piece[:ra], piece[ra:]
-    zbc = jnp.stack([pbc] + [along_z(pbc, s) for s in (1, 2, 3)])
-    pa = jnp.stack([pa, along_x(pa)])
-    pa = jnp.stack([pa, along_y(pa)], axis=1)
-    pb, pc = zbc[:, :rb], zbc[:, rb:]
-    pb = jnp.stack([pb, along_x(pb)])
-    pc = jnp.stack([pc, along_y(pc)])
-    pa = jnp.stack([pa] + [along_z(pa, s) for s in (1, 2, 3)], axis=1)
-    pb = jnp.stack([pb, along_y(pb)], axis=1)
-    pc = jnp.stack([pc, along_x(pc)])
-    pieces = jnp.concatenate(
-        [pa.reshape(2, 8 * ra, lanes), pb.reshape(2, 8 * rb, lanes), pc.reshape(2, 8 * rc, lanes)],
-        axis=1,
-    )
-
-    order = []
-    for r, (off, count, axes) in enumerate(((0, ra, "sy"), (ra, rb, "ys"), (ra + rb, rc, "ys"))):
-        grid = np.indices((4, 2, count) if axes == "sy" else (2, 4, count)).reshape(3, -1)
-        s, yr = (grid[0], grid[1]) if axes == "sy" else (grid[1], grid[0])
-        order.append(np.stack([s, yr, off + grid[2]]))
-    order = np.concatenate(order, axis=1).astype(np.int32)
-    block = ((z - order[0]) % 4) * 4 + (y ^ order[1]) * 2
+    def turned(v):
+        return jnp.where(core == 0, v.swapaxes(0, 1), v)
+
+    pa, pb = piece[:ra], piece[ra:]
+    own = jnp.concatenate([pb] + [along_z(pb, s) for s in (1, 2, 3)])
+    pa = jnp.stack([pa, along_xy(pa)])
+    pa = turned(jnp.stack([pa, along_yx(pa)])).reshape(2, 2 * ra, lanes)
+    near = along_xy(own)
+    az = [pa] + [along_z(pa, s) for s in (1, 2, 3)]
+    far = along_yx(jnp.stack([own, near]))
+
+    at_a = np.indices((4, 2, ra)).reshape(3, -1)
+    at_b = np.indices((2, 4, rb)).reshape(3, -1)
+    dist_z = np.concatenate([at_a[0], at_b[1]]).astype(np.int32)
+    dist_y = np.concatenate([at_a[1], at_b[0]]).astype(np.int32)
+    within = np.concatenate([at_a[2], ra + at_b[2]]).astype(np.int32)
+    block = ((z - dist_z) % 4) * 4 + (y ^ dist_y) * 2
     per = weight.shape[2]
     everything = jnp.arange(channels, dtype=jnp.int32)
-    pick_own = ((block + core) * per + order[2])[:, None] == everything[None, :]
-    pick_other = ((block + 1 - core) * per + order[2])[:, None] == everything[None, :]
+    pick_own = ((block + core) * per + within)[:, None] == everything[None, :]
+    pick_other = ((block + 1 - core) * per + within)[:, None] == everything[None, :]
     pick = jnp.concatenate([pick_own, pick_other]).astype(BF)
-    rows = order.shape[1]
+    rows = within.shape[0]
 
     banded = with_halo(latents)
     x = wide_cells(jnp.concatenate([banded, along_core(banded)]))
     t = mm(pick, target.reshape(cells, channels), NT).astype(BF)
     t = jnp.concatenate([t[:rows], along_core(t[rows:])], axis=1)
 
-    kernel, student, error, a0, a1, a2, a3, b0, b1, c0, c1 = vmem_call(
+    kernel, student, error, g0, g1, g2, g3, keep, send = vmem_call(
         functools.partial(routed_kernel, width),
         (shape(rows, TAPS * channels), shape(rows, 2 * cells), shape(rows, 2 * cells))
         + (shape(2, 2 * ra, lanes),) * 4
-        + (shape(2, 4 * rb, lanes),) * 2
-        + (shape(8 * rc, lanes),) * 2,
+        + (shape(2, 4 * rb, lanes),) * 2,
         1,
-        half.astype(jnp.int32).reshape(1),
-        pieces,
+        jnp.stack([half, core]).astype(jnp.int32),
+        *az,
+        own,
+        near,
+        far,
         x,
         t,
         scratch=[pltpu.VMEM((TAPS, rows, 128), F32)],
@@ -308,25 +322,16 @@
             total = total + term.astype(F32)
         return total
 
-    gb = along_y(b1)
-    gc = along_x(c1)
-    az = [along_z(v, -s) for s, v in ((1, a1), (2, a2), (3, a3))]
-    gb_out = plus(b0[1], gb[1]).astype(BF)
-    gc = gc.reshape(2, 4 * rc, lanes)
-    c0 = c0.reshape(2, 4 * rc, lanes)
-    gc_out = plus(c0[1], gc[1]).astype(BF)
-    gb2 = along_x(gb_out)
-    gc2 = along_y(gc_out)
-    gb = plus(b0[0], gb[0], gb2).astype(BF).reshape(4, rb, lanes)
-    gc = plus(c0[0], gc[0], gc2).astype(BF).reshape(4, rc, lanes)
-    gbc = jnp.concatenate([gb, gc], axis=1)
-    bcz = [along_z(gbc[s], -s) for s in (1, 2, 3)]
-    ga = plus(a0, *az).reshape(2, 2, ra, lanes)
-    ga_in = along_y(ga[:, 1].astype(BF))
-    ga = plus(ga[:, 0], ga_in)
-    ga_in = along_x(ga[1].astype(BF))
+    got = along_yx(send)
+    az = [along_z(v, -s) for s, v in ((1, g1), (2, g2), (3, g3))]
+    got2 = along_xy(plus(keep[1], got[1]).astype(BF))
+    gb = plus(keep[0], got[0], got2).astype(BF).reshape(4, rb, lanes)
+    bz = [along_z(gb[s], -s) for s in (1, 2, 3)]
+    ga = turned(plus(g0, *az).reshape(2, 2, ra, lanes))
+    ga_in = along_yx(ga[1].astype(BF))
     ga = plus(ga[0], ga_in)
-    grad = jnp.concatenate([ga, plus(gbc[0], *bcz)], axis=0) / F32(b * lax.axis_size("dp"))
+    ga = plus(ga[0], along_xy(ga[1].astype(BF)))
+    grad = jnp.concatenate([ga, plus(gb[0], *bz)], axis=0) / F32(b * lax.axis_size("dp"))
     grad = jnp.concatenate(
         [
             grad[:, : TAPS * 256].reshape(-1, TAPS, 256),
@@ -340,14 +345,14 @@
     out = mm(both, pick, (((0,), (0,)), ((), ()))).astype(BF).reshape(latents.shape)
 
     error = error.T.reshape(2, band, width, rows)
-    back = vmem_call(
+    back_own, back_other = vmem_call(
         functools.partial(back_kernel, width),
-        shape(2, cells, channels, dtype=F32),
+        (shape(cells, channels, dtype=F32),) * 2,
         0,
         kernel,
         back_cells(with_halo(error)),
     )
-    input_grad = (back[0] + along_core(back[1])).astype(BF).reshape(latents.shape)
+    input_grad = (back_own + along_core(back_other)).astype(BF).reshape(latents.shape)
     return (out, input_grad, *adam(weight, moment1, moment2, grad))
 
 

time: 159 us -> 140 us (0.88)
  starting transfers between devices: 37.7 us -> 31.4 us
  other arithmetic: 16.7 us -> 10.5 us
  waiting for transfers between devices: 66.8 us -> 62 us
    ppermute x28 -> x24, starting transfers between devices: 35.7 us -> 28.3 us  [hop(): return lambda v: lax.ppermute(v, ('dp', 'rows'), pairs)]
    concatenate x1 -> x0, other arithmetic: 4.02 us -> none  [routed_device(): jnp.concatenate([pa.reshape(2, 8 * ra, lanes), pb.reshape(2, 8 * rb, lane...]
    ppermute x2, waiting for transfers between devices: 2.37 us -> 0.01 us  [with_halo(): got = lax.ppermute(edge, 'rows', [(0, 1), (1, 0)])]
    ppermute x28 -> x24, waiting for transfers between devices: 64.4 us -> 62 us  [hop(): return lambda v: lax.ppermute(v, ('dp', 'rows'), pairs)]
    sub x1, other arithmetic: 3.29 us -> 1.64 us  [adam(): new_weight = weight - 0.01 * new_moment1 / (jnp.sqrt(new_moment2) + 1e-08)]
  transfers between devices with their start and end apart: 30 -> 26, of which waited for: 16 -> 12; matrix products, arithmetic and copies ran while one was open for 10% -> 9% of each run, Pallas kernels for 6% -> 6%
where the time goes in v2:
time: 140 us
  waiting for transfers between devices  62 us (44%)
  starting transfers between devices  31.4 us (22%)
  Pallas kernels  23.7 us (17%)
  other arithmetic  10.5 us (8%)
  local copies, waits for them, and re-layouts  8.74 us (6%)
  matrix products  2.34 us (2%)
    ppermute x24, waiting for transfers between devices, hop(): return lambda v: lax.ppermute(v, ('dp', 'rows'), pairs)  62 us
    ppermute x24, starting transfers between devices, hop(): return lambda v: lax.ppermute(v, ('dp', 'rows'), pairs)  28.3 us
    pallas_call x2, Pallas kernels, vmem_call(): pl.pallas_call(kernel, out_shape=outs, in_specs=[pl.BlockSpec(memory_spac...  23.7 us
    ppermute x2, starting transfers between devices, with_halo(): got = lax.ppermute(edge, 'rows', [(0, 1), (1, 0)])  3.12 us
    unnamed x29, local copies, waits for them, and re-layouts  3.08 us
    concatenate x1, other arithmetic, wide_cells(): jnp.concatenate([column_shift(cells, k - 1) for k in range(3)], axis=3)  2.93 us
  transfers between devices with their start and end apart: 26, of which 12 were waited for; matrix products, arithmetic and copies ran while one was open for 9% of the time, Pallas kernels for 6%

profile of v2, /device:TPU:0, one launch (start us, length us, event | category | flops | bytes accessed | tf_op | source)
XLA Modules:
  0.0 139.8 jit_solution(1949141435011068076)
XLA Ops:
  0.6 1.0 slice.141
  1.7 1.2 slice.140
  2.9 1.2 fusion.10
  4.5 5.1 %collective-permute-start.7 = (bf16[32,2944]{1,0:T(8,128)(2,1)S(1)}, bf16[32,2944]{1,0:T(8,128)(2,1)}, u32[]{:S(2)}, u32[]{:S(2)}) collective-permute-start(bf16[32,2944]{1,0:T(8,128)(2,1)S(1)} %slice.145), channel_id=1, source_target_pairs={{0,24},{1,25},{2,26},{3,27},{4,28},{5,29},{6,30},{7,31},{8,0},{9,1... | collective-permute-start | bytes 565256 | tf_op jit(solution)/shard_map/ppermute | solution.py:247
  9.6 1.0 collective-permute-start.5
  10.6 1.6 %collective-permute-start.10 = (bf16[1,1,32,640]{3,2,1,0:T(8,128)(2,1)S(1)}, bf16[1,1,32,640]{3,2,1,0:T(8,128)(2,1)S(1)}, u32[]{:S(2)}, u32[]{:S(2)}) collective-permute-start(bf16[1,1,32,640]{3,2,1,0:T(8,128)(2,1)S(1)} %slice_select_fusion.1), channel_id=1, source_target_pairs={{0,1},{1,0},{2,3},{3,2},{4,5},{5,4},{6,7},{7,6},{8,9},{9,8},{10,11... | collective-permute-start | bytes 122888 | tf_op jit(solution)/shard_map/ppermute | solution.py:180
  12.2 0.6 collective-permute-start
  13.1 0.7 copy-done.6
  13.9 0.7 convolution_convert_fusion.1
  14.6 0.8 fusion.31
  15.6 0.7 collective-permute-done
  16.3 1.6 %collective-permute-start.1 = (bf16[2,8,2944]{2,1,0:T(8,128)(2,1)S(1)}, bf16[2,8,2944]{2,1,0:T(8,128)(2,1)S(1)}, u32[]{:S(2)}, u32[]{:S(2)}) collective-permute-start(bf16[2,8,2944]{2,1,0:T(8,128)(2,1)S(1)} %get-tuple-element.51), channel_id=1, source_target_pairs={{0,4},{1,5},{2,3},{3,2},{4,0},{5,1},{6,7},{7,6},{8,12},{9,13},{10,... | collective-permute-start | bytes 282632 | tf_op jit(solution)/shard_map/ppermute | solution.py:247
  17.9 7.8 %collective-permute-done.6 = bf16[32,2944]{1,0:T(8,128)(2,1)} collective-permute-done((bf16[32,2944]{1,0:T(8,128)(2,1)S(1)}, bf16[32,2944]{1,0:T(8,128)(2,1)}, u32[]{:S(2)}, u32[]{:S(2)}) %collective-permute-start.6) | collective-permute-done | bytes 188448 | tf_op jit(solution)/shard_map/ppermute | solution.py:247
  25.7 1.2 fusion.25
  26.9 1.6 %collective-permute-start.8 = (bf16[128,2944]{1,0:T(8,128)(2,1)S(1)}, bf16[128,2944]{1,0:T(8,128)(2,1)S(1)}, u32[]{:S(2)}, u32[]{:S(2)}) collective-permute-start(bf16[128,2944]{1,0:T(8,128)(2,1)S(1)} %get-tuple-element.43.own_ref), channel_id=1, source_target_pairs={{0,1},{1,0},{2,6},{3,7},{4,5},{5,4},{6,2},{7,3},{8,9},{9,8},{10,14... | collective-permute-start | bytes 2261000 | tf_op jit(solution)/shard_map/ppermute | solution.py:247
  28.5 0.6 collective-permute-start.4
  29.1 2.3 %collective-permute-start.3 = (bf16[2,16,2944]{2,1,0:T(8,128)(2,1)S(1)}, bf16[2,16,2944]{2,1,0:T(8,128)(2,1)S(1)}, u32[]{:S(2)}, u32[]{:S(2)}) collective-permute-start(bf16[2,16,2944]{2,1,0:T(8,128)(2,1)S(1)} %fusion.13.a0), channel_id=1, source_target_pairs={{0,16},{1,17},{2,18},{3,19},{4,20},{5,21},{6,22},{7,23},{8,24},{9,... | collective-permute-start | bytes 565256 | tf_op jit(solution)/shard_map/ppermute | solution.py:247
  31.4 7.2 %collective-permute-done.8.near_ref = bf16[128,2944]{1,0:T(8,128)(2,1)S(1)} collective-permute-done((bf16[128,2944]{1,0:T(8,128)(2,1)S(1)}, bf16[128,2944]{1,0:T(8,128)(2,1)S(1)}, u32[]{:S(2)}, u32[]{:S(2)}) %collective-permute-start.8) | collective-permute-done | bytes 753696 | tf_op jit(solution)/shard_map/ppermute | solution.py:247
  38.6 0.8 collective-permute-start.2
  39.5 1.6 %collective-permute-start.9 = (bf16[2,128,2944]{2,1,0:T(8,128)(2,1)S(1)}, bf16[2,128,2944]{2,1,0:T(8,128)(2,1)S(1)}, u32[]{:S(2)}, u32[]{:S(2)}) collective-permute-start(bf16[2,128,2944]{2,1,0:T(8,128)(2,1)S(1)} %pad_maximum_fusion.1), channel_id=1, source_target_pairs={{0,4},{1,5},{2,3},{3,2},{4,0},{5,1},{6,7},{7,6},{8,12},{9,13},{10,... | collective-permute-start | bytes 4521992 | tf_op jit(solution)/shard_map/ppermute | solution.py:247
  41.4 0.8 fusion.27
  42.2 2.9 %fusion.2 = bf16[2,18,32,1920]{3,2,1,0:T(8,128)(2,1)} fusion(bf16[2,18,31,640]{3,2,1,0:T(8,128)(2,1)S(1)} %get-tuple-element.36, bf16[2,18,31,640]{3,2,1,0:T(8,128)(2,1)S(1)} %get-tuple-element.35, bf16[1,18,32,640]{3,2,1,0:T(8,128)(2,1)S(1)} %collective-permute-done.11, bf16[1,1,32,640]{3,2,1,0:T(8,128)(2,1)S(1)} %get-tuple-element.55, ...), kind=kLoop, calls=%fused_computation.4 | loop fusion | flops 35389440 | bytes 8755200 | tf_op jit(solution)/shard_map/concatenate | solution.py:192
  45.1 2.2 %collective-permute-done.3.a2 = bf16[2,16,2944]{2,1,0:T(8,128)(2,1)S(1)} collective-permute-done((bf16[2,16,2944]{2,1,0:T(8,128)(2,1)S(1)}, bf16[2,16,2944]{2,1,0:T(8,128)(2,1)S(1)}, u32[]{:S(2)}, u32[]{:S(2)}) %collective-permute-start.3) | collective-permute-done | bytes 188448 | tf_op jit(solution)/shard_map/ppermute | solution.py:247
  47.4 12.0 %collective-permute-done.9.far_ref = bf16[2,128,2944]{2,1,0:T(8,128)(2,1)S(1)} collective-permute-done((bf16[2,128,2944]{2,1,0:T(8,128)(2,1)S(1)}, bf16[2,128,2944]{2,1,0:T(8,128)(2,1)S(1)}, u32[]{:S(2)}, u32[]{:S(2)}) %collective-permute-start.9) | collective-permute-done | bytes 1507360 | tf_op jit(solution)/shard_map/ppermute | solution.py:247
  59.3 1.2 copy-done.13
  60.5 14.7 %shard_map.119 = (bf16[320,5760]{1,0:T(8,128)(2,1)}, bf16[320,1024]{1,0:T(8,128)(2,1)S(1)}, bf16[320,1024]{1,0:T(8,128)(2,1)S(1)}, bf16[2,16,2944]{2,1,0:T(8,128...) custom-call(s32[2]{0:T(128)S(1)} %pad_add_fusion.3.place_ref, ...), custom_call_target="tpu_custom_call" | custom-call | flops 3774873600 | bytes 8388608 | tf_op jit(solution)/shard_map/pallas_call | solution.py:143
  75.6 1.6 %collective-permute-start.14 = (bf16[2,1,32,320]{3,2,1,0:T(8,128)(2,1)S(1)}, bf16[2,1,32,320]{3,2,1,0:T(8,128)(2,1)S(1)}, u32[]{:S(2)}, u32[]{:S(2)}) collective-permute-start(bf16[2,1,32,320]{3,2,1,0:T(8,128)(2,1)S(1)} %slice_select_fusion), channel_id=1, source_target_pairs={{0,1},{1,0},{2,3},{3,2},{4,5},{5,4},{6,7},{7,6},{8,9},{9,8},{10,11... | collective-permute-start | bytes 122888 | tf_op jit(solution)/shard_map/ppermute | solution.py:180
  77.2 3.1 %collective-permute-start.16 = (bf16[2,16,2944]{2,1,0:T(8,128)(2,1)S(1)}, bf16[2,16,2944]{2,1,0:T(8,128)(2,1)S(1)}, u32[]{:S(2)}, u32[]{:S(2)}) collective-permute-start(bf16[2,16,2944]{2,1,0:T(8,128)(2,1)S(1)} %get-tuple-element.22), channel_id=1, source_target_pairs={{0,24},{1,25},{2,26},{3,27},{4,28},{5,29},{6,30},{7,31},{8,0},{9,1... | collective-permute-start | bytes 565256 | tf_op jit(solution)/shard_map/ppermute | solution.py:247
  80.3 1.0 collective-permute-start.17
  81.3 1.6 %collective-permute-start.21 = (bf16[2,128,2944]{2,1,0:T(8,128)(2,1)}, bf16[2,128,2944]{2,1,0:T(8,128)(2,1)S(1)}, u32[]{:S(2)}, u32[]{:S(2)}) collective-permute-start(bf16[2,128,2944]{2,1,0:T(8,128)(2,1)} %get-tuple-element.26), channel_id=1, source_target_pairs={{0,4},{1,5},{2,3},{3,2},{4,0},{5,1},{6,7},{7,6},{8,12},{9,13},{10,... | collective-permute-start | bytes 4521992 | tf_op jit(solution)/shard_map/ppermute | solution.py:247
  83.1 0.5 fusion.28
  84.0 0.6 pad_maximum_fusion.e_ref
  84.6 0.8 collective-permute-done.16
  85.4 9.5 %collective-permute-done.17 = bf16[2,16,2944]{2,1,0:T(8,128)(2,1)S(1)} collective-permute-done((bf16[2,16,2944]{2,1,0:T(8,128)(2,1)S(1)}, bf16[2,16,2944]{2,1,0:T(8,128)(2,1)S(1)}, u32[]{:S(2)}, u32[]{:S(2)}) %collective-permute-start.17) | collective-permute-done | bytes 188448 | tf_op jit(solution)/shard_map/ppermute | solution.py:247
  95.1 1.6 %collective-permute-start.19 = (bf16[2,8,2944]{2,1,0:T(8,128)(2,1)S(1)}, bf16[2,8,2944]{2,1,0:T(8,128)(2,1)S(1)}, u32[]{:S(2)}, u32[]{:S(2)}) collective-permute-start(bf16[2,8,2944]{2,1,0:T(8,128)(2,1)S(1)} %fusion.15), channel_id=1, source_target_pairs={{0,4},{1,5},{2,3},{3,2},{4,0},{5,1},{6,7},{7,6},{8,12},{9,13},{10,... | collective-permute-start | bytes 282632 | tf_op jit(solution)/shard_map/ppermute | solution.py:247
  96.7 9.0 %shard_map.120 = (f32[512,640]{1,0:T(8,128)S(1)}, f32[512,640]{1,0:T(8,128)S(1)}) custom-call(bf16[320,5760]{1,0:T(8,128)(2,1)} %get-tuple-element.17.kernel_ref, bf16[3,2,576,320]{3,2,1,0:T(8,128)(2,1)S(1)} %pad_maximum_fusion.e_ref), custom_call_target="tpu_custom_call" | custom-call | flops 3774873600 | bytes 8388608 | tf_op jit(solution)/shard_map/pallas_call | solution.py:143
  105.9 0.6 collective-permute-start.20
  106.6 1.6 %collective-permute-start.22 = (bf16[128,2944]{1,0:T(8,128)(2,1)S(1)}, bf16[128,2944]{1,0:T(8,128)(2,1)S(1)}, u32[]{:S(2)}, u32[]{:S(2)}) collective-permute-start(bf16[128,2944]{1,0:T(8,128)(2,1)S(1)} %fusion.5), channel_id=1, source_target_pairs={{0,1},{1,0},{2,6},{3,7},{4,5},{5,4},{6,2},{7,3},{8,9},{9,8},{10,14... | collective-permute-start | bytes 2261000 | tf_op jit(solution)/shard_map/ppermute | solution.py:247
  108.2 1.6 %convolution_convert_fusion = bf16[512,640]{1,0:T(8,128)(2,1)} fusion(bf16[320,512]{1,0:T(8,128)(2,1)S(1)} %collective-permute-done.13, bf16[320,512]{1,0:T(8,128)(2,1)S(1)} %get-tuple-element.44, pred[320,640]{1,0:T(32,128)(4,1)S(1)} %copy-done.7, pred[320,640]{1,0:T(32,128)(4,1)S(1)} %copy-done.9), kind=kOutput, calls=%fused_computation.13 | convolution fusion | flops 421478400 | bytes 1720320 | tf_op jit(solution)/shard_map/dot_general | solution.py:21
  110.0 8.3 %collective-permute-done.22 = bf16[128,2944]{1,0:T(8,128)(2,1)S(1)} collective-permute-done((bf16[128,2944]{1,0:T(8,128)(2,1)S(1)}, bf16[128,2944]{1,0:T(8,128)(2,1)S(1)}, u32[]{:S(2)}, u32[]{:S(2)}) %collective-permute-start.22) | collective-permute-done | bytes 753696 | tf_op jit(solution)/shard_map/ppermute | solution.py:247
  119.0 1.8 %collective-permute-start.25 = (bf16[32,2944]{1,0:T(8,128)(2,1)S(1)}, bf16[32,2944]{1,0:T(8,128)(2,1)S(1)}, u32[]{:S(2)}, u32[]{:S(2)}) collective-permute-start(bf16[32,2944]{1,0:T(8,128)(2,1)S(1)} %get-tuple-element.40), channel_id=1, source_target_pairs={{0,8},{1,9},{2,10},{3,11},{4,12},{5,13},{6,14},{7,15},{8,16},{9,17... | collective-permute-start | bytes 565256 | tf_op jit(solution)/shard_map/ppermute | solution.py:247
  120.8 1.5 %collective-permute-start.24 = (bf16[32,2944]{1,0:T(8,128)(2,1)S(1)}, bf16[32,2944]{1,0:T(8,128)(2,1)S(1)}, u32[]{:S(2)}, u32[]{:S(2)}) collective-permute-start(bf16[32,2944]{1,0:T(8,128)(2,1)S(1)} %get-tuple-element.41), channel_id=1, source_target_pairs={{0,16},{1,17},{2,18},{3,19},{4,20},{5,21},{6,22},{7,23},{8,24},{9,... | collective-permute-start | bytes 565256 | tf_op jit(solution)/shard_map/ppermute | solution.py:247
  122.4 1.0 add_convert_fusion.1
  123.3 5.4 %collective-permute-done.23 = bf16[32,2944]{1,0:T(8,128)(2,1)S(1)} collective-permute-done((bf16[32,2944]{1,0:T(8,128)(2,1)S(1)}, bf16[32,2944]{1,0:T(8,128)(2,1)S(1)}, u32[]{:S(2)}, u32[]{:S(2)}) %collective-permute-start.23) | collective-permute-done | bytes 188448 | tf_op jit(solution)/shard_map/ppermute | solution.py:247
  128.7 2.9 %collective-permute-done.25 = bf16[32,2944]{1,0:T(8,128)(2,1)S(1)} collective-permute-done((bf16[32,2944]{1,0:T(8,128)(2,1)S(1)}, bf16[32,2944]{1,0:T(8,128)(2,1)S(1)}, u32[]{:S(2)}, u32[]{:S(2)}) %collective-permute-start.25) | collective-permute-done | bytes 188448 | tf_op jit(solution)/shard_map/ppermute | solution.py:247
  131.6 5.1 %collective-permute-done.24 = bf16[32,2944]{1,0:T(8,128)(2,1)S(1)} collective-permute-done((bf16[32,2944]{1,0:T(8,128)(2,1)S(1)}, bf16[32,2944]{1,0:T(8,128)(2,1)S(1)}, u32[]{:S(2)}, u32[]{:S(2)}) %collective-permute-start.24) | collective-permute-done | bytes 188448 | tf_op jit(solution)/shard_map/ppermute | solution.py:247
  137.1 0.8 copy-done.2
  138.2 1.6 %divide_subtract_fusion = (f32[9,320,40]{1,2,0:T(8,128)}, f32[9,320,40]{1,2,0:T(8,128)}, f32[9,320,40]{1,2,0:T(8,128)}) fusion(f32[9,320,40]{1,2,0:T(8,128)S(1)} %copy-done.2, f32[40,9,256]{2,0,1:T(8,128)S(1)} %bitcast.79, f32[40,9,64]{2,0,1:T(8,128)S(1)} %copy.40, pred[]{:T(512)S(6)} %eq.22, f32[9,320,40]{1,2,0:T(8,128)S(1)} %copy-done.4, ...), kind=kLoop, calls=%fused_computation.32 | loop fusion | flops 1612800 | bytes 3225601 | tf_op jit(solution)/shard_map/sub | solution.py:171
  (90 shorter events, 4.5 us)
Async XLA Ops:
  0.6 12.5 %copy-start = (bf16[1,16,32,640]{3,2,1,0:T(8,128)(2,1)S(1)}, bf16[1,16,32,640]{3,2,1,0:T(8,128)(2,1)}, u32[]{:S(2)}) copy-start(bf16[1,16,32,640]{3,2,1,0:T(8,128)(2,1)} %param.9) | copy-start | bytes 1966084
  2.8 7.8 %copy-start.1 = (bf16[1,16,32,640]{3,2,1,0:T(8,128)(2,1)S(1)}, bf16[1,16,32,640]{3,2,1,0:T(8,128)(2,1)}, u32[]{:S(2)}) copy-start(bf16[1,16,32,640]{3,2,1,0:T(8,128)(2,1)} %param.8) | copy-start | bytes 1966084
  4.1 8.7 %copy-start.10 = (s32[320]{0:T(512)S(1)}, s32[320]{0:T(512)}, u32[]{:S(2)}) copy-start(s32[320]{0:T(512)} %constant.107) | copy-start | bytes 3844
  4.1 8.7 %copy-start.11 = (s32[320]{0:T(512)S(1)}, s32[320]{0:T(512)}, u32[]{:S(2)}) copy-start(s32[320]{0:T(512)} %constant.93.clone) | copy-start | bytes 3844
  4.1 8.7 %copy-start.12 = (s32[320]{0:T(512)S(1)}, s32[320]{0:T(512)}, u32[]{:S(2)}) copy-start(s32[320]{0:T(512)} %constant.92.clone) | copy-start | bytes 3844
  4.5 11.9 %collective-permute-start.7 = (bf16[32,2944]{1,0:T(8,128)(2,1)S(1)}, bf16[32,2944]{1,0:T(8,128)(2,1)}, u32[]{:S(2)}, u32[]{:S(2)}) collective-permute-start(bf16[32,2944]{1,0:T(8,128)(2,1)S(1)} %slice.145), channel_id=1, source_target_pairs={{0,24},{1,25},{2,26},{3,27},{4,28},{5,29},{6,30},{7,31},{8,0},{9,1... | collective-permute-start | bytes 565256 | tf_op jit(solution)/shard_map/ppermute | solution.py:247
  9.6 16.1 %collective-permute-start.6 = (bf16[32,2944]{1,0:T(8,128)(2,1)S(1)}, bf16[32,2944]{1,0:T(8,128)(2,1)}, u32[]{:S(2)}, u32[]{:S(2)}) collective-permute-start(bf16[32,2944]{1,0:T(8,128)(2,1)S(1)} %slice.145), channel_id=1, source_target_pairs={{0,16},{1,17},{2,18},{3,19},{4,20},{5,21},{6,22},{7,23},{8,24},{9,... | collective-permute-start | bytes 565256 | tf_op jit(solution)/shard_map/ppermute | solution.py:247
  9.6 16.1 %collective-permute-start.5 = (bf16[32,2944]{1,0:T(8,128)(2,1)S(1)}, bf16[32,2944]{1,0:T(8,128)(2,1)}, u32[]{:S(2)}, u32[]{:S(2)}) collective-permute-start(bf16[32,2944]{1,0:T(8,128)(2,1)S(1)} %slice.145), channel_id=1, source_target_pairs={{0,8},{1,9},{2,10},{3,11},{4,12},{5,13},{6,14},{7,15},{8,16},{9,17... | collective-permute-start | bytes 565256 | tf_op jit(solution)/shard_map/ppermute | solution.py:247
  10.6 4.8 %collective-permute-start.10 = (bf16[1,1,32,640]{3,2,1,0:T(8,128)(2,1)S(1)}, bf16[1,1,32,640]{3,2,1,0:T(8,128)(2,1)S(1)}, u32[]{:S(2)}, u32[]{:S(2)}) collective-permute-start(bf16[1,1,32,640]{3,2,1,0:T(8,128)(2,1)S(1)} %slice_select_fusion.1), channel_id=1, source_target_pairs={{0,1},{1,0},{2,3},{3,2},{4,5},{5,4},{6,7},{7,6},{8,9},{9,8},{10,11... | collective-permute-start | bytes 122888 | tf_op jit(solution)/shard_map/ppermute | solution.py:180
  12.2 4.1 %collective-permute-start = (bf16[8,2944]{1,0:T(8,128)(2,1)S(1)}, bf16[8,2944]{1,0:T(8,128)(2,1)S(1)}, u32[]{:S(2)}, u32[]{:S(2)}) collective-permute-start(bf16[8,2944]{1,0:T(8,128)(2,1)S(1)} %get-tuple-element.49), channel_id=1, source_target_pairs={{0,1},{1,0},{2,6},{3,7},{4,5},{5,4},{6,2},{7,3},{8,9},{9,8},{10,14... | collective-permute-start | bytes 141320 | tf_op jit(solution)/shard_map/ppermute | solution.py:247
  13.1 0.7 copy-start.6
  13.1 0.7 copy-start.8
  15.4 24.1 %collective-permute-start.12 = (bf16[320,512]{1,0:T(8,128)(2,1)}, bf16[320,512]{1,0:T(8,128)(2,1)S(1)}, u32[]{:S(2)}, u32[]{:S(2)}) collective-permute-start(bf16[320,512]{1,0:T(8,128)(2,1)} %get-tuple-element.47), channel_id=1, source_target_pairs={{0,2},{1,3},{2,0},{3,1},{4,6},{5,7},{6,4},{7,5},{8,10},{9,11},{10,... | collective-permute-start | bytes 983048 | tf_op jit(solution)/shard_map/ppermute | solution.py:247
  16.3 24.9 %collective-permute-start.11 = (bf16[1,18,32,640]{3,2,1,0:T(8,128)(2,1)S(1)}, bf16[1,18,32,640]{3,2,1,0:T(8,128)(2,1)S(1)}, u32[]{:S(2)}, u32[]{:S(2)}) collective-permute-start(bf16[1,18,32,640]{3,2,1,0:T(8,128)(2,1)S(1)} %pad_maximum_fusion.5), channel_id=1, source_target_pairs={{0,2},{1,3},{2,0},{3,1},{4,6},{5,7},{6,4},{7,5},{8,10},{9,11},{10,... | collective-permute-start | bytes 2211848 | tf_op jit(solution)/shard_map/ppermute | solution.py:247
  16.3 12.1 %collective-permute-start.1 = (bf16[2,8,2944]{2,1,0:T(8,128)(2,1)S(1)}, bf16[2,8,2944]{2,1,0:T(8,128)(2,1)S(1)}, u32[]{:S(2)}, u32[]{:S(2)}) collective-permute-start(bf16[2,8,2944]{2,1,0:T(8,128)(2,1)S(1)} %get-tuple-element.51), channel_id=1, source_target_pairs={{0,4},{1,5},{2,3},{3,2},{4,0},{5,1},{6,7},{7,6},{8,12},{9,13},{10,... | collective-permute-start | bytes 282632 | tf_op jit(solution)/shard_map/ppermute | solution.py:247
  26.9 11.7 %collective-permute-start.8 = (bf16[128,2944]{1,0:T(8,128)(2,1)S(1)}, bf16[128,2944]{1,0:T(8,128)(2,1)S(1)}, u32[]{:S(2)}, u32[]{:S(2)}) collective-permute-start(bf16[128,2944]{1,0:T(8,128)(2,1)S(1)} %get-tuple-element.43.own_ref), channel_id=1, source_target_pairs={{0,1},{1,0},{2,6},{3,7},{4,5},{5,4},{6,2},{7,3},{8,9},{9,8},{10,14... | collective-permute-start | bytes 2261000 | tf_op jit(solution)/shard_map/ppermute | solution.py:247
  28.5 16.6 %collective-permute-start.4 = (bf16[2,16,2944]{2,1,0:T(8,128)(2,1)S(1)}, bf16[2,16,2944]{2,1,0:T(8,128)(2,1)S(1)}, u32[]{:S(2)}, u32[]{:S(2)}) collective-permute-start(bf16[2,16,2944]{2,1,0:T(8,128)(2,1)S(1)} %fusion.13.a0), channel_id=1, source_target_pairs={{0,24},{1,25},{2,26},{3,27},{4,28},{5,29},{6,30},{7,31},{8,0},{9,1... | collective-permute-start | bytes 565256 | tf_op jit(solution)/shard_map/ppermute | solution.py:247
  29.1 18.2 %collective-permute-start.3 = (bf16[2,16,2944]{2,1,0:T(8,128)(2,1)S(1)}, bf16[2,16,2944]{2,1,0:T(8,128)(2,1)S(1)}, u32[]{:S(2)}, u32[]{:S(2)}) collective-permute-start(bf16[2,16,2944]{2,1,0:T(8,128)(2,1)S(1)} %fusion.13.a0), channel_id=1, source_target_pairs={{0,16},{1,17},{2,18},{3,19},{4,20},{5,21},{6,22},{7,23},{8,24},{9,... | collective-permute-start | bytes 565256 | tf_op jit(solution)/shard_map/ppermute | solution.py:247
  38.6 8.8 %collective-permute-start.2 = (bf16[2,16,2944]{2,1,0:T(8,128)(2,1)S(1)}, bf16[2,16,2944]{2,1,0:T(8,128)(2,1)S(1)}, u32[]{:S(2)}, u32[]{:S(2)}) collective-permute-start(bf16[2,16,2944]{2,1,0:T(8,128)(2,1)S(1)} %fusion.13.a0), channel_id=1, source_target_pairs={{0,8},{1,9},{2,10},{3,11},{4,12},{5,13},{6,14},{7,15},{8,16},{9,17... | collective-permute-start | bytes 565256 | tf_op jit(solution)/shard_map/ppermute | solution.py:247
  39.5 19.8 %collective-permute-start.9 = (bf16[2,128,2944]{2,1,0:T(8,128)(2,1)S(1)}, bf16[2,128,2944]{2,1,0:T(8,128)(2,1)S(1)}, u32[]{:S(2)}, u32[]{:S(2)}) collective-permute-start(bf16[2,128,2944]{2,1,0:T(8,128)(2,1)S(1)} %pad_maximum_fusion.1), channel_id=1, source_target_pairs={{0,4},{1,5},{2,3},{3,2},{4,0},{5,1},{6,7},{7,6},{8,12},{9,13},{10,... | collective-permute-start | bytes 4521992 | tf_op jit(solution)/shard_map/ppermute | solution.py:247
  59.3 1.2 copy-start.13
  75.6 5.7 %collective-permute-start.14 = (bf16[2,1,32,320]{3,2,1,0:T(8,128)(2,1)S(1)}, bf16[2,1,32,320]{3,2,1,0:T(8,128)(2,1)S(1)}, u32[]{:S(2)}, u32[]{:S(2)}) collective-permute-start(bf16[2,1,32,320]{3,2,1,0:T(8,128)(2,1)S(1)} %slice_select_fusion), channel_id=1, source_target_pairs={{0,1},{1,0},{2,3},{3,2},{4,5},{5,4},{6,7},{7,6},{8,9},{9,8},{10,11... | collective-permute-start | bytes 122888 | tf_op jit(solution)/shard_map/ppermute | solution.py:180
  77.2 8.3 %collective-permute-start.16 = (bf16[2,16,2944]{2,1,0:T(8,128)(2,1)S(1)}, bf16[2,16,2944]{2,1,0:T(8,128)(2,1)S(1)}, u32[]{:S(2)}, u32[]{:S(2)}) collective-permute-start(bf16[2,16,2944]{2,1,0:T(8,128)(2,1)S(1)} %get-tuple-element.22), channel_id=1, source_target_pairs={{0,24},{1,25},{2,26},{3,27},{4,28},{5,29},{6,30},{7,31},{8,0},{9,1... | collective-permute-start | bytes 565256 | tf_op jit(solution)/shard_map/ppermute | solution.py:247
  80.3 14.7 %collective-permute-start.17 = (bf16[2,16,2944]{2,1,0:T(8,128)(2,1)S(1)}, bf16[2,16,2944]{2,1,0:T(8,128)(2,1)S(1)}, u32[]{:S(2)}, u32[]{:S(2)}) collective-permute-start(bf16[2,16,2944]{2,1,0:T(8,128)(2,1)S(1)} %get-tuple-element.23), channel_id=1, source_target_pairs={{0,16},{1,17},{2,18},{3,19},{4,20},{5,21},{6,22},{7,23},{8,24},{9,... | collective-permute-start | bytes 565256 | tf_op jit(solution)/shard_map/ppermute | solution.py:247
  81.3 13.7 %collective-permute-start.18 = (bf16[2,16,2944]{2,1,0:T(8,128)(2,1)S(1)}, bf16[2,16,2944]{2,1,0:T(8,128)(2,1)S(1)}, u32[]{:S(2)}, u32[]{:S(2)}) collective-permute-start(bf16[2,16,2944]{2,1,0:T(8,128)(2,1)S(1)} %get-tuple-element.24), channel_id=1, source_target_pairs={{0,8},{1,9},{2,10},{3,11},{4,12},{5,13},{6,14},{7,15},{8,16},{9,17... | collective-permute-start | bytes 565256 | tf_op jit(solution)/shard_map/ppermute | solution.py:247
  81.3 26.9 %collective-permute-start.13 = (bf16[320,512]{1,0:T(8,128)(2,1)S(1)}, bf16[320,512]{1,0:T(8,128)(2,1)S(1)}, u32[]{:S(2)}, u32[]{:S(2)}) collective-permute-start(bf16[320,512]{1,0:T(8,128)(2,1)S(1)} %get-tuple-element.45), channel_id=1, source_target_pairs={{0,2},{1,3},{2,0},{3,1},{4,6},{5,7},{6,4},{7,5},{8,10},{9,11},{10,... | collective-permute-start | bytes 983048 | tf_op jit(solution)/shard_map/ppermute | solution.py:247
  81.3 25.2 %collective-permute-start.21 = (bf16[2,128,2944]{2,1,0:T(8,128)(2,1)}, bf16[2,128,2944]{2,1,0:T(8,128)(2,1)S(1)}, u32[]{:S(2)}, u32[]{:S(2)}) collective-permute-start(bf16[2,128,2944]{2,1,0:T(8,128)(2,1)} %get-tuple-element.26), channel_id=1, source_target_pairs={{0,4},{1,5},{2,3},{3,2},{4,0},{5,1},{6,7},{7,6},{8,12},{9,13},{10,... | collective-permute-start | bytes 4521992 | tf_op jit(solution)/shard_map/ppermute | solution.py:247
  95.1 10.7 %collective-permute-start.19 = (bf16[2,8,2944]{2,1,0:T(8,128)(2,1)S(1)}, bf16[2,8,2944]{2,1,0:T(8,128)(2,1)S(1)}, u32[]{:S(2)}, u32[]{:S(2)}) collective-permute-start(bf16[2,8,2944]{2,1,0:T(8,128)(2,1)S(1)} %fusion.15), channel_id=1, source_target_pairs={{0,4},{1,5},{2,3},{3,2},{4,0},{5,1},{6,7},{7,6},{8,12},{9,13},{10,... | collective-permute-start | bytes 282632 | tf_op jit(solution)/shard_map/ppermute | solution.py:247
  96.7 9.8 %copy-start.3 = (bf16[2,128,2944]{2,1,0:T(8,128)(2,1)S(1)}, bf16[2,128,2944]{2,1,0:T(8,128)(2,1)}, u32[]{:S(2)}) copy-start(bf16[2,128,2944]{2,1,0:T(8,128)(2,1)} %get-tuple-element.25) | copy-start | bytes 4521988
  105.7 2.5 %copy-start.7 = (pred[320,640]{1,0:T(32,128)(4,1)S(1)}, pred[320,640]{1,0:T(32,128)(4,1)}, u32[]{:S(2)}) copy-start(pred[320,640]{1,0:T(32,128)(4,1)} %copy-done.6) | copy-start | bytes 614404
  105.7 2.5 %copy-start.9 = (pred[320,640]{1,0:T(32,128)(4,1)S(1)}, pred[320,640]{1,0:T(32,128)(4,1)}, u32[]{:S(2)}) copy-start(pred[320,640]{1,0:T(32,128)(4,1)} %copy-done.8) | copy-start | bytes 614404
  105.7 16.6 %collective-permute-start.15 = (f32[512,640]{1,0:T(8,128)S(1)}, f32[512,640]{1,0:T(8,128)S(1)}, u32[]{:S(2)}, u32[]{:S(2)}) collective-permute-start(f32[512,640]{1,0:T(8,128)S(1)} %get-tuple-element.20), channel_id=1, source_target_pairs={{0,2},{1,3},{2,0},{3,1},{4,6},{5,7},{6,4},{7,5},{8,10},{9,11},{10,... | collective-permute-start | bytes 3932168 | tf_op jit(solution)/shard_map/ppermute | solution.py:247
  105.9 4.1 %collective-permute-start.20 = (bf16[8,2944]{1,0:T(8,128)(2,1)S(1)}, bf16[8,2944]{1,0:T(8,128)(2,1)S(1)}, u32[]{:S(2)}, u32[]{:S(2)}) collective-permute-start(bf16[8,2944]{1,0:T(8,128)(2,1)S(1)} %fusion.17), channel_id=1, source_target_pairs={{0,1},{1,0},{2,6},{3,7},{4,5},{5,4},{6,2},{7,3},{8,9},{9,8},{10,14... | collective-permute-start | bytes 141320 | tf_op jit(solution)/shard_map/ppermute | solution.py:247
  106.6 11.7 %collective-permute-start.22 = (bf16[128,2944]{1,0:T(8,128)(2,1)S(1)}, bf16[128,2944]{1,0:T(8,128)(2,1)S(1)}, u32[]{:S(2)}, u32[]{:S(2)}) collective-permute-start(bf16[128,2944]{1,0:T(8,128)(2,1)S(1)} %fusion.5), channel_id=1, source_target_pairs={{0,1},{1,0},{2,6},{3,7},{4,5},{5,4},{6,2},{7,3},{8,9},{9,8},{10,14... | collective-permute-start | bytes 2261000 | tf_op jit(solution)/shard_map/ppermute | solution.py:247
  118.7 10.0 %collective-permute-start.23 = (bf16[32,2944]{1,0:T(8,128)(2,1)S(1)}, bf16[32,2944]{1,0:T(8,128)(2,1)S(1)}, u32[]{:S(2)}, u32[]{:S(2)}) collective-permute-start(bf16[32,2944]{1,0:T(8,128)(2,1)S(1)} %get-tuple-element.39), channel_id=1, source_target_pairs={{0,24},{1,25},{2,26},{3,27},{4,28},{5,29},{6,30},{7,31},{8,0},{9,1... | collective-permute-start | bytes 565256 | tf_op jit(solution)/shard_map/ppermute | solution.py:247
  119.0 12.6 %collective-permute-start.25 = (bf16[32,2944]{1,0:T(8,128)(2,1)S(1)}, bf16[32,2944]{1,0:T(8,128)(2,1)S(1)}, u32[]{:S(2)}, u32[]{:S(2)}) collective-permute-start(bf16[32,2944]{1,0:T(8,128)(2,1)S(1)} %get-tuple-element.40), channel_id=1, source_target_pairs={{0,8},{1,9},{2,10},{3,11},{4,12},{5,13},{6,14},{7,15},{8,16},{9,17... | collective-permute-start | bytes 565256 | tf_op jit(solution)/shard_map/ppermute | solution.py:247
  120.8 15.9 %collective-permute-start.24 = (bf16[32,2944]{1,0:T(8,128)(2,1)S(1)}, bf16[32,2944]{1,0:T(8,128)(2,1)S(1)}, u32[]{:S(2)}, u32[]{:S(2)}) collective-permute-start(bf16[32,2944]{1,0:T(8,128)(2,1)S(1)} %get-tuple-element.41), channel_id=1, source_target_pairs={{0,16},{1,17},{2,18},{3,19},{4,20},{5,21},{6,22},{7,23},{8,24},{9,... | collective-permute-start | bytes 565256 | tf_op jit(solution)/shard_map/ppermute | solution.py:247
  136.8 1.1 copy-start.2
  136.8 1.2 copy-start.4
  136.8 1.4 copy-start.5

commit v3 on v2

--- a/solution.py
+++ b/solution.py
@@ -12,16 +12,16 @@
 F32 = jnp.float32
 NT = (((1,), (1,)), ((), ()))
 NN = (((1,), (0,)), ((), ()))
-VMEM_LIMIT = 48 << 20
+VMEM_LIMIT = 28 << 20
 TAPS = 9
-ROUTES = (8, 32)
+CHUNKS = (24, 16)
 
 
 def mm(a, b, dims):
     return lax.dot_general(a, b, dims, preferred_element_type=F32)
 
 
-def conv_student(kernel_ref, x_ref, t_ref, s_ref, e_ref, width):
+def conv_student(kernel_ref, x_ref, t_ref, s_ref, e_ref, width, by_cell=None):
     wide = x_ref.shape[2]
     cells = x_ref.shape[1] - 2 * width
     for l in range(x_ref.shape[0]):
@@ -36,7 +36,10 @@
             total = term if total is None else total + term
         student = total.astype(BF)
         s_ref[:, at] = student
-        e_ref[:, at] = (student.astype(F32) - t_ref[:, at].astype(F32)).astype(BF)
+        error = student.astype(F32) - t_ref[:, at].astype(F32)
+        e_ref[:, at] = error.astype(BF)
+        if by_cell is not None:
+            by_cell[at, :] = error.T.astype(BF)
 
 
 def tap_grad(x_ref, e_ref, tap, width):
@@ -64,20 +67,18 @@
 
 
 def routed_kernel(
-    width, place_ref, a0, a1, a2, a3, own_ref, near_ref, far_ref, x_ref, t_ref, k_ref, s_ref, e_ref, *outs
+    width, place_ref, own_ref, near_ref, far_ref, x_ref, t_ref, k_ref, s_ref, e_ref, keep_ref, send_ref, mid_ref, flat_ref
 ):
-    g_refs, (keep_ref, send_ref, mid_ref) = outs[:4], outs[4:]
-    a_refs = (a0, a1, a2, a3)
     first, on_core0 = place_ref[0] == 0, place_ref[1] == 0
     rows = k_ref.shape[0]
+    near_y, far_y = slice(0, rows // 2), slice(rows // 2, rows)
     low = lax.broadcasted_iota(jnp.int32, (rows, 128), 1) < 64
     spare = TAPS * 256
 
     def load(at):
         near, far = near_ref[:, at], far_ref[0, :, at]
-        own = [r[0, :, at] for r in a_refs] + [own_ref[:, at], jnp.where(on_core0, far, near)]
-        other = [r[1, :, at] for r in a_refs] + [jnp.where(on_core0, near, far), far_ref[1, :, at]]
-        own, other = jnp.concatenate(own), jnp.concatenate(other)
+        own = jnp.concatenate([own_ref[:, at], jnp.where(on_core0, far, near)])
+        other = jnp.concatenate([jnp.where(on_core0, near, far), far_ref[1, :, at]])
         return jnp.where(first, own, other), jnp.where(first, other, own)
 
     for tap in range(TAPS):
@@ -94,22 +95,19 @@
             k_ref[:, (2 * pair + 1) * 640 + 256 : (2 * pair + 1) * 640 + 384] = jnp.where(
                 low, pltpu.roll(left, 64, 1), right
             ).astype(BF)
-    conv_student(k_ref, x_ref, t_ref, s_ref, e_ref, width)
+    conv_student(k_ref, x_ref, t_ref, s_ref, flat_ref, width, e_ref)
 
     def put(at, left, right):
         left, right = left.astype(BF), right.astype(BF)
         own, other = jnp.where(first, left, right), jnp.where(first, right, left)
-        for s in range(4):
-            g_refs[s][0, :, at] = own[s * 16 : (s + 1) * 16]
-            g_refs[s][1, :, at] = other[s * 16 : (s + 1) * 16]
-        own_far, other_near = own[192:], other[64:192]
-        keep_ref[0, :, at] = own[64:192]
-        send_ref[1, :, at] = other[192:]
+        own_far, other_near = own[far_y], other[near_y]
+        keep_ref[0, :, at] = own[near_y]
+        send_ref[1, :, at] = other[far_y]
         send_ref[0, :, at] = jnp.where(on_core0, own_far, other_near)
         keep_ref[1, :, at] = jnp.where(on_core0, other_near, own_far)
 
     for tap in range(TAPS):
-        grad = tap_grad(x_ref, e_ref, tap, width)
+        grad = tap_grad(x_ref, flat_ref, tap, width)
         put(slice(tap * 256, (tap + 1) * 256), grad[:, :256], grad[:, 384:])
         mid_ref[tap] = grad[:, 256:384]
     for pair in range(5):
@@ -122,24 +120,82 @@
         )
 
 
-def back_kernel(width, kernel_ref, e_ref, *out_refs):
-    channels = kernel_ref.shape[1] // TAPS
-    cells = e_ref.shape[2] - 2 * width
-    for l in range(e_ref.shape[1]):
-        total = None
-        for tap in range(TAPS):
-            a, c = divmod(tap, 3)
+def twice(half_tile):
+    return jnp.concatenate([half_tile, half_tile], axis=1)
+
+
+def pack_kernel(place_ref, w_ref, out_ref):
+    first = place_ref[0] == 0
+    low = lax.broadcasted_iota(jnp.int32, (w_ref.shape[1], 128), 1) < 64
+    swap = lambda v: pltpu.roll(v, 64, 1)
+    spare = []
+    for tap in range(TAPS):
+        t0, t1 = w_ref[tap, :, :128], w_ref[tap, :, 128:256]
+        t2 = twice(w_ref[tap, :, 256:])
+        r1 = swap(t1)
+        out_ref[:, tap * 256 : tap * 256 + 128] = jnp.where(
+            first, t0, jnp.where(low, swap(t0), r1)
+        ).astype(BF)
+        out_ref[:, tap * 256 + 128 : (tap + 1) * 256] = jnp.where(
+            first, t1, jnp.where(low, r1, t2)
+        ).astype(BF)
+        spare.append(jnp.where(first, t2, jnp.where(low, t0, swap(t0))))
+    spare.append(jnp.zeros_like(spare[0]))
+    for pair in range(5):
+        at = TAPS * 256 + pair * 128
+        out_ref[:, at : at + 128] = jnp.where(low, spare[2 * pair], spare[2 * pair + 1]).astype(BF)
+
+
+def adam_kernel(scale, place_ref, w_ref, m1_ref, m2_ref, *refs):
+    parts, outs = refs[:-3], refs[-3:]
+    first = place_ref[0] == 0
+    low = lax.broadcasted_iota(jnp.int32, (w_ref.shape[1], 128), 1) < 64
+    swap = lambda v: pltpu.roll(v, 64, 1)
+
+    def grad(at):
+        sums = []
+        for i in range(0, len(parts), 4):
+            p0, p1, p2, p3 = [ref[:, at].astype(F32) for ref in parts[i : i + 4]]
+            sums.append((p0 + p1) + (p2 + p3))
+        return jnp.concatenate(sums) * scale
+
+    for tap in range(TAPS):
+        if tap % 2 == 0:
+            spare = grad(slice(TAPS * 256 + tap * 64, TAPS * 256 + tap * 64 + 128))
+            spare_swap = swap(spare)
+        at_low = spare if tap % 2 == 0 else spare_swap
+        left = grad(slice(tap * 256, tap * 256 + 128))
+        right = grad(slice(tap * 256 + 128, (tap + 1) * 256))
+        left_swap, right_swap = swap(left), swap(right)
+        tiles = (
+            jnp.where(first, left, jnp.where(low, at_low, left_swap)),
+            jnp.where(first, right, jnp.where(low, left_swap, right_swap)),
+            jnp.where(first, at_low, right_swap)[:, :64],
+        )
+        for tile, at in zip(tiles, (slice(0, 128), slice(128, 256), slice(256, 320))):
+            new = adam(w_ref[tap, :, at], m1_ref[tap, :, at], m2_ref[tap, :, at], tile)
+            for out_ref, value in zip(outs, new):
+                out_ref[tap, :, at] = value
+
+
+def back_kernel(width, parts, *refs):
+    kernel_refs, e_refs, out_ref = refs[:parts], refs[parts : 2 * parts], refs[-1]
+    channels = kernel_refs[0].shape[1] // TAPS
+    cells = e_refs[0].shape[1] - 2 * width
+    total = None
+    for tap in range(TAPS):
+        a, c = divmod(tap, 3)
+        for kernel_ref, e_ref in zip(kernel_refs, e_refs):
             term = mm(
-                e_ref[c, l, (2 - a) * width : (2 - a) * width + cells, :],
+                e_ref[c, (2 - a) * width : (2 - a) * width + cells, :],
                 kernel_ref[:, tap * channels : (tap + 1) * channels],
                 NN,
             )
             total = term if total is None else total + term
-        out_refs[l][...] = total
-
-
-def vmem_call(kernel, outs, scalars, *args, scratch=()):
-    flops = 2 * 1024 * 320 * 5760
+    out_ref[...] = total
+
+
+def vmem_call(kernel, outs, scalars, *args, scratch=(), flops=0):
     return pl.pallas_call(
         kernel,
         out_shape=outs,
@@ -147,7 +203,7 @@
         + [pl.BlockSpec(memory_space=pltpu.VMEM)] * (len(args) - scalars),
         out_specs=jax.tree.map(lambda _: pl.BlockSpec(memory_space=pltpu.VMEM), outs),
         scratch_shapes=scratch,
-        cost_estimate=pl.CostEstimate(flops=flops, bytes_accessed=8 << 20, transcendentals=0),
+        cost_estimate=pl.CostEstimate(flops=flops, bytes_accessed=1 << 20, transcendentals=0),
         compiler_params=pltpu.CompilerParams(vmem_limit_bytes=VMEM_LIMIT),
     )(*args)
 
@@ -220,13 +276,17 @@
         t,
     )
     error = error.T.reshape(b, band, width, total_out)
-    back = vmem_call(
-        functools.partial(back_kernel, width),
-        (shape(band * width, channels, dtype=F32),) * b,
-        0,
-        kernel,
-        back_cells(with_halo(error)),
-    )
+    shifted = back_cells(with_halo(error))
+    back = [
+        vmem_call(
+            functools.partial(back_kernel, width, 1),
+            shape(band * width, channels, dtype=F32),
+            0,
+            kernel,
+            shifted[:, l],
+        )
+        for l in range(b)
+    ]
     grad = grad.astype(F32).reshape(total_out, TAPS, row_count, part).transpose(2, 0, 1, 3)
     grad = lax.psum_scatter(grad, "rows", scatter_dimension=0, tiled=True)[0]
     grad = lax.psum_scatter(grad, "dp", scatter_dimension=0, tiled=True)
@@ -245,6 +305,10 @@
         z, y, core, x = pairs_of(z, y, core, x)
         pairs.append((i, ((z % 4 * 2 + y) * 2 + core) * 2 + x))
     return lambda v: lax.ppermute(v, ("dp", "rows"), pairs)
+
+
+def phase(*values):
+    return lax.optimization_barrier(values)
 
 
 def routed_device(latents, target, weight, moment1, moment2):
@@ -257,64 +321,27 @@
     along_xy = hop(lambda z, y, core, x: (z, y ^ core, core, x ^ 1 ^ core))
     along_yx = hop(lambda z, y, core, x: (z, y ^ 1 ^ core, core, x ^ core))
     along_z = lambda v, s: hop(lambda z, y, core, x: (z + s, y, core, x))(v)
-    ra, rb = ROUTES
     lanes = TAPS * 256 + 640
 
-    piece = weight.transpose(2, 0, 1)
-    piece = jnp.where(half == 0, piece, jnp.roll(piece, -64, axis=2)).astype(BF)
-    piece = jnp.concatenate(
-        [
-            piece[:, :, :256].reshape(-1, TAPS * 256),
-            piece[:, :, 256:].reshape(-1, TAPS * 64),
-            jnp.zeros((piece.shape[0], 64), BF),
-        ],
-        axis=1,
-    )
-
-    def turned(v):
-        return jnp.where(core == 0, v.swapaxes(0, 1), v)
-
-    pa, pb = piece[:ra], piece[ra:]
-    own = jnp.concatenate([pb] + [along_z(pb, s) for s in (1, 2, 3)])
-    pa = jnp.stack([pa, along_xy(pa)])
-    pa = turned(jnp.stack([pa, along_yx(pa)])).reshape(2, 2 * ra, lanes)
-    near = along_xy(own)
-    az = [pa] + [along_z(pa, s) for s in (1, 2, 3)]
-    far = along_yx(jnp.stack([own, near]))
-
-    at_a = np.indices((4, 2, ra)).reshape(3, -1)
-    at_b = np.indices((2, 4, rb)).reshape(3, -1)
-    dist_z = np.concatenate([at_a[0], at_b[1]]).astype(np.int32)
-    dist_y = np.concatenate([at_a[1], at_b[0]]).astype(np.int32)
-    within = np.concatenate([at_a[2], ra + at_b[2]]).astype(np.int32)
+    place = jnp.stack([half, core]).astype(jnp.int32)
+    by_tap = lambda v: v.transpose(0, 2, 1)
+    per = weight.shape[2]
+    piece = vmem_call(pack_kernel, shape(per, lanes), 1, place, by_tap(weight))
+    piece, latents, target = phase(piece, latents, target)
+
+    chunk_a, chunk_b = CHUNKS
+    grids = [
+        np.indices((2, 4, chunk_a)).reshape(3, -1),
+        np.indices((2, 4, chunk_b)).reshape(3, -1) + [[0], [0], [chunk_a]],
+    ]
+    dist_y, dist_z, within = np.concatenate(grids, axis=1).astype(np.int32)
     block = ((z - dist_z) % 4) * 4 + (y ^ dist_y) * 2
-    per = weight.shape[2]
     everything = jnp.arange(channels, dtype=jnp.int32)
     pick_own = ((block + core) * per + within)[:, None] == everything[None, :]
     pick_other = ((block + 1 - core) * per + within)[:, None] == everything[None, :]
     pick = jnp.concatenate([pick_own, pick_other]).astype(BF)
     rows = within.shape[0]
-
-    banded = with_halo(latents)
-    x = wide_cells(jnp.concatenate([banded, along_core(banded)]))
-    t = mm(pick, target.reshape(cells, channels), NT).astype(BF)
-    t = jnp.concatenate([t[:rows], along_core(t[rows:])], axis=1)
-
-    kernel, student, error, g0, g1, g2, g3, keep, send = vmem_call(
-        functools.partial(routed_kernel, width),
-        (shape(rows, TAPS * channels), shape(rows, 2 * cells), shape(rows, 2 * cells))
-        + (shape(2, 2 * ra, lanes),) * 4
-        + (shape(2, 4 * rb, lanes),) * 2,
-        1,
-        jnp.stack([half, core]).astype(jnp.int32),
-        *az,
-        own,
-        near,
-        far,
-        x,
-        t,
-        scratch=[pltpu.VMEM((TAPS, rows, 128), F32)],
-    )
+    rows_a = 8 * chunk_a
 
     def plus(*terms):
         total = terms[0].astype(F32)
@@ -322,38 +349,88 @@
             total = total + term.astype(F32)
         return total
 
-    got = along_yx(send)
-    az = [along_z(v, -s) for s, v in ((1, g1), (2, g2), (3, g3))]
-    got2 = along_xy(plus(keep[1], got[1]).astype(BF))
-    gb = plus(keep[0], got[0], got2).astype(BF).reshape(4, rb, lanes)
-    bz = [along_z(gb[s], -s) for s in (1, 2, 3)]
-    ga = turned(plus(g0, *az).reshape(2, 2, ra, lanes))
-    ga_in = along_yx(ga[1].astype(BF))
-    ga = plus(ga[0], ga_in)
-    ga = plus(ga[0], along_xy(ga[1].astype(BF)))
-    grad = jnp.concatenate([ga, plus(gb[0], *bz)], axis=0) / F32(b * lax.axis_size("dp"))
-    grad = jnp.concatenate(
-        [
-            grad[:, : TAPS * 256].reshape(-1, TAPS, 256),
-            grad[:, TAPS * 256 : TAPS * 320].reshape(-1, TAPS, 64),
-        ],
-        axis=2,
-    )
-    grad = jnp.where(half == 0, grad, jnp.roll(grad, 64, axis=2)).transpose(1, 2, 0)
-
+    bz = [along_z(piece, s) for s in (1, 2, 3)]
+    banded = with_halo(latents)
+    t = mm(pick, target.reshape(cells, channels), NT).astype(BF)
+    bz, banded, t = phase(bz, banded, t)
+    t = jnp.concatenate([t[:rows], along_core(t[rows:])], axis=1)
+    own_a = jnp.concatenate([v[:chunk_a] for v in [piece] + bz])
+    own_b = jnp.concatenate([v[chunk_a:] for v in [piece] + bz])
+    near_a, near_b = along_xy(own_a), along_xy(own_b)
+    x = wide_cells(jnp.concatenate([banded, along_core(banded)]))
+    far_a = along_yx(jnp.stack([own_a, near_a]))
+    far_b = along_yx(jnp.stack([own_b, near_b]))
+
+    def compute(own, near, far, t):
+        n = t.shape[0]
+        return vmem_call(
+            functools.partial(routed_kernel, width),
+            (shape(n, TAPS * channels), shape(n, 2 * cells), shape(2 * cells, n))
+            + (shape(2, n // 2, lanes),) * 2,
+            1,
+            place,
+            own,
+            near,
+            far,
+            x,
+            t,
+            scratch=[pltpu.VMEM((TAPS, n, 128), F32), pltpu.VMEM((n, 2 * cells), BF)],
+            flops=30 * 10**9,
+        )
+
+    far_a, near_b, x, t = phase(far_a, near_b, x, t)
+    kernel_a, student_a, error_a, keep_a, send_a = compute(own_a, near_a, far_a, t[:rows_a])
+    got_a = along_yx(send_a)
+    kernel_b, student_b, error_b, keep_b, send_b = compute(own_b, near_b, far_b, t[rows_a:])
+    got_b = along_yx(send_b)
+    got_a, send_b, error_b = phase(got_a, send_b, error_b)
+
+    got2_a = along_xy(plus(keep_a[1], got_a[1]).astype(BF))
+    error = jnp.concatenate([error_a, error_b], axis=1)
+    shifted = back_cells(with_halo(error.reshape(2, band, width, rows)))
+
+    def back(l):
+        return vmem_call(
+            functools.partial(back_kernel, width, 2),
+            shape(cells, channels, dtype=F32),
+            0,
+            kernel_a,
+            kernel_b,
+            shifted[:, l, :, :rows_a],
+            shifted[:, l, :, rows_a:],
+            flops=20 * 10**9,
+        )
+
+    back_other = back(1)
+    got2_a, got_b, back_other, shifted = phase(got2_a, got_b, back_other, shifted)
+    back_in = along_core(back_other)
+    gb_a = plus(keep_a[0], got_a[0], got2_a).astype(BF).reshape(4, chunk_a, lanes)
+    bz_a = [along_z(gb_a[s], -s) for s in (1, 2, 3)]
+    got2_b = along_xy(plus(keep_b[1], got_b[1]).astype(BF))
+    got2_b, shifted, student_a, student_b = phase(got2_b, shifted, student_a, student_b)
+    gb_b = plus(keep_b[0], got_b[0], got2_b).astype(BF).reshape(4, chunk_b, lanes)
+    bz_b = [along_z(gb_b[s], -s) for s in (1, 2, 3)]
+    back_own = back(0)
+
+    student = jnp.concatenate([student_a, student_b])
     both = jnp.concatenate([student[:, :cells], along_core(student[:, cells:])])
     out = mm(both, pick, (((0,), (0,)), ((), ()))).astype(BF).reshape(latents.shape)
-
-    error = error.T.reshape(2, band, width, rows)
-    back_own, back_other = vmem_call(
-        functools.partial(back_kernel, width),
-        (shape(cells, channels, dtype=F32),) * 2,
-        0,
-        kernel,
-        back_cells(with_halo(error)),
+    input_grad = (back_own + back_in).astype(BF).reshape(latents.shape)
+    bz_a, bz_b, out, input_grad = phase(bz_a, bz_b, out, input_grad)
+    news = vmem_call(
+        functools.partial(adam_kernel, 1.0 / (b * lax.axis_size("dp"))),
+        (shape(TAPS, per, weight.shape[1], dtype=F32),) * 3,
+        1,
+        place,
+        by_tap(weight),
+        by_tap(moment1),
+        by_tap(moment2),
+        gb_a[0],
+        *bz_a,
+        gb_b[0],
+        *bz_b,
     )
-    input_grad = (back_own + along_core(back_other)).astype(BF).reshape(latents.shape)
-    return (out, input_grad, *adam(weight, moment1, moment2, grad))
+    return (out, input_grad, *map(by_tap, news))
 
 
 def solution(mesh):

time: 140 us -> 121 us (0.86)
  waiting for transfers between devices: 62 us -> 46.4 us
  starting transfers between devices: 31.4 us -> 36.2 us
  local copies, waits for them, and re-layouts: 8.74 us -> 4.07 us
  other arithmetic: 10.5 us -> 5.98 us
    ppermute x24 -> x21, waiting for transfers between devices: 62 us -> 43.3 us  [hop(): return lambda v: lax.ppermute(v, ('dp', 'rows'), pairs)]
    ppermute x24 -> x21, starting transfers between devices: 28.3 us -> 33.1 us  [hop(): return lambda v: lax.ppermute(v, ('dp', 'rows'), pairs)]
    ppermute x2, waiting for transfers between devices: 0.01 us -> 3.14 us  [with_halo(): got = lax.ppermute(edge, 'rows', [(0, 1), (1, 0)])]
    slice x8 -> x12, local copies, waits for them, and re-layouts: 2.31 us -> 0.19 us  [the longest x4 0.05 us: routed_device(): own_a = jnp.concatenate([v[:chunk_a] for v in [piece] + bz])]
    concatenate x1, other arithmetic: 2.93 us -> 0.87 us  [wide_cells(): jnp.concatenate([column_shift(cells, k - 1) for k in range(3)], axis=3)]
    unnamed x29 -> x14, local copies, waits for them, and re-layouts: 3.08 us -> 1.22 us
    sub x1 -> x0, other arithmetic: 1.64 us -> none  [adam(): new_weight = weight - 0.01 * new_moment1 / (jnp.sqrt(new_moment2) + 1e-08)]
    pallas_call x2 -> x6, Pallas kernels: 23.7 us -> 24.2 us  [vmem_call(): pl.pallas_call(kernel, out_shape=outs, in_specs=[pl.BlockSpec(memory_spac...]
  transfers between devices with their start and end apart: 26 -> 23, of which waited for: 12 -> 11; matrix products, arithmetic and copies ran while one was open for 9% -> 9% of each run, Pallas kernels for 6% -> 18%
where the time goes in v3:
time: 121 us; the launch traced here: 120 us
  waiting for transfers between devices  46.4 us (38%)
  starting transfers between devices  36.2 us (30%)
  Pallas kernels  24.2 us (20%)
  other arithmetic  5.98 us (5%)
  local copies, waits for them, and re-layouts  4.07 us (3%)
  matrix products  2.35 us (2%)
    ppermute x21, waiting for transfers between devices, hop(): return lambda v: lax.ppermute(v, ('dp', 'rows'), pairs)  43.3 us
    ppermute x21, starting transfers between devices, hop(): return lambda v: lax.ppermute(v, ('dp', 'rows'), pairs)  33.1 us
    pallas_call x6, Pallas kernels, vmem_call(): pl.pallas_call(kernel, out_shape=outs, in_specs=[pl.BlockSpec(memory_spac...  24.2 us
    ppermute x2, waiting for transfers between devices, with_halo(): got = lax.ppermute(edge, 'rows', [(0, 1), (1, 0)])  3.14 us
    ppermute x2, starting transfers between devices, with_halo(): got = lax.ppermute(edge, 'rows', [(0, 1), (1, 0)])  3.1 us
  transfers between devices with their start and end apart: 23, of which 11 were waited for; matrix products, arithmetic and copies ran while one was open for 9% of the time, Pallas kernels for 18%

profile of v3, /device:TPU:0, one launch (start us, length us, event | category | flops | bytes accessed | tf_op | source)
XLA Modules:
  0.0 120.3 jit_solution(16583296582941217670)
XLA Ops:
  0.7 1.1 copy-done.1
  1.8 0.7 shard_map.119
  2.5 3.1 %collective-permute-start = (bf16[40,2944]{1,0:T(8,128)(2,1)S(1)}, bf16[40,2944]{1,0:T(8,128)(2,1)S(1)}, u32[]{:S(2)}, u32[]{:S(2)}) collective-permute-start(bf16[40,2944]{1,0:T(8,128)(2,1)S(1)} %shard_map.119), channel_id=1, source_target_pairs={{0,8},{1,9},{2,10},{3,11},{4,12},{5,13},{6,14},{7,15},{8,16},{9,17... | collective-permute-start | bytes 706568 | tf_op jit(solution)/shard_map/ppermute | solution.py:307
  5.6 2.6 %collective-permute-start.1 = (bf16[40,2944]{1,0:T(8,128)(2,1)S(1)}, bf16[40,2944]{1,0:T(8,128)(2,1)S(1)}, u32[]{:S(2)}, u32[]{:S(2)}) collective-permute-start(bf16[40,2944]{1,0:T(8,128)(2,1)S(1)} %shard_map.119), channel_id=1, source_target_pairs={{0,16},{1,17},{2,18},{3,19},{4,20},{5,21},{6,22},{7,23},{8,24},{9,... | collective-permute-start | bytes 706568 | tf_op jit(solution)/shard_map/ppermute | solution.py:307
  8.2 1.3 %collective-permute-start.2 = (bf16[40,2944]{1,0:T(8,128)(2,1)S(1)}, bf16[40,2944]{1,0:T(8,128)(2,1)S(1)}, u32[]{:S(2)}, u32[]{:S(2)}) collective-permute-start(bf16[40,2944]{1,0:T(8,128)(2,1)S(1)} %shard_map.119), channel_id=1, source_target_pairs={{0,24},{1,25},{2,26},{3,27},{4,28},{5,29},{6,30},{7,31},{8,0},{9,1... | collective-permute-start | bytes 706568 | tf_op jit(solution)/shard_map/ppermute | solution.py:307
  9.6 0.8 slice_select_fusion.1
  10.4 1.5 %collective-permute-start.3 = (bf16[1,1,32,640]{3,2,1,0:T(8,128)(2,1)S(1)}, bf16[1,1,32,640]{3,2,1,0:T(8,128)(2,1)S(1)}, u32[]{:S(2)}, u32[]{:S(2)}) collective-permute-start(bf16[1,1,32,640]{3,2,1,0:T(8,128)(2,1)S(1)} %slice_select_fusion.1), channel_id=1, source_target_pairs={{0,1},{1,0},{2,3},{3,2},{4,5},{5,4},{6,7},{7,6},{8,9},{9,8},{10,11... | collective-permute-start | bytes 122888 | tf_op jit(solution)/shard_map/ppermute | solution.py:236
  11.9 0.7 multiply_add_fusion.1
  13.0 0.7 convolution_convert_fusion.1
  13.7 0.7 collective-permute-done.3
  14.6 9.0 %collective-permute-done.1 = bf16[40,2944]{1,0:T(8,128)(2,1)S(1)} collective-permute-done((bf16[40,2944]{1,0:T(8,128)(2,1)S(1)}, bf16[40,2944]{1,0:T(8,128)(2,1)S(1)}, u32[]{:S(2)}, u32[]{:S(2)}) %collective-permute-start.1) | collective-permute-done | bytes 235552 | tf_op jit(solution)/shard_map/ppermute | solution.py:307
  23.8 1.6 %collective-permute-start.4 = (bf16[96,2944]{1,0:T(8,128)(2,1)S(1)}, bf16[96,2944]{1,0:T(8,128)(2,1)S(1)}, u32[]{:S(2)}, u32[]{:S(2)}) collective-permute-start(bf16[96,2944]{1,0:T(8,128)(2,1)S(1)} %get-tuple-element.104.own_ref), channel_id=1, source_target_pairs={{0,1},{1,0},{2,6},{3,7},{4,5},{5,4},{6,2},{7,3},{8,9},{9,8},{10,14... | collective-permute-start | bytes 1695752 | tf_op jit(solution)/shard_map/ppermute | solution.py:307
  25.5 1.2 %collective-permute-start.6 = (bf16[64,2944]{1,0:T(8,128)(2,1)S(1)}, bf16[64,2944]{1,0:T(8,128)(2,1)S(1)}, u32[]{:S(2)}, u32[]{:S(2)}) collective-permute-start(bf16[64,2944]{1,0:T(8,128)(2,1)S(1)} %get-tuple-element.110.own_ref), channel_id=1, source_target_pairs={{0,1},{1,0},{2,6},{3,7},{4,5},{5,4},{6,2},{7,3},{8,9},{9,8},{10,14... | collective-permute-start | bytes 1130504 | tf_op jit(solution)/shard_map/ppermute | solution.py:307
  26.8 0.6 collective-permute-start.7
  27.5 6.0 %collective-permute-done.4.near_ref = bf16[96,2944]{1,0:T(8,128)(2,1)S(1)} collective-permute-done((bf16[96,2944]{1,0:T(8,128)(2,1)S(1)}, bf16[96,2944]{1,0:T(8,128)(2,1)S(1)}, u32[]{:S(2)}, u32[]{:S(2)}) %collective-permute-start.4) | collective-permute-done | bytes 565280 | tf_op jit(solution)/shard_map/ppermute | solution.py:307
  33.6 1.6 %collective-permute-start.5 = (bf16[2,96,2944]{2,1,0:T(8,128)(2,1)S(1)}, bf16[2,96,2944]{2,1,0:T(8,128)(2,1)S(1)}, u32[]{:S(2)}, u32[]{:S(2)}) collective-permute-start(bf16[2,96,2944]{2,1,0:T(8,128)(2,1)S(1)} %pad_maximum_fusion.1), channel_id=1, source_target_pairs={{0,4},{1,5},{2,3},{3,2},{4,0},{5,1},{6,7},{7,6},{8,12},{9,13},{10,... | collective-permute-start | bytes 3391496 | tf_op jit(solution)/shard_map/ppermute | solution.py:307
  35.2 4.5 %collective-permute-done.6.near_ref = bf16[64,2944]{1,0:T(8,128)(2,1)S(1)} collective-permute-done((bf16[64,2944]{1,0:T(8,128)(2,1)S(1)}, bf16[64,2944]{1,0:T(8,128)(2,1)S(1)}, u32[]{:S(2)}, u32[]{:S(2)}) %collective-permute-start.6) | collective-permute-done | bytes 376864 | tf_op jit(solution)/shard_map/ppermute | solution.py:307
  39.7 1.6 %collective-permute-start.10 = (bf16[2,64,2944]{2,1,0:T(8,128)(2,1)S(1)}, bf16[2,64,2944]{2,1,0:T(8,128)(2,1)S(1)}, u32[]{:S(2)}, u32[]{:S(2)}) collective-permute-start(bf16[2,64,2944]{2,1,0:T(8,128)(2,1)S(1)} %pad_maximum_fusion.4), channel_id=1, source_target_pairs={{0,4},{1,5},{2,3},{3,2},{4,0},{5,1},{6,7},{7,6},{8,12},{9,13},{10,... | collective-permute-start | bytes 2261000 | tf_op jit(solution)/shard_map/ppermute | solution.py:307
  41.4 0.8 fusion.19
  42.2 0.9 fusion.2
  43.1 6.3 %collective-permute-done.5.far_ref = bf16[2,96,2944]{2,1,0:T(8,128)(2,1)S(1)} collective-permute-done((bf16[2,96,2944]{2,1,0:T(8,128)(2,1)S(1)}, bf16[2,96,2944]{2,1,0:T(8,128)(2,1)S(1)}, u32[]{:S(2)}, u32[]{:S(2)}) %collective-permute-start.5) | collective-permute-done | bytes 1130528 | tf_op jit(solution)/shard_map/ppermute | solution.py:307
  49.4 7.7 %shard_map.120 = (bf16[192,5760]{1,0:T(8,128)(2,1)S(1)}, bf16[192,1024]{1,0:T(8,128)(2,1)S(1)}, bf16[1024,192]{1,0:T(8,128)(2,1)S(1)}, bf16[2,96,2944]{2,1,0:T(8,128)(2,1)S(1)}, bf16[2,96,2944]{2,1,0:T(8,128)(2,1)S(1)}) custom-call(s32[2]{0:T(128)S(1)} %pad_add_fusion.3.place_ref, bf16[96,2944]{1,0:T(8,128)(2,1)S(1)} %get-tuple-element.104.own_ref, ...), custom_call_target="tpu_custom_call" | custom-call | flops 30000001024 | bytes 1048576 | tf_op jit(solution)/shard_map/pallas_call | solution.py:199
  57.1 1.6 %collective-permute-start.9 = (bf16[2,96,2944]{2,1,0:T(8,128)(2,1)S(1)}, bf16[2,96,2944]{2,1,0:T(8,128)(2,1)S(1)}, u32[]{:S(2)}, u32[]{:S(2)}) collective-permute-start(bf16[2,96,2944]{2,1,0:T(8,128)(2,1)S(1)} %get-tuple-element.60), channel_id=1, source_target_pairs={{0,4},{1,5},{2,3},{3,2},{4,0},{5,1},{6,7},{7,6},{8,12},{9,13},{10,... | collective-permute-start | bytes 3391496 | tf_op jit(solution)/shard_map/ppermute | solution.py:307
  58.7 6.6 %shard_map.121 = (bf16[128,5760]{1,0:T(8,128)(2,1)S(1)}, bf16[128,1024]{1,0:T(8,128)(2,1)S(1)}, bf16[1024,128]{1,0:T(8,128)(2,1)S(1)}, bf16[2,64,2944]{2,1,0:T(8,128)(2,1)S(1)}, bf16[2,64,2944]{2,1,0:T(8,128)(2,1)S(1)}) custom-call(s32[2]{0:T(128)S(1)} %pad_add_fusion.3.place_ref, bf16[64,2944]{1,0:T(8,128)(2,1)S(1)} %get-tuple-element.110.own_ref, ...), custom_call_target="tpu_custom_call" | custom-call | flops 30000001024 | bytes 1048576 | tf_op jit(solution)/shard_map/pallas_call | solution.py:199
  65.3 0.6 collective-permute-start.12
  65.8 7.0 %collective-permute-done.9 = bf16[2,96,2944]{2,1,0:T(8,128)(2,1)S(1)} collective-permute-done((bf16[2,96,2944]{2,1,0:T(8,128)(2,1)S(1)}, bf16[2,96,2944]{2,1,0:T(8,128)(2,1)S(1)}, u32[]{:S(2)}, u32[]{:S(2)}) %collective-permute-start.9) | collective-permute-done | bytes 1130528 | tf_op jit(solution)/shard_map/ppermute | solution.py:307
  73.1 1.6 %collective-permute-start.13 = (bf16[2,1,32,320]{3,2,1,0:T(8,128)(2,1)S(1)}, bf16[2,1,32,320]{3,2,1,0:T(8,128)(2,1)S(1)}, u32[]{:S(2)}, u32[]{:S(2)}) collective-permute-start(bf16[2,1,32,320]{3,2,1,0:T(8,128)(2,1)S(1)} %slice_select_fusion), channel_id=1, source_target_pairs={{0,1},{1,0},{2,3},{3,2},{4,5},{5,4},{6,7},{7,6},{8,9},{9,8},{10,11... | collective-permute-start | bytes 122888 | tf_op jit(solution)/shard_map/ppermute | solution.py:236
  74.8 0.6 collective-permute-start.11
  75.4 2.5 %collective-permute-done.13 = bf16[2,1,32,320]{3,2,1,0:T(8,128)(2,1)S(1)} collective-permute-done((bf16[2,1,32,320]{3,2,1,0:T(8,128)(2,1)S(1)}, bf16[2,1,32,320]{3,2,1,0:T(8,128)(2,1)S(1)}, u32[]{:S(2)}, u32[]{:S(2)}) %collective-permute-start.13) | collective-permute-done | bytes 40992 | tf_op jit(solution)/shard_map/ppermute | solution.py:236
  78.1 0.5 fusion.20
  78.6 0.4 concatenate.58
  79.0 0.6 pad_maximum_fusion
  79.7 0.4 slice_bitcast_fusion.2.refs_3_
  80.1 3.5 %shard_map.122 = f32[512,640]{1,0:T(8,128)S(1)} custom-call(bf16[192,5760]{1,0:T(8,128)(2,1)S(1)} %get-tuple-element.65.refs_0_, bf16[128,5760]{1,0:T(8,128)(2,1)S(1)} %get-tuple-element.66.refs_1_, bf16[3,576,192]{2,1,0:T(8,128)(2,1)S(1)} %slice_bitcast_fusion.refs_2_, bf16[3,576,128]{2,1,0:T(8,128)(2,1)S(1)} %slice_bitcast_fusion.2.refs_3_), custom_call_target="tpu_custom_call" | custom-call | flops 20000000000 | bytes 1048576 | tf_op jit(solution)/shard_map/pallas_call | solution.py:199
  83.6 1.4 %collective-permute-done.12 = bf16[2,64,2944]{2,1,0:T(8,128)(2,1)S(1)} collective-permute-done((bf16[2,64,2944]{2,1,0:T(8,128)(2,1)S(1)}, bf16[2,64,2944]{2,1,0:T(8,128)(2,1)S(1)}, u32[]{:S(2)}, u32[]{:S(2)}) %collective-permute-start.12) | collective-permute-done | bytes 753696 | tf_op jit(solution)/shard_map/ppermute | solution.py:307
  85.0 2.4 %collective-permute-done.11 = bf16[96,2944]{1,0:T(8,128)(2,1)S(1)} collective-permute-done((bf16[96,2944]{1,0:T(8,128)(2,1)S(1)}, bf16[96,2944]{1,0:T(8,128)(2,1)S(1)}, u32[]{:S(2)}, u32[]{:S(2)}) %collective-permute-start.11) | collective-permute-done | bytes 565280 | tf_op jit(solution)/shard_map/ppermute | solution.py:307
  87.8 1.6 %collective-permute-start.17 = (bf16[64,2944]{1,0:T(8,128)(2,1)S(1)}, bf16[64,2944]{1,0:T(8,128)(2,1)S(1)}, u32[]{:S(2)}, u32[]{:S(2)}) collective-permute-start(bf16[64,2944]{1,0:T(8,128)(2,1)S(1)} %fusion.10), channel_id=1, source_target_pairs={{0,1},{1,0},{2,6},{3,7},{4,5},{5,4},{6,2},{7,3},{8,9},{9,8},{10,14... | collective-permute-start | bytes 1130504 | tf_op jit(solution)/shard_map/ppermute | solution.py:307
  89.4 6.6 %collective-permute-start.14 = (bf16[24,2944]{1,0:T(8,128)(2,1)S(1)}, bf16[24,2944]{1,0:T(8,128)(2,1)S(1)}, u32[]{:S(2)}, u32[]{:S(2)}) collective-permute-start(bf16[24,2944]{1,0:T(8,128)(2,1)S(1)} %get-tuple-element.102), channel_id=1, source_target_pairs={{0,24},{1,25},{2,26},{3,27},{4,28},{5,29},{6,30},{7,31},{8,0},{9,1... | collective-permute-start | bytes 423944 | tf_op jit(solution)/shard_map/ppermute | solution.py:307
  96.0 0.4 collective-permute-start.15
  96.6 1.9 %collective-permute-start.22 = (f32[512,640]{1,0:T(8,128)S(1)}, f32[512,640]{1,0:T(8,128)S(1)}, u32[]{:S(2)}, u32[]{:S(2)}) collective-permute-start(f32[512,640]{1,0:T(8,128)S(1)} %shard_map.122), channel_id=1, source_target_pairs={{0,2},{1,3},{2,0},{3,1},{4,6},{5,7},{6,4},{7,5},{8,10},{9,11},{10,... | collective-permute-start | bytes 3932168 | tf_op jit(solution)/shard_map/ppermute | solution.py:307
  99.0 3.5 %shard_map.123 = f32[512,640]{1,0:T(8,128)S(1)} custom-call(bf16[192,5760]{1,0:T(8,128)(2,1)S(1)} %get-tuple-element.65.refs_0_, bf16[128,5760]{1,0:T(8,128)(2,1)S(1)} %get-tuple-element.66.refs_1_, bf16[3,576,192]{2,1,0:T(8,128)(2,1)S(1)} %slice_bitcast_fusion.1.refs_2_, bf16[3,576,128]{2,1,0:T(8,128)(2,1)S(1)} %slice_bitcast_fusion.3.refs_3_), custom_call_target="tpu_custom_call" | custom-call | flops 20000000000 | bytes 1048576 | tf_op jit(solution)/shard_map/pallas_call | solution.py:199
  102.7 5.3 %collective-permute-start.18 = (bf16[16,2944]{1,0:T(8,128)(2,1)S(1)}, bf16[16,2944]{1,0:T(8,128)(2,1)S(1)}, u32[]{:S(2)}, u32[]{:S(2)}) collective-permute-start(bf16[16,2944]{1,0:T(8,128)(2,1)S(1)} %get-tuple-element.108), channel_id=1, source_target_pairs={{0,24},{1,25},{2,26},{3,27},{4,28},{5,29},{6,30},{7,31},{8,0},{9,1... | collective-permute-start | bytes 282632 | tf_op jit(solution)/shard_map/ppermute | solution.py:307
  108.1 1.6 %convolution_convert_fusion = bf16[512,640]{1,0:T(8,128)(2,1)} fusion(bf16[320,512]{1,0:T(8,128)(2,1)S(1)} %collective-permute-done.21, bf16[320,512]{1,0:T(8,128)(2,1)S(1)} %get-tuple-element.95, pred[320,640]{1,0:T(32,128)(4,1)S(1)} %get-tuple-element.117, pred[320,640]{1,0:T(32,128)(4,1)S(1)} %get-tuple-element.118), kind=kOutput, calls=%fused_computation.8 | convolution fusion | flops 421478400 | bytes 1720320 | tf_op jit(solution)/shard_map/dot_general | solution.py:21
  109.9 0.5 collective-permute-start.20
  110.3 1.0 add_convert_fusion
  111.3 0.4 collective-permute-done.18.refs_5_
  111.8 6.3 %collective-permute-done.19.refs_6_ = bf16[16,2944]{1,0:T(8,128)(2,1)S(1)} collective-permute-done((bf16[16,2944]{1,0:T(8,128)(2,1)S(1)}, bf16[16,2944]{1,0:T(8,128)(2,1)S(1)}, u32[]{:S(2)}, u32[]{:S(2)}) %collective-permute-start.19) | collective-permute-done | bytes 94240 | tf_op jit(solution)/shard_map/ppermute | solution.py:307
  118.1 2.2 %shard_map.124 = (f32[9,40,320]{2,1,0:T(8,128)}, f32[9,40,320]{2,1,0:T(8,128)}, f32[9,40,320]{2,1,0:T(8,128)}) custom-call(s32[2]{0:T(128)S(1)} %pad_add_fusion.3.place_ref, f32[9,40,320]{2,1,0:T(8,128)S(1)} %bitcast.47, f32[9,40,320]{2,1,0:T(8,128)S(1)} %bitcast.49, f32[9,40,320]{2,1,0:T(8,128)S(1)} %bitcast.50, ...), custom_call_target="tpu_custom_call" | custom-call | bytes 1048576 | tf_op jit(solution)/shard_map/pallas_call | solution.py:199
  (66 shorter events, 3.5 us)
Async XLA Ops:
  0.6 12.3 %copy-start = (bf16[1,16,32,640]{3,2,1,0:T(8,128)(2,1)S(1)}, bf16[1,16,32,640]{3,2,1,0:T(8,128)(2,1)}, u32[]{:S(2)}) copy-start(bf16[1,16,32,640]{3,2,1,0:T(8,128)(2,1)} %param.9) | copy-start | bytes 1966084
  0.7 1.1 copy-start.1
  2.5 12.0 %collective-permute-start = (bf16[40,2944]{1,0:T(8,128)(2,1)S(1)}, bf16[40,2944]{1,0:T(8,128)(2,1)S(1)}, u32[]{:S(2)}, u32[]{:S(2)}) collective-permute-start(bf16[40,2944]{1,0:T(8,128)(2,1)S(1)} %shard_map.119), channel_id=1, source_target_pairs={{0,8},{1,9},{2,10},{3,11},{4,12},{5,13},{6,14},{7,15},{8,16},{9,17... | collective-permute-start | bytes 706568 | tf_op jit(solution)/shard_map/ppermute | solution.py:307
  5.6 18.0 %collective-permute-start.1 = (bf16[40,2944]{1,0:T(8,128)(2,1)S(1)}, bf16[40,2944]{1,0:T(8,128)(2,1)S(1)}, u32[]{:S(2)}, u32[]{:S(2)}) collective-permute-start(bf16[40,2944]{1,0:T(8,128)(2,1)S(1)} %shard_map.119), channel_id=1, source_target_pairs={{0,16},{1,17},{2,18},{3,19},{4,20},{5,21},{6,22},{7,23},{8,24},{9,... | collective-permute-start | bytes 706568 | tf_op jit(solution)/shard_map/ppermute | solution.py:307
  8.2 15.4 %collective-permute-start.2 = (bf16[40,2944]{1,0:T(8,128)(2,1)S(1)}, bf16[40,2944]{1,0:T(8,128)(2,1)S(1)}, u32[]{:S(2)}, u32[]{:S(2)}) collective-permute-start(bf16[40,2944]{1,0:T(8,128)(2,1)S(1)} %shard_map.119), channel_id=1, source_target_pairs={{0,24},{1,25},{2,26},{3,27},{4,28},{5,29},{6,30},{7,31},{8,0},{9,1... | collective-permute-start | bytes 706568 | tf_op jit(solution)/shard_map/ppermute | solution.py:307
  10.4 4.1 %collective-permute-start.3 = (bf16[1,1,32,640]{3,2,1,0:T(8,128)(2,1)S(1)}, bf16[1,1,32,640]{3,2,1,0:T(8,128)(2,1)S(1)}, u32[]{:S(2)}, u32[]{:S(2)}) collective-permute-start(bf16[1,1,32,640]{3,2,1,0:T(8,128)(2,1)S(1)} %slice_select_fusion.1), channel_id=1, source_target_pairs={{0,1},{1,0},{2,3},{3,2},{4,5},{5,4},{6,7},{7,6},{8,9},{9,8},{10,11... | collective-permute-start | bytes 122888 | tf_op jit(solution)/shard_map/ppermute | solution.py:236
  12.9 1.5 %copy-start.5 = (bf16[1,16,32,640]{3,2,1,0:T(8,128)(2,1)S(1)}, bf16[1,16,32,640]{3,2,1,0:T(8,128)(2,1)}, u32[]{:S(2)}) copy-start(bf16[1,16,32,640]{3,2,1,0:T(8,128)(2,1)} %param.8) | copy-start | bytes 1966084
  23.8 9.7 %collective-permute-start.4 = (bf16[96,2944]{1,0:T(8,128)(2,1)S(1)}, bf16[96,2944]{1,0:T(8,128)(2,1)S(1)}, u32[]{:S(2)}, u32[]{:S(2)}) collective-permute-start(bf16[96,2944]{1,0:T(8,128)(2,1)S(1)} %get-tuple-element.104.own_ref), channel_id=1, source_target_pairs={{0,1},{1,0},{2,6},{3,7},{4,5},{5,4},{6,2},{7,3},{8,9},{9,8},{10,14... | collective-permute-start | bytes 1695752 | tf_op jit(solution)/shard_map/ppermute | solution.py:307
  25.4 2.0 %collective-permute-start.8 = (bf16[320,512]{1,0:T(8,128)(2,1)S(1)}, bf16[320,512]{1,0:T(8,128)(2,1)S(1)}, u32[]{:S(2)}, u32[]{:S(2)}) collective-permute-start(bf16[320,512]{1,0:T(8,128)(2,1)S(1)} %get-tuple-element.98), channel_id=1, source_target_pairs={{0,2},{1,3},{2,0},{3,1},{4,6},{5,7},{6,4},{7,5},{8,10},{9,11},{10,... | collective-permute-start | bytes 983048 | tf_op jit(solution)/shard_map/ppermute | solution.py:307
  25.5 14.1 %collective-permute-start.6 = (bf16[64,2944]{1,0:T(8,128)(2,1)S(1)}, bf16[64,2944]{1,0:T(8,128)(2,1)S(1)}, u32[]{:S(2)}, u32[]{:S(2)}) collective-permute-start(bf16[64,2944]{1,0:T(8,128)(2,1)S(1)} %get-tuple-element.110.own_ref), channel_id=1, source_target_pairs={{0,1},{1,0},{2,6},{3,7},{4,5},{5,4},{6,2},{7,3},{8,9},{9,8},{10,14... | collective-permute-start | bytes 1130504 | tf_op jit(solution)/shard_map/ppermute | solution.py:307
  26.8 14.6 %collective-permute-start.7 = (bf16[1,18,32,640]{3,2,1,0:T(8,128)(2,1)S(1)}, bf16[1,18,32,640]{3,2,1,0:T(8,128)(2,1)S(1)}, u32[]{:S(2)}, u32[]{:S(2)}) collective-permute-start(bf16[1,18,32,640]{3,2,1,0:T(8,128)(2,1)S(1)} %pad_maximum_fusion.5), channel_id=1, source_target_pairs={{0,2},{1,3},{2,0},{3,1},{4,6},{5,7},{6,4},{7,5},{8,10},{9,11},{10,... | collective-permute-start | bytes 2211848 | tf_op jit(solution)/shard_map/ppermute | solution.py:307
  33.6 15.7 %collective-permute-start.5 = (bf16[2,96,2944]{2,1,0:T(8,128)(2,1)S(1)}, bf16[2,96,2944]{2,1,0:T(8,128)(2,1)S(1)}, u32[]{:S(2)}, u32[]{:S(2)}) collective-permute-start(bf16[2,96,2944]{2,1,0:T(8,128)(2,1)S(1)} %pad_maximum_fusion.1), channel_id=1, source_target_pairs={{0,4},{1,5},{2,3},{3,2},{4,0},{5,1},{6,7},{7,6},{8,12},{9,13},{10,... | collective-permute-start | bytes 3391496 | tf_op jit(solution)/shard_map/ppermute | solution.py:307
  39.7 18.9 %collective-permute-start.10 = (bf16[2,64,2944]{2,1,0:T(8,128)(2,1)S(1)}, bf16[2,64,2944]{2,1,0:T(8,128)(2,1)S(1)}, u32[]{:S(2)}, u32[]{:S(2)}) collective-permute-start(bf16[2,64,2944]{2,1,0:T(8,128)(2,1)S(1)} %pad_maximum_fusion.4), channel_id=1, source_target_pairs={{0,4},{1,5},{2,3},{3,2},{4,0},{5,1},{6,7},{7,6},{8,12},{9,13},{10,... | collective-permute-start | bytes 2261000 | tf_op jit(solution)/shard_map/ppermute | solution.py:307
  57.1 15.7 %collective-permute-start.9 = (bf16[2,96,2944]{2,1,0:T(8,128)(2,1)S(1)}, bf16[2,96,2944]{2,1,0:T(8,128)(2,1)S(1)}, u32[]{:S(2)}, u32[]{:S(2)}) collective-permute-start(bf16[2,96,2944]{2,1,0:T(8,128)(2,1)S(1)} %get-tuple-element.60), channel_id=1, source_target_pairs={{0,4},{1,5},{2,3},{3,2},{4,0},{5,1},{6,7},{7,6},{8,12},{9,13},{10,... | collective-permute-start | bytes 3391496 | tf_op jit(solution)/shard_map/ppermute | solution.py:307
  65.3 19.7 %collective-permute-start.12 = (bf16[2,64,2944]{2,1,0:T(8,128)(2,1)S(1)}, bf16[2,64,2944]{2,1,0:T(8,128)(2,1)S(1)}, u32[]{:S(2)}, u32[]{:S(2)}) collective-permute-start(bf16[2,64,2944]{2,1,0:T(8,128)(2,1)S(1)} %get-tuple-element.62), channel_id=1, source_target_pairs={{0,4},{1,5},{2,3},{3,2},{4,0},{5,1},{6,7},{7,6},{8,12},{9,13},{10,... | collective-permute-start | bytes 2261000 | tf_op jit(solution)/shard_map/ppermute | solution.py:307
  73.1 4.7 %collective-permute-start.13 = (bf16[2,1,32,320]{3,2,1,0:T(8,128)(2,1)S(1)}, bf16[2,1,32,320]{3,2,1,0:T(8,128)(2,1)S(1)}, u32[]{:S(2)}, u32[]{:S(2)}) collective-permute-start(bf16[2,1,32,320]{3,2,1,0:T(8,128)(2,1)S(1)} %slice_select_fusion), channel_id=1, source_target_pairs={{0,1},{1,0},{2,3},{3,2},{4,5},{5,4},{6,7},{7,6},{8,9},{9,8},{10,11... | collective-permute-start | bytes 122888 | tf_op jit(solution)/shard_map/ppermute | solution.py:236
  74.8 12.6 %collective-permute-start.11 = (bf16[96,2944]{1,0:T(8,128)(2,1)S(1)}, bf16[96,2944]{1,0:T(8,128)(2,1)S(1)}, u32[]{:S(2)}, u32[]{:S(2)}) collective-permute-start(bf16[96,2944]{1,0:T(8,128)(2,1)S(1)} %fusion.9), channel_id=1, source_target_pairs={{0,1},{1,0},{2,6},{3,7},{4,5},{5,4},{6,2},{7,3},{8,9},{9,8},{10,14... | collective-permute-start | bytes 1695752 | tf_op jit(solution)/shard_map/ppermute | solution.py:307
  87.8 10.8 %collective-permute-start.17 = (bf16[64,2944]{1,0:T(8,128)(2,1)S(1)}, bf16[64,2944]{1,0:T(8,128)(2,1)S(1)}, u32[]{:S(2)}, u32[]{:S(2)}) collective-permute-start(bf16[64,2944]{1,0:T(8,128)(2,1)S(1)} %fusion.10), channel_id=1, source_target_pairs={{0,1},{1,0},{2,6},{3,7},{4,5},{5,4},{6,2},{7,3},{8,9},{9,8},{10,14... | collective-permute-start | bytes 1130504 | tf_op jit(solution)/shard_map/ppermute | solution.py:307
  89.4 20.3 %collective-permute-start.14 = (bf16[24,2944]{1,0:T(8,128)(2,1)S(1)}, bf16[24,2944]{1,0:T(8,128)(2,1)S(1)}, u32[]{:S(2)}, u32[]{:S(2)}) collective-permute-start(bf16[24,2944]{1,0:T(8,128)(2,1)S(1)} %get-tuple-element.102), channel_id=1, source_target_pairs={{0,24},{1,25},{2,26},{3,27},{4,28},{5,29},{6,30},{7,31},{8,0},{9,1... | collective-permute-start | bytes 423944 | tf_op jit(solution)/shard_map/ppermute | solution.py:307
  96.0 15.3 %collective-permute-start.15 = (bf16[24,2944]{1,0:T(8,128)(2,1)S(1)}, bf16[24,2944]{1,0:T(8,128)(2,1)S(1)}, u32[]{:S(2)}, u32[]{:S(2)}) collective-permute-start(bf16[24,2944]{1,0:T(8,128)(2,1)S(1)} %get-tuple-element.101), channel_id=1, source_target_pairs={{0,16},{1,17},{2,18},{3,19},{4,20},{5,21},{6,22},{7,23},{8,24},{9,... | collective-permute-start | bytes 423944 | tf_op jit(solution)/shard_map/ppermute | solution.py:307
  96.4 14.9 %collective-permute-start.16 = (bf16[24,2944]{1,0:T(8,128)(2,1)S(1)}, bf16[24,2944]{1,0:T(8,128)(2,1)S(1)}, u32[]{:S(2)}, u32[]{:S(2)}) collective-permute-start(bf16[24,2944]{1,0:T(8,128)(2,1)S(1)} %get-tuple-element.100), channel_id=1, source_target_pairs={{0,8},{1,9},{2,10},{3,11},{4,12},{5,13},{6,14},{7,15},{8,16},{9,17... | collective-permute-start | bytes 423944 | tf_op jit(solution)/shard_map/ppermute | solution.py:307
  96.6 13.2 %collective-permute-start.22 = (f32[512,640]{1,0:T(8,128)S(1)}, f32[512,640]{1,0:T(8,128)S(1)}, u32[]{:S(2)}, u32[]{:S(2)}) collective-permute-start(f32[512,640]{1,0:T(8,128)S(1)} %shard_map.122), channel_id=1, source_target_pairs={{0,2},{1,3},{2,0},{3,1},{4,6},{5,7},{6,4},{7,5},{8,10},{9,11},{10,... | collective-permute-start | bytes 3932168 | tf_op jit(solution)/shard_map/ppermute | solution.py:307
  98.9 3.8 %collective-permute-start.21 = (bf16[320,512]{1,0:T(8,128)(2,1)S(1)}, bf16[320,512]{1,0:T(8,128)(2,1)S(1)}, u32[]{:S(2)}, u32[]{:S(2)}) collective-permute-start(bf16[320,512]{1,0:T(8,128)(2,1)S(1)} %get-tuple-element.96), channel_id=1, source_target_pairs={{0,2},{1,3},{2,0},{3,1},{4,6},{5,7},{6,4},{7,5},{8,10},{9,11},{10,... | collective-permute-start | bytes 983048 | tf_op jit(solution)/shard_map/ppermute | solution.py:307
  102.7 9.0 %collective-permute-start.18 = (bf16[16,2944]{1,0:T(8,128)(2,1)S(1)}, bf16[16,2944]{1,0:T(8,128)(2,1)S(1)}, u32[]{:S(2)}, u32[]{:S(2)}) collective-permute-start(bf16[16,2944]{1,0:T(8,128)(2,1)S(1)} %get-tuple-element.108), channel_id=1, source_target_pairs={{0,24},{1,25},{2,26},{3,27},{4,28},{5,29},{6,30},{7,31},{8,0},{9,1... | collective-permute-start | bytes 282632 | tf_op jit(solution)/shard_map/ppermute | solution.py:307
  109.7 8.3 %collective-permute-start.19 = (bf16[16,2944]{1,0:T(8,128)(2,1)S(1)}, bf16[16,2944]{1,0:T(8,128)(2,1)S(1)}, u32[]{:S(2)}, u32[]{:S(2)}) collective-permute-start(bf16[16,2944]{1,0:T(8,128)(2,1)S(1)} %get-tuple-element.107), channel_id=1, source_target_pairs={{0,16},{1,17},{2,18},{3,19},{4,20},{5,21},{6,22},{7,23},{8,24},{9,... | collective-permute-start | bytes 282632 | tf_op jit(solution)/shard_map/ppermute | solution.py:307
  109.9 8.2 %copy-start.2 = (f32[9,320,40]{1,2,0:T(8,128)S(1)}, f32[9,320,40]{1,2,0:T(8,128)}, u32[]{:S(2)}) copy-start(f32[9,320,40]{1,2,0:T(8,128)} %param.10) | copy-start | bytes 1382404
  109.9 8.2 %copy-start.3 = (f32[9,320,40]{1,2,0:T(8,128)S(1)}, f32[9,320,40]{1,2,0:T(8,128)}, u32[]{:S(2)}) copy-start(f32[9,320,40]{1,2,0:T(8,128)} %param.11) | copy-start | bytes 1382404
  109.9 8.2 %copy-start.4 = (f32[9,320,40]{1,2,0:T(8,128)S(1)}, f32[9,320,40]{1,2,0:T(8,128)}, u32[]{:S(2)}) copy-start(f32[9,320,40]{1,2,0:T(8,128)} %param.12) | copy-start | bytes 1382404
  109.9 8.2 %collective-permute-start.20 = (bf16[16,2944]{1,0:T(8,128)(2,1)S(1)}, bf16[16,2944]{1,0:T(8,128)(2,1)S(1)}, u32[]{:S(2)}, u32[]{:S(2)}) collective-permute-start(bf16[16,2944]{1,0:T(8,128)(2,1)S(1)} %get-tuple-element.106), channel_id=1, source_target_pairs={{0,8},{1,9},{2,10},{3,11},{4,12},{5,13},{6,14},{7,15},{8,16},{9,17... | collective-permute-start | bytes 282632 | tf_op jit(solution)/shard_map/ppermute | solution.py:307

commit v4 on v3

--- a/solution.py
+++ b/solution.py
@@ -15,6 +15,7 @@
 VMEM_LIMIT = 28 << 20
 TAPS = 9
 CHUNKS = (24, 16)
+ROUTE_A = 8
 
 
 def mm(a, b, dims):
@@ -66,9 +67,9 @@
         ).astype(BF)
 
 
-def routed_kernel(
-    width, place_ref, own_ref, near_ref, far_ref, x_ref, t_ref, k_ref, s_ref, e_ref, keep_ref, send_ref, mid_ref, flat_ref
-):
+def routed_kernel(width, extra, place_ref, own_ref, near_ref, far_ref, x_ref, t_ref, *refs):
+    a_refs, refs = refs[:extra], refs[extra:]
+    k_ref, s_ref, e_ref, keep_ref, send_ref, mid_ref, flat_ref = refs
     first, on_core0 = place_ref[0] == 0, place_ref[1] == 0
     rows = k_ref.shape[0]
     near_y, far_y = slice(0, rows // 2), slice(rows // 2, rows)
@@ -77,8 +78,13 @@
 
     def load(at):
         near, far = near_ref[:, at], far_ref[0, :, at]
-        own = jnp.concatenate([own_ref[:, at], jnp.where(on_core0, far, near)])
-        other = jnp.concatenate([jnp.where(on_core0, near, far), far_ref[1, :, at]])
+        own = [own_ref[:, at], jnp.where(on_core0, far, near)]
+        other = [jnp.where(on_core0, near, far), far_ref[1, :, at]]
+        for a_ref in a_refs:
+            half = a_ref.shape[1] // 2
+            own = [a_ref[0, :half, at], own[0], a_ref[0, half:, at], own[1]]
+            other = [a_ref[1, :half, at], other[0], a_ref[1, half:, at], other[1]]
+        own, other = jnp.concatenate(own), jnp.concatenate(other)
         return jnp.where(first, own, other), jnp.where(first, other, own)
 
     for tap in range(TAPS):
@@ -154,9 +160,9 @@
 
     def grad(at):
         sums = []
-        for i in range(0, len(parts), 4):
-            p0, p1, p2, p3 = [ref[:, at].astype(F32) for ref in parts[i : i + 4]]
-            sums.append((p0 + p1) + (p2 + p3))
+        for i in range(0, len(parts), 3):
+            p0, p1, p2 = [ref[:, at].astype(F32) for ref in parts[i : i + 3]]
+            sums.append((p0 + p1) + p2)
         return jnp.concatenate(sums) * scale
 
     for tap in range(TAPS):
@@ -321,6 +327,7 @@
     along_xy = hop(lambda z, y, core, x: (z, y ^ core, core, x ^ 1 ^ core))
     along_yx = hop(lambda z, y, core, x: (z, y ^ 1 ^ core, core, x ^ core))
     along_z = lambda v, s: hop(lambda z, y, core, x: (z + s, y, core, x))(v)
+    along_pair = hop(lambda z, y, core, x: (z ^ 1, y, core, x))
     lanes = TAPS * 256 + 640
 
     place = jnp.stack([half, core]).astype(jnp.int32)
@@ -329,11 +336,18 @@
     piece = vmem_call(pack_kernel, shape(per, lanes), 1, place, by_tap(weight))
     piece, latents, target = phase(piece, latents, target)
 
+    def turned(v):
+        return jnp.where(core == 0, v.swapaxes(0, 1), v)
+
     chunk_a, chunk_b = CHUNKS
-    grids = [
-        np.indices((2, 4, chunk_a)).reshape(3, -1),
-        np.indices((2, 4, chunk_b)).reshape(3, -1) + [[0], [0], [chunk_a]],
-    ]
+    grids = []
+    for begin, counts in ((0, (ROUTE_A, chunk_a - ROUTE_A)), (chunk_a, (chunk_b,))):
+        for dist_y in range(2):
+            at = begin
+            for count in counts:
+                dist_z, within = np.indices((4, count)).reshape(2, -1)
+                grids.append(np.stack([np.full_like(dist_z, dist_y), dist_z, at + within]))
+                at += count
     dist_y, dist_z, within = np.concatenate(grids, axis=1).astype(np.int32)
     block = ((z - dist_z) % 4) * 4 + (y ^ dist_y) * 2
     everything = jnp.arange(channels, dtype=jnp.int32)
@@ -349,22 +363,32 @@
             total = total + term.astype(F32)
         return total
 
-    bz = [along_z(piece, s) for s in (1, 2, 3)]
+    pa, pb = piece[:ROUTE_A], piece[ROUTE_A:]
+    bz = [along_z(pb, s) for s in (1, 2, 3)]
+    pa = jnp.stack([pa, along_xy(pa)])
+    t = mm(pick, target.reshape(cells, channels), NT).astype(BF)
+    pa, latents, t = phase(pa, latents, t)
     banded = with_halo(latents)
-    t = mm(pick, target.reshape(cells, channels), NT).astype(BF)
-    bz, banded, t = phase(bz, banded, t)
-    t = jnp.concatenate([t[:rows], along_core(t[rows:])], axis=1)
-    own_a = jnp.concatenate([v[:chunk_a] for v in [piece] + bz])
-    own_b = jnp.concatenate([v[chunk_a:] for v in [piece] + bz])
+    pa = turned(jnp.stack([pa, along_yx(pa)]))
+    bz, pa, banded, t = phase(bz, pa, banded, t)
+    t_in, banded_in = along_core(t[rows:]), along_core(banded)
+    t = jnp.concatenate([t[:rows], t_in], axis=1)
+    pa, t_in = phase(pa, t_in)
+    cut = chunk_a - ROUTE_A
+    own_a = jnp.concatenate([v[:cut] for v in [pb] + bz])
+    own_b = jnp.concatenate([v[cut:] for v in [pb] + bz])
     near_a, near_b = along_xy(own_a), along_xy(own_b)
-    x = wide_cells(jnp.concatenate([banded, along_core(banded)]))
+    az = [along_z(pa, s) for s in (1, 2, 3)]
+    x = wide_cells(jnp.concatenate([banded, banded_in]))
     far_a = along_yx(jnp.stack([own_a, near_a]))
     far_b = along_yx(jnp.stack([own_b, near_b]))
-
-    def compute(own, near, far, t):
+    far_a, near_b, x, t, az = phase(far_a, near_b, x, t, az)
+    by_a = jnp.stack([pa] + az, axis=2).reshape(2, 8 * ROUTE_A, lanes)
+
+    def compute(own, near, far, t, *extra):
         n = t.shape[0]
         return vmem_call(
-            functools.partial(routed_kernel, width),
+            functools.partial(routed_kernel, width, len(extra)),
             (shape(n, TAPS * channels), shape(n, 2 * cells), shape(2 * cells, n))
             + (shape(2, n // 2, lanes),) * 2,
             1,
@@ -374,18 +398,16 @@
             far,
             x,
             t,
+            *extra,
             scratch=[pltpu.VMEM((TAPS, n, 128), F32), pltpu.VMEM((n, 2 * cells), BF)],
             flops=30 * 10**9,
         )
 
-    far_a, near_b, x, t = phase(far_a, near_b, x, t)
-    kernel_a, student_a, error_a, keep_a, send_a = compute(own_a, near_a, far_a, t[:rows_a])
+    kernel_a, student_a, error_a, keep_a, send_a = compute(own_a, near_a, far_a, t[:rows_a], by_a)
     got_a = along_yx(send_a)
     kernel_b, student_b, error_b, keep_b, send_b = compute(own_b, near_b, far_b, t[rows_a:])
     got_b = along_yx(send_b)
     got_a, send_b, error_b = phase(got_a, send_b, error_b)
-
-    got2_a = along_xy(plus(keep_a[1], got_a[1]).astype(BF))
     error = jnp.concatenate([error_a, error_b], axis=1)
     shifted = back_cells(with_halo(error.reshape(2, band, width, rows)))
 
@@ -401,22 +423,37 @@
             flops=20 * 10**9,
         )
 
+    got2_a = along_xy(plus(keep_a[1], got_a[1]).astype(BF))
     back_other = back(1)
-    got2_a, got_b, back_other, shifted = phase(got2_a, got_b, back_other, shifted)
+    student = jnp.concatenate([student_a, student_b])
+    student_in = along_core(student[:, cells:])
+    got2_a, got_b, back_other, shifted, student_in = phase(
+        got2_a, got_b, back_other, shifted, student_in
+    )
+    even = z % 2 == 0
+
+    def outward(keep, got, got2, *counts):
+        g = plus(keep[0], got[0], got2).astype(BF)
+        cuts = np.cumsum([4 * count for count in counts])[:-1]
+        g = [v.reshape(4, -1, lanes) for v in jnp.split(g, cuts)]
+        g = jnp.concatenate(g, axis=1)
+        send = jnp.where(even, jnp.stack([g[3], g[1]]), jnp.stack([g[1], g[3]]))
+        return g, along_pair(send)
+
+    g_a, pair_a = outward(keep_a, got_a, got2_a, ROUTE_A, cut)
+    got2_b = along_xy(plus(keep_b[1], got_b[1]).astype(BF))
+    back_own = back(0)
+    got2_b, student, student_in, back_own, back_other = phase(
+        got2_b, student, student_in, back_own, back_other
+    )
+    g_b, pair_b = outward(keep_b, got_b, got2_b, chunk_b)
+    last_a = along_z(plus(g_a[2], pair_a[1]).astype(BF), 2)
+    last_b = along_z(plus(g_b[2], pair_b[1]).astype(BF), 2)
     back_in = along_core(back_other)
-    gb_a = plus(keep_a[0], got_a[0], got2_a).astype(BF).reshape(4, chunk_a, lanes)
-    bz_a = [along_z(gb_a[s], -s) for s in (1, 2, 3)]
-    got2_b = along_xy(plus(keep_b[1], got_b[1]).astype(BF))
-    got2_b, shifted, student_a, student_b = phase(got2_b, shifted, student_a, student_b)
-    gb_b = plus(keep_b[0], got_b[0], got2_b).astype(BF).reshape(4, chunk_b, lanes)
-    bz_b = [along_z(gb_b[s], -s) for s in (1, 2, 3)]
-    back_own = back(0)
-
-    student = jnp.concatenate([student_a, student_b])
-    both = jnp.concatenate([student[:, :cells], along_core(student[:, cells:])])
+    both = jnp.concatenate([student[:, :cells], student_in])
     out = mm(both, pick, (((0,), (0,)), ((), ()))).astype(BF).reshape(latents.shape)
     input_grad = (back_own + back_in).astype(BF).reshape(latents.shape)
-    bz_a, bz_b, out, input_grad = phase(bz_a, bz_b, out, input_grad)
+    last_a, last_b, out, input_grad = phase(last_a, last_b, out, input_grad)
     news = vmem_call(
         functools.partial(adam_kernel, 1.0 / (b * lax.axis_size("dp"))),
         (shape(TAPS, per, weight.shape[1], dtype=F32),) * 3,
@@ -425,10 +462,12 @@
         by_tap(weight),
         by_tap(moment1),
         by_tap(moment2),
-        gb_a[0],
-        *bz_a,
-        gb_b[0],
-        *bz_b,
+        g_a[0],
+        pair_a[0],
+        last_a,
+        g_b[0],
+        pair_b[0],
+        last_b,
     )
     return (out, input_grad, *map(by_tap, news))
 

time: 121 us -> 114 us (0.942)
  waiting for transfers between devices: 46.4 us -> 34.9 us
  starting transfers between devices: 36.2 us -> 40.7 us
    ppermute x21 -> x24, waiting for transfers between devices: 43.3 us -> 31.5 us  [hop(): return lambda v: lax.ppermute(v, ('dp', 'rows'), pairs)]
    ppermute x21 -> x24, starting transfers between devices: 33.1 us -> 37.4 us  [hop(): return lambda v: lax.ppermute(v, ('dp', 'rows'), pairs)]
  transfers between devices with their start and end apart: 23 -> 26, of which waited for: 11 -> 12; matrix products, arithmetic and copies ran while one was open for 9% -> 9% of each run, Pallas kernels for 18% -> 19%
where the time goes in v4:
time: 114 us
  starting transfers between devices  40.7 us (36%)
  waiting for transfers between devices  34.9 us (31%)
  Pallas kernels  24.2 us (21%)
  other arithmetic  5.72 us (5%)
  local copies, waits for them, and re-layouts  4.87 us (4%)
  matrix products  2.35 us (2%)
  between operations  1.19 us (1%)
    ppermute x24, starting transfers between devices, hop(): return lambda v: lax.ppermute(v, ('dp', 'rows'), pairs)  37.4 us
    ppermute x24, waiting for transfers between devices, hop(): return lambda v: lax.ppermute(v, ('dp', 'rows'), pairs)  31.5 us
    pallas_call x6, Pallas kernels, vmem_call(): pl.pallas_call(kernel, out_shape=outs, in_specs=[pl.BlockSpec(memory_spac...  24.2 us
    ppermute x2, waiting for transfers between devices, with_halo(): got = lax.ppermute(edge, 'rows', [(0, 1), (1, 0)])  3.34 us
    ppermute x2, starting transfers between devices, with_halo(): got = lax.ppermute(edge, 'rows', [(0, 1), (1, 0)])  3.28 us
    dot_general x2, matrix products, mm(): return lax.dot_general(a, b, dims, preferred_element_type=F32)  2.35 us
  transfers between devices with their start and end apart: 26, of which 12 were waited for; matrix products, arithmetic and copies ran while one was open for 9% of the time, Pallas kernels for 19%

profile of v4, /device:TPU:0, one launch (start us, length us, event | category | flops | bytes accessed | tf_op | source)
XLA Modules:
  0.0 113.8 jit_solution(8613384412403208935)
XLA Ops:
  0.7 1.1 copy-done.1
  1.8 0.7 shard_map.119
  2.6 3.1 %collective-permute-start = (bf16[32,2944]{1,0:T(8,128)(2,1)S(1)}, bf16[32,2944]{1,0:T(8,128)(2,1)S(1)}, u32[]{:S(2)}, u32[]{:S(2)}) collective-permute-start(bf16[32,2944]{1,0:T(8,128)(2,1)S(1)} %slice.159), channel_id=1, source_target_pairs={{0,8},{1,9},{2,10},{3,11},{4,12},{5,13},{6,14},{7,15},{8,16},{9,17... | collective-permute-start | bytes 565256 | tf_op jit(solution)/shard_map/ppermute | solution.py:313
  5.6 2.6 %collective-permute-start.1 = (bf16[32,2944]{1,0:T(8,128)(2,1)S(1)}, bf16[32,2944]{1,0:T(8,128)(2,1)S(1)}, u32[]{:S(2)}, u32[]{:S(2)}) collective-permute-start(bf16[32,2944]{1,0:T(8,128)(2,1)S(1)} %slice.159), channel_id=1, source_target_pairs={{0,16},{1,17},{2,18},{3,19},{4,20},{5,21},{6,22},{7,23},{8,24},{9,... | collective-permute-start | bytes 565256 | tf_op jit(solution)/shard_map/ppermute | solution.py:313
  8.2 1.3 %collective-permute-start.2 = (bf16[32,2944]{1,0:T(8,128)(2,1)S(1)}, bf16[32,2944]{1,0:T(8,128)(2,1)}, u32[]{:S(2)}, u32[]{:S(2)}) collective-permute-start(bf16[32,2944]{1,0:T(8,128)(2,1)S(1)} %slice.159), channel_id=1, source_target_pairs={{0,24},{1,25},{2,26},{3,27},{4,28},{5,29},{6,30},{7,31},{8,0},{9,1... | collective-permute-start | bytes 565256 | tf_op jit(solution)/shard_map/ppermute | solution.py:313
  9.6 1.6 %collective-permute-start.3 = (bf16[8,2944]{1,0:T(8,128)(2,1)S(1)}, bf16[8,2944]{1,0:T(8,128)(2,1)S(1)}, u32[]{:S(2)}, u32[]{:S(2)}) collective-permute-start(bf16[8,2944]{1,0:T(8,128)(2,1)S(1)} %get-tuple-element.122), channel_id=1, source_target_pairs={{0,1},{1,0},{2,6},{3,7},{4,5},{5,4},{6,2},{7,3},{8,9},{9,8},{10,14... | collective-permute-start | bytes 141320 | tf_op jit(solution)/shard_map/ppermute | solution.py:313
  11.1 0.7 multiply_add_fusion.1
  12.2 0.7 convolution_convert_fusion.1
  12.9 0.8 collective-permute-done.3
  13.8 1.6 %collective-permute-start.5 = (bf16[1,1,32,640]{3,2,1,0:T(8,128)(2,1)S(1)}, bf16[1,1,32,640]{3,2,1,0:T(8,128)(2,1)S(1)}, u32[]{:S(2)}, u32[]{:S(2)}) collective-permute-start(bf16[1,1,32,640]{3,2,1,0:T(8,128)(2,1)S(1)} %slice_select_fusion.1), channel_id=1, source_target_pairs={{0,1},{1,0},{2,3},{3,2},{4,5},{5,4},{6,7},{7,6},{8,9},{9,8},{10,11... | collective-permute-start | bytes 122888 | tf_op jit(solution)/shard_map/ppermute | solution.py:242
  15.4 1.6 %collective-permute-start.4 = (bf16[2,8,2944]{2,1,0:T(8,128)(2,1)S(1)}, bf16[2,8,2944]{2,1,0:T(8,128)(2,1)S(1)}, u32[]{:S(2)}, u32[]{:S(2)}) collective-permute-start(bf16[2,8,2944]{2,1,0:T(8,128)(2,1)S(1)} %pad_maximum_fusion.12), channel_id=1, source_target_pairs={{0,4},{1,5},{2,3},{3,2},{4,0},{5,1},{6,7},{7,6},{8,12},{9,13},{10,... | collective-permute-start | bytes 282632 | tf_op jit(solution)/shard_map/ppermute | solution.py:313
  16.9 0.9 collective-permute-done.5
  18.0 2.0 %collective-permute-done.4 = bf16[2,8,2944]{2,1,0:T(8,128)(2,1)S(1)} collective-permute-done((bf16[2,8,2944]{2,1,0:T(8,128)(2,1)S(1)}, bf16[2,8,2944]{2,1,0:T(8,128)(2,1)S(1)}, u32[]{:S(2)}, u32[]{:S(2)}) %collective-permute-start.4) | collective-permute-done | bytes 94240 | tf_op jit(solution)/shard_map/ppermute | solution.py:313
  20.6 1.0 fusion.32
  21.6 1.5 %collective-permute-start.6 = (bf16[64,2944]{1,0:T(8,128)(2,1)S(1)}, bf16[64,2944]{1,0:T(8,128)(2,1)S(1)}, u32[]{:S(2)}, u32[]{:S(2)}) collective-permute-start(bf16[64,2944]{1,0:T(8,128)(2,1)S(1)} %get-tuple-element.118.own_ref), channel_id=1, source_target_pairs={{0,1},{1,0},{2,6},{3,7},{4,5},{5,4},{6,2},{7,3},{8,9},{9,8},{10,14... | collective-permute-start | bytes 1130504 | tf_op jit(solution)/shard_map/ppermute | solution.py:313
  23.4 1.2 %collective-permute-start.8 = (bf16[64,2944]{1,0:T(8,128)(2,1)S(1)}, bf16[64,2944]{1,0:T(8,128)(2,1)S(1)}, u32[]{:S(2)}, u32[]{:S(2)}) collective-permute-start(bf16[64,2944]{1,0:T(8,128)(2,1)S(1)} %get-tuple-element.116.own_ref), channel_id=1, source_target_pairs={{0,1},{1,0},{2,6},{3,7},{4,5},{5,4},{6,2},{7,3},{8,9},{9,8},{10,14... | collective-permute-start | bytes 1130504 | tf_op jit(solution)/shard_map/ppermute | solution.py:313
  24.6 0.6 collective-permute-start.9
  25.2 4.7 %collective-permute-start.11 = (bf16[2,2,8,2944]{3,2,1,0:T(8,128)(2,1)S(1)}, bf16[2,2,8,2944]{3,2,1,0:T(8,128)(2,1)S(1)}, u32[]{:S(2)}, u32[]{:S(2)}) collective-permute-start(bf16[2,2,8,2944]{3,2,1,0:T(8,128)(2,1)S(1)} %bitcast_select_fusion), channel_id=1, source_target_pairs={{0,8},{1,9},{2,10},{3,11},{4,12},{5,13},{6,14},{7,15},{8,16},{9,17... | collective-permute-start | bytes 565256 | tf_op jit(solution)/shard_map/ppermute | solution.py:313
  29.9 1.5 %collective-permute-start.12 = (bf16[2,2,8,2944]{3,2,1,0:T(8,128)(2,1)S(1)}, bf16[2,2,8,2944]{3,2,1,0:T(8,128)(2,1)S(1)}, u32[]{:S(2)}, u32[]{:S(2)}) collective-permute-start(bf16[2,2,8,2944]{3,2,1,0:T(8,128)(2,1)S(1)} %bitcast_select_fusion), channel_id=1, source_target_pairs={{0,16},{1,17},{2,18},{3,19},{4,20},{5,21},{6,22},{7,23},{8,24},{9,... | collective-permute-start | bytes 565256 | tf_op jit(solution)/shard_map/ppermute | solution.py:313
  31.5 3.3 %collective-permute-start.13 = (bf16[2,2,8,2944]{3,2,1,0:T(8,128)(2,1)S(1)}, bf16[2,2,8,2944]{3,2,1,0:T(8,128)(2,1)S(1)}, u32[]{:S(2)}, u32[]{:S(2)}) collective-permute-start(bf16[2,2,8,2944]{3,2,1,0:T(8,128)(2,1)S(1)} %bitcast_select_fusion), channel_id=1, source_target_pairs={{0,24},{1,25},{2,26},{3,27},{4,28},{5,29},{6,30},{7,31},{8,0},{9,1... | collective-permute-start | bytes 565256 | tf_op jit(solution)/shard_map/ppermute | solution.py:313
  35.0 1.6 %collective-permute-start.7 = (bf16[2,64,2944]{2,1,0:T(8,128)(2,1)S(1)}, bf16[2,64,2944]{2,1,0:T(8,128)(2,1)S(1)}, u32[]{:S(2)}, u32[]{:S(2)}) collective-permute-start(bf16[2,64,2944]{2,1,0:T(8,128)(2,1)S(1)} %pad_maximum_fusion.3), channel_id=1, source_target_pairs={{0,4},{1,5},{2,3},{3,2},{4,0},{5,1},{6,7},{7,6},{8,12},{9,13},{10,... | collective-permute-start | bytes 2261000 | tf_op jit(solution)/shard_map/ppermute | solution.py:313
  36.6 0.6 collective-permute-start.15
  37.3 0.8 fusion.25
  38.1 0.9 fusion.2
  39.0 4.9 %collective-permute-done.12 = bf16[2,2,8,2944]{3,2,1,0:T(8,128)(2,1)S(1)} collective-permute-done((bf16[2,2,8,2944]{3,2,1,0:T(8,128)(2,1)S(1)}, bf16[2,2,8,2944]{3,2,1,0:T(8,128)(2,1)S(1)}, u32[]{:S(2)}, u32[]{:S(2)}) %collective-permute-start.12) | collective-permute-done | bytes 188448 | tf_op jit(solution)/shard_map/ppermute | solution.py:313
  43.9 2.7 %collective-permute-done.7.far_ref = bf16[2,64,2944]{2,1,0:T(8,128)(2,1)S(1)} collective-permute-done((bf16[2,64,2944]{2,1,0:T(8,128)(2,1)S(1)}, bf16[2,64,2944]{2,1,0:T(8,128)(2,1)S(1)}, u32[]{:S(2)}, u32[]{:S(2)}) %collective-permute-start.7) | collective-permute-done | bytes 753696 | tf_op jit(solution)/shard_map/ppermute | solution.py:313
  46.9 7.6 %shard_map.120 = (bf16[192,5760]{1,0:T(8,128)(2,1)S(1)}, bf16[192,1024]{1,0:T(8,128)(2,1)S(1)}, bf16[1024,192]{1,0:T(8,128)(2,1)S(1)}, bf16[2,96,2944]{2,1,0:T(8,128)(2,1)S(1)}, bf16[2,96,2944]{2,1,0:T(8,128)(2,1)S(1)}) custom-call(s32[2]{0:T(128)S(1)} %pad_add_fusion.3.place_ref, bf16[64,2944]{1,0:T(8,128)(2,1)S(1)} %get-tuple-element.118.own_ref, ...), custom_call_target="tpu_custom_call" | custom-call | flops 30000001024 | bytes 1048576 | tf_op jit(solution)/shard_map/pallas_call | solution.py:205
  54.5 1.6 %collective-permute-start.14 = (bf16[2,96,2944]{2,1,0:T(8,128)(2,1)S(1)}, bf16[2,96,2944]{2,1,0:T(8,128)(2,1)S(1)}, u32[]{:S(2)}, u32[]{:S(2)}) collective-permute-start(bf16[2,96,2944]{2,1,0:T(8,128)(2,1)S(1)} %get-tuple-element.74), channel_id=1, source_target_pairs={{0,4},{1,5},{2,3},{3,2},{4,0},{5,1},{6,7},{7,6},{8,12},{9,13},{10,... | collective-permute-start | bytes 3391496 | tf_op jit(solution)/shard_map/ppermute | solution.py:313
  56.1 6.6 %shard_map.121 = (bf16[128,5760]{1,0:T(8,128)(2,1)S(1)}, bf16[128,1024]{1,0:T(8,128)(2,1)S(1)}, bf16[1024,128]{1,0:T(8,128)(2,1)S(1)}, bf16[2,64,2944]{2,1,0:T(8,128)(2,1)S(1)}, bf16[2,64,2944]{2,1,0:T(8,128)(2,1)S(1)}) custom-call(s32[2]{0:T(128)S(1)} %pad_add_fusion.3.place_ref, bf16[64,2944]{1,0:T(8,128)(2,1)S(1)} %get-tuple-element.116.own_ref, ...), custom_call_target="tpu_custom_call" | custom-call | flops 30000001024 | bytes 1048576 | tf_op jit(solution)/shard_map/pallas_call | solution.py:205
  62.7 0.6 collective-permute-start.17
  63.4 6.8 %collective-permute-done.14 = bf16[2,96,2944]{2,1,0:T(8,128)(2,1)S(1)} collective-permute-done((bf16[2,96,2944]{2,1,0:T(8,128)(2,1)S(1)}, bf16[2,96,2944]{2,1,0:T(8,128)(2,1)S(1)}, u32[]{:S(2)}, u32[]{:S(2)}) %collective-permute-start.14) | collective-permute-done | bytes 1130528 | tf_op jit(solution)/shard_map/ppermute | solution.py:313
  70.6 1.7 %collective-permute-start.18 = (bf16[2,1,32,320]{3,2,1,0:T(8,128)(2,1)S(1)}, bf16[2,1,32,320]{3,2,1,0:T(8,128)(2,1)S(1)}, u32[]{:S(2)}, u32[]{:S(2)}) collective-permute-start(bf16[2,1,32,320]{3,2,1,0:T(8,128)(2,1)S(1)} %slice_select_fusion), channel_id=1, source_target_pairs={{0,1},{1,0},{2,3},{3,2},{4,5},{5,4},{6,7},{7,6},{8,9},{9,8},{10,11... | collective-permute-start | bytes 122888 | tf_op jit(solution)/shard_map/ppermute | solution.py:242
  72.9 2.5 %collective-permute-done.18 = bf16[2,1,32,320]{3,2,1,0:T(8,128)(2,1)S(1)} collective-permute-done((bf16[2,1,32,320]{3,2,1,0:T(8,128)(2,1)S(1)}, bf16[2,1,32,320]{3,2,1,0:T(8,128)(2,1)S(1)}, u32[]{:S(2)}, u32[]{:S(2)}) %collective-permute-start.18) | collective-permute-done | bytes 40992 | tf_op jit(solution)/shard_map/ppermute | solution.py:242
  76.5 0.8 pad_maximum_fusion
  77.5 3.5 %shard_map.122 = f32[512,640]{1,0:T(8,128)S(1)} custom-call(bf16[192,5760]{1,0:T(8,128)(2,1)S(1)} %get-tuple-element.79.refs_0_, bf16[128,5760]{1,0:T(8,128)(2,1)S(1)} %get-tuple-element.80.refs_1_, bf16[3,576,192]{2,1,0:T(8,128)(2,1)S(1)} %slice_bitcast_fusion.refs_2_, bf16[3,576,128]{2,1,0:T(8,128)(2,1)S(1)} %slice_bitcast_fusion.2.refs_3_), custom_call_target="tpu_custom_call" | custom-call | flops 20000000000 | bytes 1048576 | tf_op jit(solution)/shard_map/pallas_call | solution.py:205
  81.1 3.3 %collective-permute-done.17 = bf16[2,64,2944]{2,1,0:T(8,128)(2,1)S(1)} collective-permute-done((bf16[2,64,2944]{2,1,0:T(8,128)(2,1)S(1)}, bf16[2,64,2944]{2,1,0:T(8,128)(2,1)S(1)}, u32[]{:S(2)}, u32[]{:S(2)}) %collective-permute-start.17) | collective-permute-done | bytes 753696 | tf_op jit(solution)/shard_map/ppermute | solution.py:313
  85.1 3.0 %collective-permute-start.20 = (bf16[2,24,2944]{2,1,0:T(8,128)(2,1)S(1)}, bf16[2,24,2944]{2,1,0:T(8,128)(2,1)S(1)}, u32[]{:S(2)}, u32[]{:S(2)}) collective-permute-start(bf16[2,24,2944]{2,1,0:T(8,128)(2,1)S(1)} %maximum_select_fusion), channel_id=1, source_target_pairs={{0,8},{1,9},{2,10},{3,11},{4,12},{5,13},{6,14},{7,15},{8,0},{9,1},... | collective-permute-start | bytes 847880 | tf_op jit(solution)/shard_map/ppermute | solution.py:313
  88.2 1.5 %collective-permute-start.22 = (bf16[64,2944]{1,0:T(8,128)(2,1)S(1)}, bf16[64,2944]{1,0:T(8,128)(2,1)S(1)}, u32[]{:S(2)}, u32[]{:S(2)}) collective-permute-start(bf16[64,2944]{1,0:T(8,128)(2,1)S(1)} %fusion.10), channel_id=1, source_target_pairs={{0,1},{1,0},{2,6},{3,7},{4,5},{5,4},{6,2},{7,3},{8,9},{9,8},{10,14... | collective-permute-start | bytes 1130504 | tf_op jit(solution)/shard_map/ppermute | solution.py:313
  89.7 3.5 %shard_map.123 = f32[512,640]{1,0:T(8,128)S(1)} custom-call(bf16[192,5760]{1,0:T(8,128)(2,1)S(1)} %get-tuple-element.79.refs_0_, bf16[128,5760]{1,0:T(8,128)(2,1)S(1)} %get-tuple-element.80.refs_1_, bf16[3,576,192]{2,1,0:T(8,128)(2,1)S(1)} %slice_bitcast_fusion.1.refs_2_, bf16[3,576,128]{2,1,0:T(8,128)(2,1)S(1)} %slice_bitcast_fusion.3.refs_3_), custom_call_target="tpu_custom_call" | custom-call | flops 20000000000 | bytes 1048576 | tf_op jit(solution)/shard_map/pallas_call | solution.py:205
  93.3 1.9 %collective-permute-done.20 = bf16[2,24,2944]{2,1,0:T(8,128)(2,1)S(1)} collective-permute-done((bf16[2,24,2944]{2,1,0:T(8,128)(2,1)S(1)}, bf16[2,24,2944]{2,1,0:T(8,128)(2,1)S(1)}, u32[]{:S(2)}, u32[]{:S(2)}) %collective-permute-start.20) | collective-permute-done | bytes 282656 | tf_op jit(solution)/shard_map/ppermute | solution.py:313
  95.2 1.1 collective-permute-start.21
  96.5 1.8 %collective-permute-start.23 = (bf16[2,16,2944]{2,1,0:T(8,128)(2,1)S(1)}, bf16[2,16,2944]{2,1,0:T(8,128)(2,1)S(1)}, u32[]{:S(2)}, u32[]{:S(2)}) collective-permute-start(bf16[2,16,2944]{2,1,0:T(8,128)(2,1)S(1)} %maximum_select_fusion.1), channel_id=1, source_target_pairs={{0,8},{1,9},{2,10},{3,11},{4,12},{5,13},{6,14},{7,15},{8,0},{9,1},... | collective-permute-start | bytes 565256 | tf_op jit(solution)/shard_map/ppermute | solution.py:313
  98.4 1.6 %convolution_convert_fusion = bf16[512,640]{1,0:T(8,128)(2,1)} fusion(bf16[320,512]{1,0:T(8,128)(2,1)S(1)} %collective-permute-done.19, bf16[320,512]{1,0:T(8,128)(2,1)S(1)} %slice.203, pred[320,640]{1,0:T(32,128)(4,1)S(1)} %get-tuple-element.135, pred[320,640]{1,0:T(32,128)(4,1)S(1)} %get-tuple-element.136), kind=kOutput, calls=%fused_computation.8 | convolution fusion | flops 421478400 | bytes 1720320 | tf_op jit(solution)/shard_map/dot_general | solution.py:22
  100.1 5.0 %collective-permute-done.23 = bf16[2,16,2944]{2,1,0:T(8,128)(2,1)S(1)} collective-permute-done((bf16[2,16,2944]{2,1,0:T(8,128)(2,1)S(1)}, bf16[2,16,2944]{2,1,0:T(8,128)(2,1)S(1)}, u32[]{:S(2)}, u32[]{:S(2)}) %collective-permute-start.23) | collective-permute-done | bytes 188448 | tf_op jit(solution)/shard_map/ppermute | solution.py:313
  105.1 2.0 %collective-permute-start.24 = (bf16[16,2944]{1,0:T(8,128)(2,1)S(1)}, bf16[16,2944]{1,0:T(8,128)(2,1)S(1)}, u32[]{:S(2)}, u32[]{:S(2)}) collective-permute-start(bf16[16,2944]{1,0:T(8,128)(2,1)S(1)} %fusion.11), channel_id=1, source_target_pairs={{0,16},{1,17},{2,18},{3,19},{4,20},{5,21},{6,22},{7,23},{8,24},{9,... | collective-permute-start | bytes 282632 | tf_op jit(solution)/shard_map/ppermute | solution.py:313
  107.1 1.0 add_convert_fusion
  108.1 3.5 %collective-permute-done.24.refs_5_ = bf16[16,2944]{1,0:T(8,128)(2,1)S(1)} collective-permute-done((bf16[16,2944]{1,0:T(8,128)(2,1)S(1)}, bf16[16,2944]{1,0:T(8,128)(2,1)S(1)}, u32[]{:S(2)}, u32[]{:S(2)}) %collective-permute-start.24) | collective-permute-done | bytes 94240 | tf_op jit(solution)/shard_map/ppermute | solution.py:313
  111.6 2.2 %shard_map.124 = (f32[9,40,320]{2,1,0:T(8,128)}, f32[9,40,320]{2,1,0:T(8,128)}, f32[9,40,320]{2,1,0:T(8,128)}) custom-call(s32[2]{0:T(128)S(1)} %pad_add_fusion.3.place_ref, f32[9,40,320]{2,1,0:T(8,128)S(1)} %bitcast.79, f32[9,40,320]{2,1,0:T(8,128)S(1)} %bitcast.81, f32[9,40,320]{2,1,0:T(8,128)S(1)} %bitcast.82, ...), custom_call_target="tpu_custom_call" | custom-call | bytes 1048576 | tf_op jit(solution)/shard_map/pallas_call | solution.py:205
  (84 shorter events, 5.6 us)
Async XLA Ops:
  0.6 11.5 %copy-start = (bf16[1,16,32,640]{3,2,1,0:T(8,128)(2,1)S(1)}, bf16[1,16,32,640]{3,2,1,0:T(8,128)(2,1)}, u32[]{:S(2)}) copy-start(bf16[1,16,32,640]{3,2,1,0:T(8,128)(2,1)} %param.9) | copy-start | bytes 1966084
  0.7 1.1 copy-start.1
  2.6 17.5 %collective-permute-start = (bf16[32,2944]{1,0:T(8,128)(2,1)S(1)}, bf16[32,2944]{1,0:T(8,128)(2,1)S(1)}, u32[]{:S(2)}, u32[]{:S(2)}) collective-permute-start(bf16[32,2944]{1,0:T(8,128)(2,1)S(1)} %slice.159), channel_id=1, source_target_pairs={{0,8},{1,9},{2,10},{3,11},{4,12},{5,13},{6,14},{7,15},{8,16},{9,17... | collective-permute-start | bytes 565256 | tf_op jit(solution)/shard_map/ppermute | solution.py:313
  5.6 14.9 %collective-permute-start.1 = (bf16[32,2944]{1,0:T(8,128)(2,1)S(1)}, bf16[32,2944]{1,0:T(8,128)(2,1)S(1)}, u32[]{:S(2)}, u32[]{:S(2)}) collective-permute-start(bf16[32,2944]{1,0:T(8,128)(2,1)S(1)} %slice.159), channel_id=1, source_target_pairs={{0,16},{1,17},{2,18},{3,19},{4,20},{5,21},{6,22},{7,23},{8,24},{9,... | collective-permute-start | bytes 565256 | tf_op jit(solution)/shard_map/ppermute | solution.py:313
  8.2 12.3 %collective-permute-start.2 = (bf16[32,2944]{1,0:T(8,128)(2,1)S(1)}, bf16[32,2944]{1,0:T(8,128)(2,1)}, u32[]{:S(2)}, u32[]{:S(2)}) collective-permute-start(bf16[32,2944]{1,0:T(8,128)(2,1)S(1)} %slice.159), channel_id=1, source_target_pairs={{0,24},{1,25},{2,26},{3,27},{4,28},{5,29},{6,30},{7,31},{8,0},{9,1... | collective-permute-start | bytes 565256 | tf_op jit(solution)/shard_map/ppermute | solution.py:313
  9.6 4.1 %collective-permute-start.3 = (bf16[8,2944]{1,0:T(8,128)(2,1)S(1)}, bf16[8,2944]{1,0:T(8,128)(2,1)S(1)}, u32[]{:S(2)}, u32[]{:S(2)}) collective-permute-start(bf16[8,2944]{1,0:T(8,128)(2,1)S(1)} %get-tuple-element.122), channel_id=1, source_target_pairs={{0,1},{1,0},{2,6},{3,7},{4,5},{5,4},{6,2},{7,3},{8,9},{9,8},{10,14... | collective-permute-start | bytes 141320 | tf_op jit(solution)/shard_map/ppermute | solution.py:313
  12.2 1.6 %copy-start.5 = (bf16[1,16,32,640]{3,2,1,0:T(8,128)(2,1)S(1)}, bf16[1,16,32,640]{3,2,1,0:T(8,128)(2,1)}, u32[]{:S(2)}) copy-start(bf16[1,16,32,640]{3,2,1,0:T(8,128)(2,1)} %param.8) | copy-start | bytes 1966084
  13.8 4.1 %collective-permute-start.5 = (bf16[1,1,32,640]{3,2,1,0:T(8,128)(2,1)S(1)}, bf16[1,1,32,640]{3,2,1,0:T(8,128)(2,1)S(1)}, u32[]{:S(2)}, u32[]{:S(2)}) collective-permute-start(bf16[1,1,32,640]{3,2,1,0:T(8,128)(2,1)S(1)} %slice_select_fusion.1), channel_id=1, source_target_pairs={{0,1},{1,0},{2,3},{3,2},{4,5},{5,4},{6,7},{7,6},{8,9},{9,8},{10,11... | collective-permute-start | bytes 122888 | tf_op jit(solution)/shard_map/ppermute | solution.py:242
  15.4 4.6 %collective-permute-start.4 = (bf16[2,8,2944]{2,1,0:T(8,128)(2,1)S(1)}, bf16[2,8,2944]{2,1,0:T(8,128)(2,1)S(1)}, u32[]{:S(2)}, u32[]{:S(2)}) collective-permute-start(bf16[2,8,2944]{2,1,0:T(8,128)(2,1)S(1)} %pad_maximum_fusion.12), channel_id=1, source_target_pairs={{0,4},{1,5},{2,3},{3,2},{4,0},{5,1},{6,7},{7,6},{8,12},{9,13},{10,... | collective-permute-start | bytes 282632 | tf_op jit(solution)/shard_map/ppermute | solution.py:313
  21.6 9.9 %collective-permute-start.6 = (bf16[64,2944]{1,0:T(8,128)(2,1)S(1)}, bf16[64,2944]{1,0:T(8,128)(2,1)S(1)}, u32[]{:S(2)}, u32[]{:S(2)}) collective-permute-start(bf16[64,2944]{1,0:T(8,128)(2,1)S(1)} %get-tuple-element.118.own_ref), channel_id=1, source_target_pairs={{0,1},{1,0},{2,6},{3,7},{4,5},{5,4},{6,2},{7,3},{8,9},{9,8},{10,14... | collective-permute-start | bytes 1130504 | tf_op jit(solution)/shard_map/ppermute | solution.py:313
  23.2 2.0 %collective-permute-start.10 = (bf16[320,512]{1,0:T(8,128)(2,1)S(1)}, bf16[320,512]{1,0:T(8,128)(2,1)S(1)}, u32[]{:S(2)}, u32[]{:S(2)}) collective-permute-start(bf16[320,512]{1,0:T(8,128)(2,1)S(1)} %get-tuple-element.108), channel_id=1, source_target_pairs={{0,2},{1,3},{2,0},{3,1},{4,6},{5,7},{6,4},{7,5},{8,10},{9,11},{10,... | collective-permute-start | bytes 983048 | tf_op jit(solution)/shard_map/ppermute | solution.py:313
  23.4 11.6 %collective-permute-start.8 = (bf16[64,2944]{1,0:T(8,128)(2,1)S(1)}, bf16[64,2944]{1,0:T(8,128)(2,1)S(1)}, u32[]{:S(2)}, u32[]{:S(2)}) collective-permute-start(bf16[64,2944]{1,0:T(8,128)(2,1)S(1)} %get-tuple-element.116.own_ref), channel_id=1, source_target_pairs={{0,1},{1,0},{2,6},{3,7},{4,5},{5,4},{6,2},{7,3},{8,9},{9,8},{10,14... | collective-permute-start | bytes 1130504 | tf_op jit(solution)/shard_map/ppermute | solution.py:313
  24.6 12.0 %collective-permute-start.9 = (bf16[1,18,32,640]{3,2,1,0:T(8,128)(2,1)S(1)}, bf16[1,18,32,640]{3,2,1,0:T(8,128)(2,1)S(1)}, u32[]{:S(2)}, u32[]{:S(2)}) collective-permute-start(bf16[1,18,32,640]{3,2,1,0:T(8,128)(2,1)S(1)} %pad_maximum_fusion.6), channel_id=1, source_target_pairs={{0,2},{1,3},{2,0},{3,1},{4,6},{5,7},{6,4},{7,5},{8,10},{9,11},{10,... | collective-permute-start | bytes 2211848 | tf_op jit(solution)/shard_map/ppermute | solution.py:313
  25.2 13.7 %collective-permute-start.11 = (bf16[2,2,8,2944]{3,2,1,0:T(8,128)(2,1)S(1)}, bf16[2,2,8,2944]{3,2,1,0:T(8,128)(2,1)S(1)}, u32[]{:S(2)}, u32[]{:S(2)}) collective-permute-start(bf16[2,2,8,2944]{3,2,1,0:T(8,128)(2,1)S(1)} %bitcast_select_fusion), channel_id=1, source_target_pairs={{0,8},{1,9},{2,10},{3,11},{4,12},{5,13},{6,14},{7,15},{8,16},{9,17... | collective-permute-start | bytes 565256 | tf_op jit(solution)/shard_map/ppermute | solution.py:313
  29.9 14.0 %collective-permute-start.12 = (bf16[2,2,8,2944]{3,2,1,0:T(8,128)(2,1)S(1)}, bf16[2,2,8,2944]{3,2,1,0:T(8,128)(2,1)S(1)}, u32[]{:S(2)}, u32[]{:S(2)}) collective-permute-start(bf16[2,2,8,2944]{3,2,1,0:T(8,128)(2,1)S(1)} %bitcast_select_fusion), channel_id=1, source_target_pairs={{0,16},{1,17},{2,18},{3,19},{4,20},{5,21},{6,22},{7,23},{8,24},{9,... | collective-permute-start | bytes 565256 | tf_op jit(solution)/shard_map/ppermute | solution.py:313
  31.5 12.4 %collective-permute-start.13 = (bf16[2,2,8,2944]{3,2,1,0:T(8,128)(2,1)S(1)}, bf16[2,2,8,2944]{3,2,1,0:T(8,128)(2,1)S(1)}, u32[]{:S(2)}, u32[]{:S(2)}) collective-permute-start(bf16[2,2,8,2944]{3,2,1,0:T(8,128)(2,1)S(1)} %bitcast_select_fusion), channel_id=1, source_target_pairs={{0,24},{1,25},{2,26},{3,27},{4,28},{5,29},{6,30},{7,31},{8,0},{9,1... | collective-permute-start | bytes 565256 | tf_op jit(solution)/shard_map/ppermute | solution.py:313
  35.0 11.7 %collective-permute-start.7 = (bf16[2,64,2944]{2,1,0:T(8,128)(2,1)S(1)}, bf16[2,64,2944]{2,1,0:T(8,128)(2,1)S(1)}, u32[]{:S(2)}, u32[]{:S(2)}) collective-permute-start(bf16[2,64,2944]{2,1,0:T(8,128)(2,1)S(1)} %pad_maximum_fusion.3), channel_id=1, source_target_pairs={{0,4},{1,5},{2,3},{3,2},{4,0},{5,1},{6,7},{7,6},{8,12},{9,13},{10,... | collective-permute-start | bytes 2261000 | tf_op jit(solution)/shard_map/ppermute | solution.py:313
  36.6 19.5 %collective-permute-start.15 = (bf16[2,64,2944]{2,1,0:T(8,128)(2,1)S(1)}, bf16[2,64,2944]{2,1,0:T(8,128)(2,1)S(1)}, u32[]{:S(2)}, u32[]{:S(2)}) collective-permute-start(bf16[2,64,2944]{2,1,0:T(8,128)(2,1)S(1)} %pad_maximum_fusion.5), channel_id=1, source_target_pairs={{0,4},{1,5},{2,3},{3,2},{4,0},{5,1},{6,7},{7,6},{8,12},{9,13},{10,... | collective-permute-start | bytes 2261000 | tf_op jit(solution)/shard_map/ppermute | solution.py:313
  54.5 15.7 %collective-permute-start.14 = (bf16[2,96,2944]{2,1,0:T(8,128)(2,1)S(1)}, bf16[2,96,2944]{2,1,0:T(8,128)(2,1)S(1)}, u32[]{:S(2)}, u32[]{:S(2)}) collective-permute-start(bf16[2,96,2944]{2,1,0:T(8,128)(2,1)S(1)} %get-tuple-element.74), channel_id=1, source_target_pairs={{0,4},{1,5},{2,3},{3,2},{4,0},{5,1},{6,7},{7,6},{8,12},{9,13},{10,... | collective-permute-start | bytes 3391496 | tf_op jit(solution)/shard_map/ppermute | solution.py:313
  62.7 21.7 %collective-permute-start.17 = (bf16[2,64,2944]{2,1,0:T(8,128)(2,1)S(1)}, bf16[2,64,2944]{2,1,0:T(8,128)(2,1)S(1)}, u32[]{:S(2)}, u32[]{:S(2)}) collective-permute-start(bf16[2,64,2944]{2,1,0:T(8,128)(2,1)S(1)} %get-tuple-element.76), channel_id=1, source_target_pairs={{0,4},{1,5},{2,3},{3,2},{4,0},{5,1},{6,7},{7,6},{8,12},{9,13},{10,... | collective-permute-start | bytes 2261000 | tf_op jit(solution)/shard_map/ppermute | solution.py:313
  63.4 17.7 %collective-permute-start.19 = (bf16[320,512]{1,0:T(8,128)(2,1)S(1)}, bf16[320,512]{1,0:T(8,128)(2,1)S(1)}, u32[]{:S(2)}, u32[]{:S(2)}) collective-permute-start(bf16[320,512]{1,0:T(8,128)(2,1)S(1)} %slice.216), channel_id=1, source_target_pairs={{0,2},{1,3},{2,0},{3,1},{4,6},{5,7},{6,4},{7,5},{8,10},{9,11},{10,... | collective-permute-start | bytes 983048 | tf_op jit(solution)/shard_map/ppermute | solution.py:313
  70.6 4.7 %collective-permute-start.18 = (bf16[2,1,32,320]{3,2,1,0:T(8,128)(2,1)S(1)}, bf16[2,1,32,320]{3,2,1,0:T(8,128)(2,1)S(1)}, u32[]{:S(2)}, u32[]{:S(2)}) collective-permute-start(bf16[2,1,32,320]{3,2,1,0:T(8,128)(2,1)S(1)} %slice_select_fusion), channel_id=1, source_target_pairs={{0,1},{1,0},{2,3},{3,2},{4,5},{5,4},{6,7},{7,6},{8,9},{9,8},{10,11... | collective-permute-start | bytes 122888 | tf_op jit(solution)/shard_map/ppermute | solution.py:242
  72.4 12.0 %collective-permute-start.16 = (bf16[96,2944]{1,0:T(8,128)(2,1)S(1)}, bf16[96,2944]{1,0:T(8,128)(2,1)S(1)}, u32[]{:S(2)}, u32[]{:S(2)}) collective-permute-start(bf16[96,2944]{1,0:T(8,128)(2,1)S(1)} %fusion.9), channel_id=1, source_target_pairs={{0,1},{1,0},{2,6},{3,7},{4,5},{5,4},{6,2},{7,3},{8,9},{9,8},{10,14... | collective-permute-start | bytes 1695752 | tf_op jit(solution)/shard_map/ppermute | solution.py:313
  85.1 10.1 %collective-permute-start.20 = (bf16[2,24,2944]{2,1,0:T(8,128)(2,1)S(1)}, bf16[2,24,2944]{2,1,0:T(8,128)(2,1)S(1)}, u32[]{:S(2)}, u32[]{:S(2)}) collective-permute-start(bf16[2,24,2944]{2,1,0:T(8,128)(2,1)S(1)} %maximum_select_fusion), channel_id=1, source_target_pairs={{0,8},{1,9},{2,10},{3,11},{4,12},{5,13},{6,14},{7,15},{8,0},{9,1},... | collective-permute-start | bytes 847880 | tf_op jit(solution)/shard_map/ppermute | solution.py:313
  88.2 8.1 %collective-permute-start.22 = (bf16[64,2944]{1,0:T(8,128)(2,1)S(1)}, bf16[64,2944]{1,0:T(8,128)(2,1)S(1)}, u32[]{:S(2)}, u32[]{:S(2)}) collective-permute-start(bf16[64,2944]{1,0:T(8,128)(2,1)S(1)} %fusion.10), channel_id=1, source_target_pairs={{0,1},{1,0},{2,6},{3,7},{4,5},{5,4},{6,2},{7,3},{8,9},{9,8},{10,14... | collective-permute-start | bytes 1130504 | tf_op jit(solution)/shard_map/ppermute | solution.py:313
  95.2 12.9 %collective-permute-start.21 = (bf16[24,2944]{1,0:T(8,128)(2,1)S(1)}, bf16[24,2944]{1,0:T(8,128)(2,1)S(1)}, u32[]{:S(2)}, u32[]{:S(2)}) collective-permute-start(bf16[24,2944]{1,0:T(8,128)(2,1)S(1)} %fusion.12), channel_id=1, source_target_pairs={{0,16},{1,17},{2,18},{3,19},{4,20},{5,21},{6,22},{7,23},{8,24},{9,... | collective-permute-start | bytes 423944 | tf_op jit(solution)/shard_map/ppermute | solution.py:313
  96.5 8.5 %collective-permute-start.23 = (bf16[2,16,2944]{2,1,0:T(8,128)(2,1)S(1)}, bf16[2,16,2944]{2,1,0:T(8,128)(2,1)S(1)}, u32[]{:S(2)}, u32[]{:S(2)}) collective-permute-start(bf16[2,16,2944]{2,1,0:T(8,128)(2,1)S(1)} %maximum_select_fusion.1), channel_id=1, source_target_pairs={{0,8},{1,9},{2,10},{3,11},{4,12},{5,13},{6,14},{7,15},{8,0},{9,1},... | collective-permute-start | bytes 565256 | tf_op jit(solution)/shard_map/ppermute | solution.py:313
  98.4 8.7 %collective-permute-start.25 = (f32[512,640]{1,0:T(8,128)S(1)}, f32[512,640]{1,0:T(8,128)S(1)}, u32[]{:S(2)}, u32[]{:S(2)}) collective-permute-start(f32[512,640]{1,0:T(8,128)S(1)} %shard_map.122), channel_id=1, source_target_pairs={{0,2},{1,3},{2,0},{3,1},{4,6},{5,7},{6,4},{7,5},{8,10},{9,11},{10,... | collective-permute-start | bytes 3932168 | tf_op jit(solution)/shard_map/ppermute | solution.py:313
  105.1 6.5 %collective-permute-start.24 = (bf16[16,2944]{1,0:T(8,128)(2,1)S(1)}, bf16[16,2944]{1,0:T(8,128)(2,1)S(1)}, u32[]{:S(2)}, u32[]{:S(2)}) collective-permute-start(bf16[16,2944]{1,0:T(8,128)(2,1)S(1)} %fusion.11), channel_id=1, source_target_pairs={{0,16},{1,17},{2,18},{3,19},{4,20},{5,21},{6,22},{7,23},{8,24},{9,... | collective-permute-start | bytes 282632 | tf_op jit(solution)/shard_map/ppermute | solution.py:313
  107.1 4.5 %copy-start.2 = (f32[9,320,40]{1,2,0:T(8,128)S(1)}, f32[9,320,40]{1,2,0:T(8,128)}, u32[]{:S(2)}) copy-start(f32[9,320,40]{1,2,0:T(8,128)} %param.10) | copy-start | bytes 1382404
  107.1 4.5 %copy-start.3 = (f32[9,320,40]{1,2,0:T(8,128)S(1)}, f32[9,320,40]{1,2,0:T(8,128)}, u32[]{:S(2)}) copy-start(f32[9,320,40]{1,2,0:T(8,128)} %param.11) | copy-start | bytes 1382404
  107.1 4.5 %copy-start.4 = (f32[9,320,40]{1,2,0:T(8,128)S(1)}, f32[9,320,40]{1,2,0:T(8,128)}, u32[]{:S(2)}) copy-start(f32[9,320,40]{1,2,0:T(8,128)} %param.12) | copy-start | bytes 1382404

commit v5 on v4

--- a/solution.py
+++ b/solution.py
@@ -69,10 +69,12 @@
 
 def routed_kernel(width, extra, place_ref, own_ref, near_ref, far_ref, x_ref, t_ref, *refs):
     a_refs, refs = refs[:extra], refs[extra:]
-    k_ref, s_ref, e_ref, keep_ref, send_ref, mid_ref, flat_ref = refs
+    (k_ref, s_ref, e_ref, keep_ref, send_ref), refs = refs[:5], refs[5:]
+    g_refs, (mid_ref, flat_ref) = refs[:extra], refs[extra:]
     first, on_core0 = place_ref[0] == 0, place_ref[1] == 0
     rows = k_ref.shape[0]
-    near_y, far_y = slice(0, rows // 2), slice(rows // 2, rows)
+    skip = sum(a_ref.shape[1] for a_ref in a_refs) // 2
+    near_y, far_y = slice(skip, rows // 2), slice(rows // 2 + skip, rows)
     low = lax.broadcasted_iota(jnp.int32, (rows, 128), 1) < 64
     spare = TAPS * 256
 
@@ -81,9 +83,8 @@
         own = [own_ref[:, at], jnp.where(on_core0, far, near)]
         other = [jnp.where(on_core0, near, far), far_ref[1, :, at]]
         for a_ref in a_refs:
-            half = a_ref.shape[1] // 2
-            own = [a_ref[0, :half, at], own[0], a_ref[0, half:, at], own[1]]
-            other = [a_ref[1, :half, at], other[0], a_ref[1, half:, at], other[1]]
+            own = [a_ref[0, :skip, at], own[0], a_ref[0, skip:, at], own[1]]
+            other = [a_ref[1, :skip, at], other[0], a_ref[1, skip:, at], other[1]]
         own, other = jnp.concatenate(own), jnp.concatenate(other)
         return jnp.where(first, own, other), jnp.where(first, other, own)
 
@@ -106,6 +107,10 @@
     def put(at, left, right):
         left, right = left.astype(BF), right.astype(BF)
         own, other = jnp.where(first, left, right), jnp.where(first, right, left)
+        for g_ref in g_refs:
+            for i, rows_of in enumerate((own, other)):
+                g_ref[i, 0, :, at] = rows_of[: near_y.start]
+                g_ref[i, 1, :, at] = rows_of[near_y.stop : far_y.start]
         own_far, other_near = own[far_y], other[near_y]
         keep_ref[0, :, at] = own[near_y]
         send_ref[1, :, at] = other[far_y]
@@ -152,18 +157,15 @@
         out_ref[:, at : at + 128] = jnp.where(low, spare[2 * pair], spare[2 * pair + 1]).astype(BF)
 
 
-def adam_kernel(scale, place_ref, w_ref, m1_ref, m2_ref, *refs):
-    parts, outs = refs[:-3], refs[-3:]
+def adam_kernel(scale, rows, extra, place_ref, w_ref, m1_ref, m2_ref, *refs):
+    parts, extras, outs = refs[:3], refs[3 : 3 + extra], refs[-3:]
     first = place_ref[0] == 0
-    low = lax.broadcasted_iota(jnp.int32, (w_ref.shape[1], 128), 1) < 64
+    low = lax.broadcasted_iota(jnp.int32, (rows.stop - rows.start, 128), 1) < 64
     swap = lambda v: pltpu.roll(v, 64, 1)
 
     def grad(at):
-        sums = []
-        for i in range(0, len(parts), 3):
-            p0, p1, p2 = [ref[:, at].astype(F32) for ref in parts[i : i + 3]]
-            sums.append((p0 + p1) + p2)
-        return jnp.concatenate(sums) * scale
+        p0, p1, p2 = [ref[:, at].astype(F32) for ref in parts]
+        return jnp.concatenate([(p0 + p1) + p2] + [ref[:, at] for ref in extras]) * scale
 
     for tap in range(TAPS):
         if tap % 2 == 0:
@@ -179,9 +181,9 @@
             jnp.where(first, at_low, right_swap)[:, :64],
         )
         for tile, at in zip(tiles, (slice(0, 128), slice(128, 256), slice(256, 320))):
-            new = adam(w_ref[tap, :, at], m1_ref[tap, :, at], m2_ref[tap, :, at], tile)
+            new = adam(w_ref[tap, rows, at], m1_ref[tap, rows, at], m2_ref[tap, rows, at], tile)
             for out_ref, value in zip(outs, new):
-                out_ref[tap, :, at] = value
+                out_ref[tap, rows, at] = value
 
 
 def back_kernel(width, parts, *refs):
@@ -341,13 +343,12 @@
 
     chunk_a, chunk_b = CHUNKS
     grids = []
-    for begin, counts in ((0, (ROUTE_A, chunk_a - ROUTE_A)), (chunk_a, (chunk_b,))):
+    cut = chunk_a - ROUTE_A
+    for spans in (((chunk_b + cut, ROUTE_A), (chunk_b, cut)), ((0, chunk_b),)):
         for dist_y in range(2):
-            at = begin
-            for count in counts:
+            for begin, count in spans:
                 dist_z, within = np.indices((4, count)).reshape(2, -1)
-                grids.append(np.stack([np.full_like(dist_z, dist_y), dist_z, at + within]))
-                at += count
+                grids.append(np.stack([np.full_like(dist_z, dist_y), dist_z, begin + within]))
     dist_y, dist_z, within = np.concatenate(grids, axis=1).astype(np.int32)
     block = ((z - dist_z) % 4) * 4 + (y ^ dist_y) * 2
     everything = jnp.arange(channels, dtype=jnp.int32)
@@ -363,7 +364,7 @@
             total = total + term.astype(F32)
         return total
 
-    pa, pb = piece[:ROUTE_A], piece[ROUTE_A:]
+    pa, pb = piece[chunk_b + cut :], piece[: chunk_b + cut]
     bz = [along_z(pb, s) for s in (1, 2, 3)]
     pa = jnp.stack([pa, along_xy(pa)])
     t = mm(pick, target.reshape(cells, channels), NT).astype(BF)
@@ -371,15 +372,15 @@
     banded = with_halo(latents)
     pa = turned(jnp.stack([pa, along_yx(pa)]))
     bz, pa, banded, t = phase(bz, pa, banded, t)
-    t_in, banded_in = along_core(t[rows:]), along_core(banded)
+    t_in = along_core(t[rows:])
     t = jnp.concatenate([t[:rows], t_in], axis=1)
     pa, t_in = phase(pa, t_in)
-    cut = chunk_a - ROUTE_A
-    own_a = jnp.concatenate([v[:cut] for v in [pb] + bz])
-    own_b = jnp.concatenate([v[cut:] for v in [pb] + bz])
+    own_a = jnp.concatenate([v[chunk_b:] for v in [pb] + bz])
+    own_b = jnp.concatenate([v[:chunk_b] for v in [pb] + bz])
     near_a, near_b = along_xy(own_a), along_xy(own_b)
     az = [along_z(pa, s) for s in (1, 2, 3)]
-    x = wide_cells(jnp.concatenate([banded, banded_in]))
+    near_a, banded = phase(near_a, banded)
+    x = wide_cells(jnp.concatenate([banded, along_core(banded)]))
     far_a = along_yx(jnp.stack([own_a, near_a]))
     far_b = along_yx(jnp.stack([own_b, near_b]))
     far_a, near_b, x, t, az = phase(far_a, near_b, x, t, az)
@@ -390,7 +391,8 @@
         return vmem_call(
             functools.partial(routed_kernel, width, len(extra)),
             (shape(n, TAPS * channels), shape(n, 2 * cells), shape(2 * cells, n))
-            + (shape(2, n // 2, lanes),) * 2,
+            + (shape(2, own.shape[0], lanes),) * 2
+            + tuple(shape(2, 2, v.shape[1] // 2, lanes) for v in extra),
             1,
             place,
             own,
@@ -403,11 +405,21 @@
             flops=30 * 10**9,
         )
 
-    kernel_a, student_a, error_a, keep_a, send_a = compute(own_a, near_a, far_a, t[:rows_a], by_a)
+    kernel_a, student_a, error_a, keep_a, send_a, ga = compute(
+        own_a, near_a, far_a, t[:rows_a], by_a
+    )
     got_a = along_yx(send_a)
+    even = z % 2 == 0
+
+    def to_pair(g):
+        return along_pair(jnp.where(even, jnp.stack([g[3], g[1]]), jnp.stack([g[1], g[3]])))
+
+    ga = ga.reshape(2, 2, 4, ROUTE_A, lanes).transpose(2, 0, 1, 3, 4)
+    pair_ga = to_pair(ga)
     kernel_b, student_b, error_b, keep_b, send_b = compute(own_b, near_b, far_b, t[rows_a:])
     got_b = along_yx(send_b)
-    got_a, send_b, error_b = phase(got_a, send_b, error_b)
+    got_a, send_b, error_b, pair_ga = phase(got_a, send_b, error_b, pair_ga)
+    last_ga = along_z(plus(ga[2], pair_ga[1]).astype(BF), 2)
     error = jnp.concatenate([error_a, error_b], axis=1)
     shifted = back_cells(with_halo(error.reshape(2, band, width, rows)))
 
@@ -427,48 +439,62 @@
     back_other = back(1)
     student = jnp.concatenate([student_a, student_b])
     student_in = along_core(student[:, cells:])
-    got2_a, got_b, back_other, shifted, student_in = phase(
-        got2_a, got_b, back_other, shifted, student_in
-    )
-    even = z % 2 == 0
-
-    def outward(keep, got, got2, *counts):
-        g = plus(keep[0], got[0], got2).astype(BF)
-        cuts = np.cumsum([4 * count for count in counts])[:-1]
-        g = [v.reshape(4, -1, lanes) for v in jnp.split(g, cuts)]
-        g = jnp.concatenate(g, axis=1)
-        send = jnp.where(even, jnp.stack([g[3], g[1]]), jnp.stack([g[1], g[3]]))
-        return g, along_pair(send)
-
-    g_a, pair_a = outward(keep_a, got_a, got2_a, ROUTE_A, cut)
+    got2_a, got_b, back_other, shifted, student_in, last_ga = phase(
+        got2_a, got_b, back_other, shifted, student_in, last_ga
+    )
+
+    def second_sum(keep, got, got2):
+        return plus(keep[0], got[0], got2).astype(BF).reshape(4, -1, lanes)
+
+    g_a = second_sum(keep_a, got_a, got2_a)
+    pair_a = to_pair(g_a)
     got2_b = along_xy(plus(keep_b[1], got_b[1]).astype(BF))
+    ga = turned(plus(ga[0], pair_ga[0], last_ga))
+    ga = plus(ga[0], along_yx(ga[1].astype(BF)))
     back_own = back(0)
-    got2_b, student, student_in, back_own, back_other = phase(
-        got2_b, student, student_in, back_own, back_other
-    )
-    g_b, pair_b = outward(keep_b, got_b, got2_b, chunk_b)
+    got2_b, student, student_in, back_own, back_other, ga = phase(
+        got2_b, student, student_in, back_own, back_other, ga
+    )
+    g_b = second_sum(keep_b, got_b, got2_b)
+    pair_b = to_pair(g_b)
     last_a = along_z(plus(g_a[2], pair_a[1]).astype(BF), 2)
     last_b = along_z(plus(g_b[2], pair_b[1]).astype(BF), 2)
+    ga = plus(ga[0], along_xy(ga[1].astype(BF)))
     back_in = along_core(back_other)
     both = jnp.concatenate([student[:, :cells], student_in])
     out = mm(both, pick, (((0,), (0,)), ((), ()))).astype(BF).reshape(latents.shape)
     input_grad = (back_own + back_in).astype(BF).reshape(latents.shape)
-    last_a, last_b, out, input_grad = phase(last_a, last_b, out, input_grad)
+    last_a, ga, out, input_grad = phase(last_a, ga, out, input_grad)
+
+    scale = 1.0 / (b * lax.axis_size("dp"))
+    states = [by_tap(v) for v in (weight, moment1, moment2)]
+    whole = (shape(TAPS, per, weight.shape[1], dtype=F32),) * 3
     news = vmem_call(
-        functools.partial(adam_kernel, 1.0 / (b * lax.axis_size("dp"))),
-        (shape(TAPS, per, weight.shape[1], dtype=F32),) * 3,
+        functools.partial(adam_kernel, scale, slice(chunk_b, per), 1),
+        whole,
         1,
         place,
-        by_tap(weight),
-        by_tap(moment1),
-        by_tap(moment2),
+        *states,
         g_a[0],
         pair_a[0],
         last_a,
-        g_b[0],
-        pair_b[0],
-        last_b,
-    )
+        ga,
+    )
+    last_b, news = phase(last_b, news)
+    some = pl.BlockSpec((TAPS, chunk_b, weight.shape[1]), lambda i: (0, 0, 0))
+    full = pl.BlockSpec((chunk_b, lanes), lambda i: (0, 0))
+    news = pl.pallas_call(
+        functools.partial(adam_kernel, scale, slice(0, chunk_b), 0),
+        out_shape=whole,
+        grid=(1,),
+        in_specs=[pl.BlockSpec(memory_space=pltpu.SMEM)]
+        + [some] * 3
+        + [full] * 3
+        + [pl.BlockSpec(memory_space=pl.ANY)] * 3,
+        out_specs=(some,) * 3,
+        input_output_aliases={7: 0, 8: 1, 9: 2},
+        compiler_params=pltpu.CompilerParams(vmem_limit_bytes=VMEM_LIMIT),
+    )(place, *states, g_b[0], pair_b[0], last_b, *news)
     return (out, input_grad, *map(by_tap, news))
 
 

time: 114 us -> 112 us (0.982)
  waiting for transfers between devices: 34.9 us -> 28.9 us
  starting transfers between devices: 40.7 us -> 42.9 us
  Pallas kernels: 24.2 us -> 25.6 us
    ppermute x24 -> x28, waiting for transfers between devices: 31.5 us -> 19.4 us  [hop(): return lambda v: lax.ppermute(v, ('dp', 'rows'), pairs)]
    ppermute x2, waiting for transfers between devices: 3.34 us -> 9.47 us  [with_halo(): got = lax.ppermute(edge, 'rows', [(0, 1), (1, 0)])]
    ppermute x24 -> x28, starting transfers between devices: 37.4 us -> 40.7 us  [hop(): return lambda v: lax.ppermute(v, ('dp', 'rows'), pairs)]
    pallas_call x0 -> x1, Pallas kernels: none -> 1.61 us  [routed_device(): pl.pallas_call(functools.partial(adam_kernel, scale, slice(0, chunk_b), 0...]
  transfers between devices with their start and end apart: 26 -> 30, of which waited for: 12 -> 13; matrix products, arithmetic and copies ran while one was open for 9% -> 9% of each run, Pallas kernels for 19% -> 21%
where the time goes in v5:
time: 112 us
  starting transfers between devices  42.9 us (38%)
  waiting for transfers between devices  28.9 us (26%)
  Pallas kernels  25.6 us (23%)
  other arithmetic  5.66 us (5%)
  local copies, waits for them, and re-layouts  5.53 us (5%)
  matrix products  2.35 us (2%)
  between operations  1.26 us (1%)
    ppermute x28, starting transfers between devices, hop(): return lambda v: lax.ppermute(v, ('dp', 'rows'), pairs)  40.7 us
    pallas_call x6, Pallas kernels, vmem_call(): pl.pallas_call(kernel, out_shape=outs, in_specs=[pl.BlockSpec(memory_spac...  24 us
    ppermute x28, waiting for transfers between devices, hop(): return lambda v: lax.ppermute(v, ('dp', 'rows'), pairs)  19.4 us
    ppermute x2, waiting for transfers between devices, with_halo(): got = lax.ppermute(edge, 'rows', [(0, 1), (1, 0)])  9.47 us
    dot_general x2, matrix products, mm(): return lax.dot_general(a, b, dims, preferred_element_type=F32)  2.35 us
  transfers between devices with their start and end apart: 30, of which 13 were waited for; matrix products, arithmetic and copies ran while one was open for 9% of the time, Pallas kernels for 21%

profile of v5, /device:TPU:0, one launch (start us, length us, event | category | flops | bytes accessed | tf_op | source)
XLA Modules:
  0.0 112.2 jit_solution(5868901565264775718)
XLA Ops:
  0.7 1.1 copy-done.1
  1.8 0.7 shard_map.119
  2.6 3.1 %collective-permute-start = (bf16[32,2944]{1,0:T(8,128)(2,1)S(1)}, bf16[32,2944]{1,0:T(8,128)(2,1)S(1)}, u32[]{:S(2)}, u32[]{:S(2)}) collective-permute-start(bf16[32,2944]{1,0:T(8,128)(2,1)S(1)} %slice.201), channel_id=1, source_target_pairs={{0,8},{1,9},{2,10},{3,11},{4,12},{5,13},{6,14},{7,15},{8,16},{9,17... | collective-permute-start | bytes 565256 | tf_op jit(solution)/shard_map/ppermute | solution.py:315
  5.6 2.6 %collective-permute-start.1 = (bf16[32,2944]{1,0:T(8,128)(2,1)S(1)}, bf16[32,2944]{1,0:T(8,128)(2,1)S(1)}, u32[]{:S(2)}, u32[]{:S(2)}) collective-permute-start(bf16[32,2944]{1,0:T(8,128)(2,1)S(1)} %slice.201), channel_id=1, source_target_pairs={{0,16},{1,17},{2,18},{3,19},{4,20},{5,21},{6,22},{7,23},{8,24},{9,... | collective-permute-start | bytes 565256 | tf_op jit(solution)/shard_map/ppermute | solution.py:315
  8.2 1.3 %collective-permute-start.2 = (bf16[32,2944]{1,0:T(8,128)(2,1)S(1)}, bf16[32,2944]{1,0:T(8,128)(2,1)}, u32[]{:S(2)}, u32[]{:S(2)}) collective-permute-start(bf16[32,2944]{1,0:T(8,128)(2,1)S(1)} %slice.201), channel_id=1, source_target_pairs={{0,24},{1,25},{2,26},{3,27},{4,28},{5,29},{6,30},{7,31},{8,0},{9,1... | collective-permute-start | bytes 565256 | tf_op jit(solution)/shard_map/ppermute | solution.py:315
  9.6 1.6 %collective-permute-start.3 = (bf16[8,2944]{1,0:T(8,128)(2,1)S(1)}, bf16[8,2944]{1,0:T(8,128)(2,1)S(1)}, u32[]{:S(2)}, u32[]{:S(2)}) collective-permute-start(bf16[8,2944]{1,0:T(8,128)(2,1)S(1)} %get-tuple-element.150), channel_id=1, source_target_pairs={{0,1},{1,0},{2,6},{3,7},{4,5},{5,4},{6,2},{7,3},{8,9},{9,8},{10,14... | collective-permute-start | bytes 141320 | tf_op jit(solution)/shard_map/ppermute | solution.py:315
  11.1 0.7 multiply_add_fusion.1
  12.2 0.7 convolution_convert_fusion.1
  12.9 0.8 collective-permute-done.3
  13.8 1.6 %collective-permute-start.5 = (bf16[1,1,32,640]{3,2,1,0:T(8,128)(2,1)S(1)}, bf16[1,1,32,640]{3,2,1,0:T(8,128)(2,1)S(1)}, u32[]{:S(2)}, u32[]{:S(2)}) collective-permute-start(bf16[1,1,32,640]{3,2,1,0:T(8,128)(2,1)S(1)} %slice_select_fusion.1), channel_id=1, source_target_pairs={{0,1},{1,0},{2,3},{3,2},{4,5},{5,4},{6,7},{7,6},{8,9},{9,8},{10,11... | collective-permute-start | bytes 122888 | tf_op jit(solution)/shard_map/ppermute | solution.py:244
  15.4 1.6 %collective-permute-start.4 = (bf16[2,8,2944]{2,1,0:T(8,128)(2,1)S(1)}, bf16[2,8,2944]{2,1,0:T(8,128)(2,1)S(1)}, u32[]{:S(2)}, u32[]{:S(2)}) collective-permute-start(bf16[2,8,2944]{2,1,0:T(8,128)(2,1)S(1)} %pad_maximum_fusion.11), channel_id=1, source_target_pairs={{0,4},{1,5},{2,3},{3,2},{4,0},{5,1},{6,7},{7,6},{8,12},{9,13},{10,... | collective-permute-start | bytes 282632 | tf_op jit(solution)/shard_map/ppermute | solution.py:315
  16.9 0.9 collective-permute-done.5
  18.0 2.0 %collective-permute-done.4 = bf16[2,8,2944]{2,1,0:T(8,128)(2,1)S(1)} collective-permute-done((bf16[2,8,2944]{2,1,0:T(8,128)(2,1)S(1)}, bf16[2,8,2944]{2,1,0:T(8,128)(2,1)S(1)}, u32[]{:S(2)}, u32[]{:S(2)}) %collective-permute-start.4) | collective-permute-done | bytes 94240 | tf_op jit(solution)/shard_map/ppermute | solution.py:315
  20.6 1.0 fusion.35
  21.6 1.5 %collective-permute-start.6 = (bf16[64,2944]{1,0:T(8,128)(2,1)S(1)}, bf16[64,2944]{1,0:T(8,128)(2,1)S(1)}, u32[]{:S(2)}, u32[]{:S(2)}) collective-permute-start(bf16[64,2944]{1,0:T(8,128)(2,1)S(1)} %get-tuple-element.146.own_ref), channel_id=1, source_target_pairs={{0,1},{1,0},{2,6},{3,7},{4,5},{5,4},{6,2},{7,3},{8,9},{9,8},{10,14... | collective-permute-start | bytes 1130504 | tf_op jit(solution)/shard_map/ppermute | solution.py:315
  23.4 1.2 %collective-permute-start.8 = (bf16[64,2944]{1,0:T(8,128)(2,1)S(1)}, bf16[64,2944]{1,0:T(8,128)(2,1)S(1)}, u32[]{:S(2)}, u32[]{:S(2)}) collective-permute-start(bf16[64,2944]{1,0:T(8,128)(2,1)S(1)} %get-tuple-element.144.own_ref), channel_id=1, source_target_pairs={{0,1},{1,0},{2,6},{3,7},{4,5},{5,4},{6,2},{7,3},{8,9},{9,8},{10,14... | collective-permute-start | bytes 1130504 | tf_op jit(solution)/shard_map/ppermute | solution.py:315
  24.9 4.6 %collective-permute-start.11 = (bf16[2,2,8,2944]{3,2,1,0:T(8,128)(2,1)S(1)}, bf16[2,2,8,2944]{3,2,1,0:T(8,128)(2,1)S(1)}, u32[]{:S(2)}, u32[]{:S(2)}) collective-permute-start(bf16[2,2,8,2944]{3,2,1,0:T(8,128)(2,1)S(1)} %copy_select_fusion.1), channel_id=1, source_target_pairs={{0,8},{1,9},{2,10},{3,11},{4,12},{5,13},{6,14},{7,15},{8,16},{9,17... | collective-permute-start | bytes 565256 | tf_op jit(solution)/shard_map/ppermute | solution.py:315
  29.5 1.5 %collective-permute-start.12 = (bf16[2,2,8,2944]{3,2,1,0:T(8,128)(2,1)S(1)}, bf16[2,2,8,2944]{3,2,1,0:T(8,128)(2,1)S(1)}, u32[]{:S(2)}, u32[]{:S(2)}) collective-permute-start(bf16[2,2,8,2944]{3,2,1,0:T(8,128)(2,1)S(1)} %copy_select_fusion.1), channel_id=1, source_target_pairs={{0,16},{1,17},{2,18},{3,19},{4,20},{5,21},{6,22},{7,23},{8,24},{9,... | collective-permute-start | bytes 565256 | tf_op jit(solution)/shard_map/ppermute | solution.py:315
  31.1 0.8 collective-permute-start.13
  32.2 1.1 collective-permute-done.8.near_ref
  33.3 1.5 %collective-permute-start.7 = (bf16[2,64,2944]{2,1,0:T(8,128)(2,1)S(1)}, bf16[2,64,2944]{2,1,0:T(8,128)(2,1)S(1)}, u32[]{:S(2)}, u32[]{:S(2)}) collective-permute-start(bf16[2,64,2944]{2,1,0:T(8,128)(2,1)S(1)} %pad_maximum_fusion.3), channel_id=1, source_target_pairs={{0,4},{1,5},{2,3},{3,2},{4,0},{5,1},{6,7},{7,6},{8,12},{9,13},{10,... | collective-permute-start | bytes 2261000 | tf_op jit(solution)/shard_map/ppermute | solution.py:315
  34.9 0.8 collective-permute-start.15
  35.9 0.8 fusion.27
  36.7 0.9 fusion.2
  37.6 6.3 %collective-permute-done.12 = bf16[2,2,8,2944]{3,2,1,0:T(8,128)(2,1)S(1)} collective-permute-done((bf16[2,2,8,2944]{3,2,1,0:T(8,128)(2,1)S(1)}, bf16[2,2,8,2944]{3,2,1,0:T(8,128)(2,1)S(1)}, u32[]{:S(2)}, u32[]{:S(2)}) %collective-permute-start.12) | collective-permute-done | bytes 188448 | tf_op jit(solution)/shard_map/ppermute | solution.py:315
  43.8 1.1 %collective-permute-done.7.far_ref = bf16[2,64,2944]{2,1,0:T(8,128)(2,1)S(1)} collective-permute-done((bf16[2,64,2944]{2,1,0:T(8,128)(2,1)S(1)}, bf16[2,64,2944]{2,1,0:T(8,128)(2,1)S(1)}, u32[]{:S(2)}, u32[]{:S(2)}) %collective-permute-start.7) | collective-permute-done | bytes 753696 | tf_op jit(solution)/shard_map/ppermute | solution.py:315
  45.2 7.6 %shard_map.120 = (bf16[192,5760]{1,0:T(8,128)(2,1)S(1)}, bf16[192,1024]{1,0:T(8,128)(2,1)S(1)}, bf16[1024,192]{1,0:T(8,128)(2,1)S(1)}, bf16[2,64,2944]{2,1,0:T(8...) custom-call(s32[2]{0:T(128)S(1)} %pad_add_fusion.3.place_ref, ...), custom_call_target="tpu_custom_call" | custom-call | flops 30000001024 | bytes 1048576 | tf_op jit(solution)/shard_map/pallas_call | solution.py:207
  52.8 1.6 %collective-permute-start.14 = (bf16[2,64,2944]{2,1,0:T(8,128)(2,1)S(1)}, bf16[2,64,2944]{2,1,0:T(8,128)(2,1)S(1)}, u32[]{:S(2)}, u32[]{:S(2)}) collective-permute-start(bf16[2,64,2944]{2,1,0:T(8,128)(2,1)S(1)} %get-tuple-element.89), channel_id=1, source_target_pairs={{0,4},{1,5},{2,3},{3,2},{4,0},{5,1},{6,7},{7,6},{8,12},{9,13},{10,... | collective-permute-start | bytes 2261000 | tf_op jit(solution)/shard_map/ppermute | solution.py:315
  54.6 4.7 %collective-permute-start.16 = (bf16[2,2,2,8,2944]{4,3,2,1,0:T(8,128)(2,1)S(1)}, bf16[2,2,2,8,2944]{4,3,2,1,0:T(8,128)(2,1)S(1)}, u32[]{:S(2)}, u32[]{:S(2)}) collective-permute-start(bf16[2,2,2,8,2944]{4,3,2,1,0:T(8,128)(2,1)S(1)} %maximum_select_fusion), channel_id=1, source_target_pairs={{0,8},{1,9},{2,10},{3,11},{4,12},{5,13},{6,14},{7,15},{8,0},{9,1},... | collective-permute-start | bytes 1130504 | tf_op jit(solution)/shard_map/ppermute | solution.py:315
  59.3 6.6 %shard_map.121 = (bf16[128,5760]{1,0:T(8,128)(2,1)S(1)}, bf16[128,1024]{1,0:T(8,128)(2,1)S(1)}, bf16[1024,128]{1,0:T(8,128)(2,1)S(1)}, bf16[2,64,2944]{2,1,0:T(8,128)(2,1)S(1)}, bf16[2,64,2944]{2,1,0:T(8,128)(2,1)S(1)}) custom-call(s32[2]{0:T(128)S(1)} %pad_add_fusion.3.place_ref, bf16[64,2944]{1,0:T(8,128)(2,1)S(1)} %get-tuple-element.144.own_ref, ...), custom_call_target="tpu_custom_call" | custom-call | flops 30000001024 | bytes 1048576 | tf_op jit(solution)/shard_map/pallas_call | solution.py:207
  66.7 1.5 %collective-permute-start.17 = (bf16[64,2944]{1,0:T(8,128)(2,1)S(1)}, bf16[64,2944]{1,0:T(8,128)(2,1)S(1)}, u32[]{:S(2)}, u32[]{:S(2)}) collective-permute-start(bf16[64,2944]{1,0:T(8,128)(2,1)S(1)} %fusion.9), channel_id=1, source_target_pairs={{0,1},{1,0},{2,6},{3,7},{4,5},{5,4},{6,2},{7,3},{8,9},{9,8},{10,14... | collective-permute-start | bytes 1130504 | tf_op jit(solution)/shard_map/ppermute | solution.py:315
  69.3 1.6 %collective-permute-start.21 = (bf16[2,2,8,2944]{3,2,1,0:T(8,128)(2,1)S(1)}, bf16[2,2,8,2944]{3,2,1,0:T(8,128)(2,1)S(1)}, u32[]{:S(2)}, u32[]{:S(2)}) collective-permute-start(bf16[2,2,8,2944]{3,2,1,0:T(8,128)(2,1)S(1)} %fusion.12), channel_id=1, source_target_pairs={{0,16},{1,17},{2,18},{3,19},{4,20},{5,21},{6,22},{7,23},{8,24},{9,... | collective-permute-start | bytes 565256 | tf_op jit(solution)/shard_map/ppermute | solution.py:315
  70.8 8.6 %collective-permute-done.19 = bf16[2,1,32,320]{3,2,1,0:T(8,128)(2,1)S(1)} collective-permute-done((bf16[2,1,32,320]{3,2,1,0:T(8,128)(2,1)S(1)}, bf16[2,1,32,320]{3,2,1,0:T(8,128)(2,1)S(1)}, u32[]{:S(2)}, u32[]{:S(2)}) %collective-permute-start.19) | collective-permute-done | bytes 40992 | tf_op jit(solution)/shard_map/ppermute | solution.py:244
  80.6 0.8 pad_maximum_fusion
  81.6 3.5 %shard_map.122 = f32[512,640]{1,0:T(8,128)S(1)} custom-call(bf16[192,5760]{1,0:T(8,128)(2,1)S(1)} %get-tuple-element.95.refs_0_, bf16[128,5760]{1,0:T(8,128)(2,1)S(1)} %get-tuple-element.96.refs_1_, bf16[3,576,192]{2,1,0:T(8,128)(2,1)S(1)} %slice_bitcast_fusion.refs_2_, bf16[3,576,128]{2,1,0:T(8,128)(2,1)S(1)} %slice_bitcast_fusion.2.refs_3_), custom_call_target="tpu_custom_call" | custom-call | flops 20000000000 | bytes 1048576 | tf_op jit(solution)/shard_map/pallas_call | solution.py:207
  85.7 0.8 collective-permute-start.22
  86.6 1.1 collective-permute-start.24
  87.7 1.6 %collective-permute-start.25 = (bf16[2,8,2944]{2,1,0:T(8,128)(2,1)S(1)}, bf16[2,8,2944]{2,1,0:T(8,128)(2,1)S(1)}, u32[]{:S(2)}, u32[]{:S(2)}) collective-permute-start(bf16[2,8,2944]{2,1,0:T(8,128)(2,1)S(1)} %fusion.17), channel_id=1, source_target_pairs={{0,4},{1,5},{2,3},{3,2},{4,0},{5,1},{6,7},{7,6},{8,12},{9,13},{10,... | collective-permute-start | bytes 282632 | tf_op jit(solution)/shard_map/ppermute | solution.py:315
  89.3 3.5 %shard_map.123 = f32[512,640]{1,0:T(8,128)S(1)} custom-call(bf16[192,5760]{1,0:T(8,128)(2,1)S(1)} %get-tuple-element.95.refs_0_, bf16[128,5760]{1,0:T(8,128)(2,1)S(1)} %get-tuple-element.96.refs_1_, bf16[3,576,192]{2,1,0:T(8,128)(2,1)S(1)} %slice_bitcast_fusion.1.refs_2_, bf16[3,576,128]{2,1,0:T(8,128)(2,1)S(1)} %slice_bitcast_fusion.3.refs_3_), custom_call_target="tpu_custom_call" | custom-call | flops 20000000000 | bytes 1048576 | tf_op jit(solution)/shard_map/pallas_call | solution.py:207
  93.5 0.9 collective-permute-start.23
  95.6 1.8 %collective-permute-start.28 = (bf16[2,16,2944]{2,1,0:T(8,128)(2,1)S(1)}, bf16[2,16,2944]{2,1,0:T(8,128)(2,1)S(1)}, u32[]{:S(2)}, u32[]{:S(2)}) collective-permute-start(bf16[2,16,2944]{2,1,0:T(8,128)(2,1)S(1)} %maximum_select_fusion.2), channel_id=1, source_target_pairs={{0,8},{1,9},{2,10},{3,11},{4,12},{5,13},{6,14},{7,15},{8,0},{9,1},... | collective-permute-start | bytes 565256 | tf_op jit(solution)/shard_map/ppermute | solution.py:315
  97.4 1.6 %convolution_convert_fusion = bf16[512,640]{1,0:T(8,128)(2,1)} fusion(bf16[320,512]{1,0:T(8,128)(2,1)S(1)} %collective-permute-done.20, bf16[320,512]{1,0:T(8,128)(2,1)S(1)} %slice.249, pred[320,640]{1,0:T(32,128)(4,1)S(1)} %get-tuple-element.163, pred[320,640]{1,0:T(32,128)(4,1)S(1)} %get-tuple-element.164), kind=kOutput, calls=%fused_computation.8 | convolution fusion | flops 421478400 | bytes 1720320 | tf_op jit(solution)/shard_map/dot_general | solution.py:22
  99.1 4.0 %collective-permute-done.28 = bf16[2,16,2944]{2,1,0:T(8,128)(2,1)S(1)} collective-permute-done((bf16[2,16,2944]{2,1,0:T(8,128)(2,1)S(1)}, bf16[2,16,2944]{2,1,0:T(8,128)(2,1)S(1)}, u32[]{:S(2)}, u32[]{:S(2)}) %collective-permute-start.28) | collective-permute-done | bytes 188448 | tf_op jit(solution)/shard_map/ppermute | solution.py:315
  103.1 1.7 %collective-permute-start.29 = (bf16[16,2944]{1,0:T(8,128)(2,1)S(1)}, bf16[16,2944]{1,0:T(8,128)(2,1)S(1)}, u32[]{:S(2)}, u32[]{:S(2)}) collective-permute-start(bf16[16,2944]{1,0:T(8,128)(2,1)S(1)} %fusion.14), channel_id=1, source_target_pairs={{0,16},{1,17},{2,18},{3,19},{4,20},{5,21},{6,22},{7,23},{8,24},{9,... | collective-permute-start | bytes 282632 | tf_op jit(solution)/shard_map/ppermute | solution.py:315
  104.9 1.0 add_convert_fusion
  106.5 2.0 %shard_map.124 = (f32[9,40,320]{2,1,0:T(8,128)}, f32[9,40,320]{2,1,0:T(8,128)}, f32[9,40,320]{2,1,0:T(8,128)}) custom-call(s32[2]{0:T(128)S(1)} %pad_add_fusion.3.place_ref, f32[9,40,320]{2,1,0:T(8,128)S(1)} %bitcast.107, f32[9,40,320]{2,1,0:T(8,128)S(1)} %bitcast.111, f32[9,40,320]{2,1,0:T(8,128)S(1)} %bitcast.113, ...), custom_call_target="tpu_custom_call" | custom-call | bytes 1048576 | tf_op jit(solution)/shard_map/pallas_call | solution.py:207
  108.5 2.0 %collective-permute-done.29.refs_2_ = bf16[16,2944]{1,0:T(8,128)(2,1)S(1)} collective-permute-done((bf16[16,2944]{1,0:T(8,128)(2,1)S(1)}, bf16[16,2944]{1,0:T(8,128)(2,1)S(1)}, u32[]{:S(2)}, u32[]{:S(2)}) %collective-permute-start.29) | collective-permute-done | bytes 94240 | tf_op jit(solution)/shard_map/ppermute | solution.py:315
  110.5 1.6 %shard_map.125 = (f32[9,40,320]{2,1,0:T(8,128)}, f32[9,40,320]{2,1,0:T(8,128)}, f32[9,40,320]{2,1,0:T(8,128)}) custom-call(s32[2]{0:T(128)S(1)} %pad_add_fusion.3.place_ref, f32[9,40,320]{2,1,0:T(8,128)S(1)} %bitcast.108, f32[9,40,320]{2,1,0:T(8,128)S(1)} %bitcast.112, ...), custom_call_target="tpu_custom_call", output_to_operand_aliasing={{0}: (7, {}), {1}: (8, {}), {2}: (9, {})} | custom-call | tf_op jit(solution)/shard_map/pallas_call | solution.py:486
  (99 shorter events, 8.9 us)
Async XLA Ops:
  0.6 11.5 %copy-start = (bf16[1,16,32,640]{3,2,1,0:T(8,128)(2,1)S(1)}, bf16[1,16,32,640]{3,2,1,0:T(8,128)(2,1)}, u32[]{:S(2)}) copy-start(bf16[1,16,32,640]{3,2,1,0:T(8,128)(2,1)} %param.9) | copy-start | bytes 1966084
  0.7 1.1 copy-start.1
  2.6 17.5 %collective-permute-start = (bf16[32,2944]{1,0:T(8,128)(2,1)S(1)}, bf16[32,2944]{1,0:T(8,128)(2,1)S(1)}, u32[]{:S(2)}, u32[]{:S(2)}) collective-permute-start(bf16[32,2944]{1,0:T(8,128)(2,1)S(1)} %slice.201), channel_id=1, source_target_pairs={{0,8},{1,9},{2,10},{3,11},{4,12},{5,13},{6,14},{7,15},{8,16},{9,17... | collective-permute-start | bytes 565256 | tf_op jit(solution)/shard_map/ppermute | solution.py:315
  5.6 14.9 %collective-permute-start.1 = (bf16[32,2944]{1,0:T(8,128)(2,1)S(1)}, bf16[32,2944]{1,0:T(8,128)(2,1)S(1)}, u32[]{:S(2)}, u32[]{:S(2)}) collective-permute-start(bf16[32,2944]{1,0:T(8,128)(2,1)S(1)} %slice.201), channel_id=1, source_target_pairs={{0,16},{1,17},{2,18},{3,19},{4,20},{5,21},{6,22},{7,23},{8,24},{9,... | collective-permute-start | bytes 565256 | tf_op jit(solution)/shard_map/ppermute | solution.py:315
  8.2 12.3 %collective-permute-start.2 = (bf16[32,2944]{1,0:T(8,128)(2,1)S(1)}, bf16[32,2944]{1,0:T(8,128)(2,1)}, u32[]{:S(2)}, u32[]{:S(2)}) collective-permute-start(bf16[32,2944]{1,0:T(8,128)(2,1)S(1)} %slice.201), channel_id=1, source_target_pairs={{0,24},{1,25},{2,26},{3,27},{4,28},{5,29},{6,30},{7,31},{8,0},{9,1... | collective-permute-start | bytes 565256 | tf_op jit(solution)/shard_map/ppermute | solution.py:315
  9.6 4.1 %collective-permute-start.3 = (bf16[8,2944]{1,0:T(8,128)(2,1)S(1)}, bf16[8,2944]{1,0:T(8,128)(2,1)S(1)}, u32[]{:S(2)}, u32[]{:S(2)}) collective-permute-start(bf16[8,2944]{1,0:T(8,128)(2,1)S(1)} %get-tuple-element.150), channel_id=1, source_target_pairs={{0,1},{1,0},{2,6},{3,7},{4,5},{5,4},{6,2},{7,3},{8,9},{9,8},{10,14... | collective-permute-start | bytes 141320 | tf_op jit(solution)/shard_map/ppermute | solution.py:315
  12.2 1.6 %copy-start.5 = (bf16[1,16,32,640]{3,2,1,0:T(8,128)(2,1)S(1)}, bf16[1,16,32,640]{3,2,1,0:T(8,128)(2,1)}, u32[]{:S(2)}) copy-start(bf16[1,16,32,640]{3,2,1,0:T(8,128)(2,1)} %param.8) | copy-start | bytes 1966084
  13.8 4.1 %collective-permute-start.5 = (bf16[1,1,32,640]{3,2,1,0:T(8,128)(2,1)S(1)}, bf16[1,1,32,640]{3,2,1,0:T(8,128)(2,1)S(1)}, u32[]{:S(2)}, u32[]{:S(2)}) collective-permute-start(bf16[1,1,32,640]{3,2,1,0:T(8,128)(2,1)S(1)} %slice_select_fusion.1), channel_id=1, source_target_pairs={{0,1},{1,0},{2,3},{3,2},{4,5},{5,4},{6,7},{7,6},{8,9},{9,8},{10,11... | collective-permute-start | bytes 122888 | tf_op jit(solution)/shard_map/ppermute | solution.py:244
  15.4 4.6 %collective-permute-start.4 = (bf16[2,8,2944]{2,1,0:T(8,128)(2,1)S(1)}, bf16[2,8,2944]{2,1,0:T(8,128)(2,1)S(1)}, u32[]{:S(2)}, u32[]{:S(2)}) collective-permute-start(bf16[2,8,2944]{2,1,0:T(8,128)(2,1)S(1)} %pad_maximum_fusion.11), channel_id=1, source_target_pairs={{0,4},{1,5},{2,3},{3,2},{4,0},{5,1},{6,7},{7,6},{8,12},{9,13},{10,... | collective-permute-start | bytes 282632 | tf_op jit(solution)/shard_map/ppermute | solution.py:315
  21.6 10.3 %collective-permute-start.6 = (bf16[64,2944]{1,0:T(8,128)(2,1)S(1)}, bf16[64,2944]{1,0:T(8,128)(2,1)S(1)}, u32[]{:S(2)}, u32[]{:S(2)}) collective-permute-start(bf16[64,2944]{1,0:T(8,128)(2,1)S(1)} %get-tuple-element.146.own_ref), channel_id=1, source_target_pairs={{0,1},{1,0},{2,6},{3,7},{4,5},{5,4},{6,2},{7,3},{8,9},{9,8},{10,14... | collective-permute-start | bytes 1130504 | tf_op jit(solution)/shard_map/ppermute | solution.py:315
  23.2 1.7 %collective-permute-start.10 = (bf16[320,512]{1,0:T(8,128)(2,1)S(1)}, bf16[320,512]{1,0:T(8,128)(2,1)S(1)}, u32[]{:S(2)}, u32[]{:S(2)}) collective-permute-start(bf16[320,512]{1,0:T(8,128)(2,1)S(1)} %get-tuple-element.136), channel_id=1, source_target_pairs={{0,2},{1,3},{2,0},{3,1},{4,6},{5,7},{6,4},{7,5},{8,10},{9,11},{10,... | collective-permute-start | bytes 983048 | tf_op jit(solution)/shard_map/ppermute | solution.py:315
  23.4 10.0 %collective-permute-start.8 = (bf16[64,2944]{1,0:T(8,128)(2,1)S(1)}, bf16[64,2944]{1,0:T(8,128)(2,1)S(1)}, u32[]{:S(2)}, u32[]{:S(2)}) collective-permute-start(bf16[64,2944]{1,0:T(8,128)(2,1)S(1)} %get-tuple-element.144.own_ref), channel_id=1, source_target_pairs={{0,1},{1,0},{2,6},{3,7},{4,5},{5,4},{6,2},{7,3},{8,9},{9,8},{10,14... | collective-permute-start | bytes 1130504 | tf_op jit(solution)/shard_map/ppermute | solution.py:315
  24.9 12.6 %collective-permute-start.11 = (bf16[2,2,8,2944]{3,2,1,0:T(8,128)(2,1)S(1)}, bf16[2,2,8,2944]{3,2,1,0:T(8,128)(2,1)S(1)}, u32[]{:S(2)}, u32[]{:S(2)}) collective-permute-start(bf16[2,2,8,2944]{3,2,1,0:T(8,128)(2,1)S(1)} %copy_select_fusion.1), channel_id=1, source_target_pairs={{0,8},{1,9},{2,10},{3,11},{4,12},{5,13},{6,14},{7,15},{8,16},{9,17... | collective-permute-start | bytes 565256 | tf_op jit(solution)/shard_map/ppermute | solution.py:315
  29.5 14.3 %collective-permute-start.12 = (bf16[2,2,8,2944]{3,2,1,0:T(8,128)(2,1)S(1)}, bf16[2,2,8,2944]{3,2,1,0:T(8,128)(2,1)S(1)}, u32[]{:S(2)}, u32[]{:S(2)}) collective-permute-start(bf16[2,2,8,2944]{3,2,1,0:T(8,128)(2,1)S(1)} %copy_select_fusion.1), channel_id=1, source_target_pairs={{0,16},{1,17},{2,18},{3,19},{4,20},{5,21},{6,22},{7,23},{8,24},{9,... | collective-permute-start | bytes 565256 | tf_op jit(solution)/shard_map/ppermute | solution.py:315
  31.1 12.8 %collective-permute-start.13 = (bf16[2,2,8,2944]{3,2,1,0:T(8,128)(2,1)S(1)}, bf16[2,2,8,2944]{3,2,1,0:T(8,128)(2,1)S(1)}, u32[]{:S(2)}, u32[]{:S(2)}) collective-permute-start(bf16[2,2,8,2944]{3,2,1,0:T(8,128)(2,1)S(1)} %copy_select_fusion.1), channel_id=1, source_target_pairs={{0,24},{1,25},{2,26},{3,27},{4,28},{5,29},{6,30},{7,31},{8,0},{9,1... | collective-permute-start | bytes 565256 | tf_op jit(solution)/shard_map/ppermute | solution.py:315
  32.0 3.0 %collective-permute-start.9 = (bf16[1,18,32,640]{3,2,1,0:T(8,128)(2,1)S(1)}, bf16[1,18,32,640]{3,2,1,0:T(8,128)(2,1)S(1)}, u32[]{:S(2)}, u32[]{:S(2)}) collective-permute-start(bf16[1,18,32,640]{3,2,1,0:T(8,128)(2,1)S(1)} %pad_maximum_fusion.6), channel_id=1, source_target_pairs={{0,2},{1,3},{2,0},{3,1},{4,6},{5,7},{6,4},{7,5},{8,10},{9,11},{10,... | collective-permute-start | bytes 2211848 | tf_op jit(solution)/shard_map/ppermute | solution.py:315
  33.3 11.6 %collective-permute-start.7 = (bf16[2,64,2944]{2,1,0:T(8,128)(2,1)S(1)}, bf16[2,64,2944]{2,1,0:T(8,128)(2,1)S(1)}, u32[]{:S(2)}, u32[]{:S(2)}) collective-permute-start(bf16[2,64,2944]{2,1,0:T(8,128)(2,1)S(1)} %pad_maximum_fusion.3), channel_id=1, source_target_pairs={{0,4},{1,5},{2,3},{3,2},{4,0},{5,1},{6,7},{7,6},{8,12},{9,13},{10,... | collective-permute-start | bytes 2261000 | tf_op jit(solution)/shard_map/ppermute | solution.py:315
  34.9 24.3 %collective-permute-start.15 = (bf16[2,64,2944]{2,1,0:T(8,128)(2,1)S(1)}, bf16[2,64,2944]{2,1,0:T(8,128)(2,1)S(1)}, u32[]{:S(2)}, u32[]{:S(2)}) collective-permute-start(bf16[2,64,2944]{2,1,0:T(8,128)(2,1)S(1)} %pad_maximum_fusion.5), channel_id=1, source_target_pairs={{0,4},{1,5},{2,3},{3,2},{4,0},{5,1},{6,7},{7,6},{8,12},{9,13},{10,... | collective-permute-start | bytes 2261000 | tf_op jit(solution)/shard_map/ppermute | solution.py:315
  52.8 13.8 %collective-permute-start.14 = (bf16[2,64,2944]{2,1,0:T(8,128)(2,1)S(1)}, bf16[2,64,2944]{2,1,0:T(8,128)(2,1)S(1)}, u32[]{:S(2)}, u32[]{:S(2)}) collective-permute-start(bf16[2,64,2944]{2,1,0:T(8,128)(2,1)S(1)} %get-tuple-element.89), channel_id=1, source_target_pairs={{0,4},{1,5},{2,3},{3,2},{4,0},{5,1},{6,7},{7,6},{8,12},{9,13},{10,... | collective-permute-start | bytes 2261000 | tf_op jit(solution)/shard_map/ppermute | solution.py:315
  54.6 12.0 %collective-permute-start.16 = (bf16[2,2,2,8,2944]{4,3,2,1,0:T(8,128)(2,1)S(1)}, bf16[2,2,2,8,2944]{4,3,2,1,0:T(8,128)(2,1)S(1)}, u32[]{:S(2)}, u32[]{:S(2)}) collective-permute-start(bf16[2,2,2,8,2944]{4,3,2,1,0:T(8,128)(2,1)S(1)} %maximum_select_fusion), channel_id=1, source_target_pairs={{0,8},{1,9},{2,10},{3,11},{4,12},{5,13},{6,14},{7,15},{8,0},{9,1},... | collective-permute-start | bytes 1130504 | tf_op jit(solution)/shard_map/ppermute | solution.py:315
  65.9 19.3 %collective-permute-start.18 = (bf16[2,64,2944]{2,1,0:T(8,128)(2,1)S(1)}, bf16[2,64,2944]{2,1,0:T(8,128)(2,1)S(1)}, u32[]{:S(2)}, u32[]{:S(2)}) collective-permute-start(bf16[2,64,2944]{2,1,0:T(8,128)(2,1)S(1)} %get-tuple-element.91), channel_id=1, source_target_pairs={{0,4},{1,5},{2,3},{3,2},{4,0},{5,1},{6,7},{7,6},{8,12},{9,13},{10,... | collective-permute-start | bytes 2261000 | tf_op jit(solution)/shard_map/ppermute | solution.py:315
  66.5 18.6 %collective-permute-start.20 = (bf16[320,512]{1,0:T(8,128)(2,1)S(1)}, bf16[320,512]{1,0:T(8,128)(2,1)S(1)}, u32[]{:S(2)}, u32[]{:S(2)}) collective-permute-start(bf16[320,512]{1,0:T(8,128)(2,1)S(1)} %slice.272), channel_id=1, source_target_pairs={{0,2},{1,3},{2,0},{3,1},{4,6},{5,7},{6,4},{7,5},{8,10},{9,11},{10,... | collective-permute-start | bytes 983048 | tf_op jit(solution)/shard_map/ppermute | solution.py:315
  66.7 18.5 %collective-permute-start.17 = (bf16[64,2944]{1,0:T(8,128)(2,1)S(1)}, bf16[64,2944]{1,0:T(8,128)(2,1)S(1)}, u32[]{:S(2)}, u32[]{:S(2)}) collective-permute-start(bf16[64,2944]{1,0:T(8,128)(2,1)S(1)} %fusion.9), channel_id=1, source_target_pairs={{0,1},{1,0},{2,6},{3,7},{4,5},{5,4},{6,2},{7,3},{8,9},{9,8},{10,14... | collective-permute-start | bytes 1130504 | tf_op jit(solution)/shard_map/ppermute | solution.py:315
  68.6 10.8 %collective-permute-start.19 = (bf16[2,1,32,320]{3,2,1,0:T(8,128)(2,1)S(1)}, bf16[2,1,32,320]{3,2,1,0:T(8,128)(2,1)S(1)}, u32[]{:S(2)}, u32[]{:S(2)}) collective-permute-start(bf16[2,1,32,320]{3,2,1,0:T(8,128)(2,1)S(1)} %slice_select_fusion), channel_id=1, source_target_pairs={{0,1},{1,0},{2,3},{3,2},{4,5},{5,4},{6,7},{7,6},{8,9},{9,8},{10,11... | collective-permute-start | bytes 122888 | tf_op jit(solution)/shard_map/ppermute | solution.py:244
  69.3 15.9 %collective-permute-start.21 = (bf16[2,2,8,2944]{3,2,1,0:T(8,128)(2,1)S(1)}, bf16[2,2,8,2944]{3,2,1,0:T(8,128)(2,1)S(1)}, u32[]{:S(2)}, u32[]{:S(2)}) collective-permute-start(bf16[2,2,8,2944]{3,2,1,0:T(8,128)(2,1)S(1)} %fusion.12), channel_id=1, source_target_pairs={{0,16},{1,17},{2,18},{3,19},{4,20},{5,21},{6,22},{7,23},{8,24},{9,... | collective-permute-start | bytes 565256 | tf_op jit(solution)/shard_map/ppermute | solution.py:315
  85.7 7.8 %collective-permute-start.22 = (bf16[2,16,2944]{2,1,0:T(8,128)(2,1)S(1)}, bf16[2,16,2944]{2,1,0:T(8,128)(2,1)S(1)}, u32[]{:S(2)}, u32[]{:S(2)}) collective-permute-start(bf16[2,16,2944]{2,1,0:T(8,128)(2,1)S(1)} %maximum_select_fusion.1), channel_id=1, source_target_pairs={{0,8},{1,9},{2,10},{3,11},{4,12},{5,13},{6,14},{7,15},{8,0},{9,1},... | collective-permute-start | bytes 565256 | tf_op jit(solution)/shard_map/ppermute | solution.py:315
  86.6 8.4 %collective-permute-start.24 = (bf16[64,2944]{1,0:T(8,128)(2,1)S(1)}, bf16[64,2944]{1,0:T(8,128)(2,1)S(1)}, u32[]{:S(2)}, u32[]{:S(2)}) collective-permute-start(bf16[64,2944]{1,0:T(8,128)(2,1)S(1)} %fusion.10), channel_id=1, source_target_pairs={{0,1},{1,0},{2,6},{3,7},{4,5},{5,4},{6,2},{7,3},{8,9},{9,8},{10,14... | collective-permute-start | bytes 1130504 | tf_op jit(solution)/shard_map/ppermute | solution.py:315
  87.7 5.7 %collective-permute-start.25 = (bf16[2,8,2944]{2,1,0:T(8,128)(2,1)S(1)}, bf16[2,8,2944]{2,1,0:T(8,128)(2,1)S(1)}, u32[]{:S(2)}, u32[]{:S(2)}) collective-permute-start(bf16[2,8,2944]{2,1,0:T(8,128)(2,1)S(1)} %fusion.17), channel_id=1, source_target_pairs={{0,4},{1,5},{2,3},{3,2},{4,0},{5,1},{6,7},{7,6},{8,12},{9,13},{10,... | collective-permute-start | bytes 282632 | tf_op jit(solution)/shard_map/ppermute | solution.py:315
  93.5 12.4 %collective-permute-start.23 = (bf16[16,2944]{1,0:T(8,128)(2,1)S(1)}, bf16[16,2944]{1,0:T(8,128)(2,1)S(1)}, u32[]{:S(2)}, u32[]{:S(2)}) collective-permute-start(bf16[16,2944]{1,0:T(8,128)(2,1)S(1)} %fusion.15), channel_id=1, source_target_pairs={{0,16},{1,17},{2,18},{3,19},{4,20},{5,21},{6,22},{7,23},{8,24},{9,... | collective-permute-start | bytes 282632 | tf_op jit(solution)/shard_map/ppermute | solution.py:315
  94.9 4.1 %collective-permute-start.26 = (bf16[8,2944]{1,0:T(8,128)(2,1)S(1)}, bf16[8,2944]{1,0:T(8,128)(2,1)S(1)}, u32[]{:S(2)}, u32[]{:S(2)}) collective-permute-start(bf16[8,2944]{1,0:T(8,128)(2,1)S(1)} %fusion.18), channel_id=1, source_target_pairs={{0,1},{1,0},{2,6},{3,7},{4,5},{5,4},{6,2},{7,3},{8,9},{9,8},{10,14... | collective-permute-start | bytes 141320 | tf_op jit(solution)/shard_map/ppermute | solution.py:315
  95.3 9.5 %collective-permute-start.27 = (f32[512,640]{1,0:T(8,128)S(1)}, f32[512,640]{1,0:T(8,128)S(1)}, u32[]{:S(2)}, u32[]{:S(2)}) collective-permute-start(f32[512,640]{1,0:T(8,128)S(1)} %shard_map.122), channel_id=1, source_target_pairs={{0,2},{1,3},{2,0},{3,1},{4,6},{5,7},{6,4},{7,5},{8,10},{9,11},{10,... | collective-permute-start | bytes 3932168 | tf_op jit(solution)/shard_map/ppermute | solution.py:315
  95.6 7.4 %collective-permute-start.28 = (bf16[2,16,2944]{2,1,0:T(8,128)(2,1)S(1)}, bf16[2,16,2944]{2,1,0:T(8,128)(2,1)S(1)}, u32[]{:S(2)}, u32[]{:S(2)}) collective-permute-start(bf16[2,16,2944]{2,1,0:T(8,128)(2,1)S(1)} %maximum_select_fusion.2), channel_id=1, source_target_pairs={{0,8},{1,9},{2,10},{3,11},{4,12},{5,13},{6,14},{7,15},{8,0},{9,1},... | collective-permute-start | bytes 565256 | tf_op jit(solution)/shard_map/ppermute | solution.py:315
  103.1 7.4 %collective-permute-start.29 = (bf16[16,2944]{1,0:T(8,128)(2,1)S(1)}, bf16[16,2944]{1,0:T(8,128)(2,1)S(1)}, u32[]{:S(2)}, u32[]{:S(2)}) collective-permute-start(bf16[16,2944]{1,0:T(8,128)(2,1)S(1)} %fusion.14), channel_id=1, source_target_pairs={{0,16},{1,17},{2,18},{3,19},{4,20},{5,21},{6,22},{7,23},{8,24},{9,... | collective-permute-start | bytes 282632 | tf_op jit(solution)/shard_map/ppermute | solution.py:315
  104.8 1.1 copy-start.2
  104.9 1.4 %copy-start.3 = (f32[9,320,40]{1,2,0:T(8,128)S(1)}, f32[9,320,40]{1,2,0:T(8,128)}, u32[]{:S(2)}) copy-start(f32[9,320,40]{1,2,0:T(8,128)} %param.11) | copy-start | bytes 1382404
  104.9 1.6 %copy-start.4 = (f32[9,320,40]{1,2,0:T(8,128)S(1)}, f32[9,320,40]{1,2,0:T(8,128)}, u32[]{:S(2)}) copy-start(f32[9,320,40]{1,2,0:T(8,128)} %param.12) | copy-start | bytes 1382404

commit v6 on v5

--- a/solution.py
+++ b/solution.py
@@ -12,7 +12,7 @@
 F32 = jnp.float32
 NT = (((1,), (1,)), ((), ()))
 NN = (((1,), (0,)), ((), ()))
-VMEM_LIMIT = 28 << 20
+VMEM_LIMIT = 22 << 20
 TAPS = 9
 CHUNKS = (24, 16)
 ROUTE_A = 8

time: 112 us -> 112 us (level)
  no operation moved by 1% of the time
where the time goes in v6:
time: 112 us
  starting transfers between devices  42.9 us (38%)
  waiting for transfers between devices  28.9 us (26%)
  Pallas kernels  25.6 us (23%)
  other arithmetic  5.67 us (5%)
  local copies, waits for them, and re-layouts  5.51 us (5%)
  matrix products  2.34 us (2%)
  between operations  1.26 us (1%)
    ppermute x28, starting transfers between devices, hop(): return lambda v: lax.ppermute(v, ('dp', 'rows'), pairs)  40.8 us
    pallas_call x6, Pallas kernels, vmem_call(): pl.pallas_call(kernel, out_shape=outs, in_specs=[pl.BlockSpec(memory_spac...  24 us
    ppermute x28, waiting for transfers between devices, hop(): return lambda v: lax.ppermute(v, ('dp', 'rows'), pairs)  19.4 us
    ppermute x2, waiting for transfers between devices, with_halo(): got = lax.ppermute(edge, 'rows', [(0, 1), (1, 0)])  9.47 us
    dot_general x2, matrix products, mm(): return lax.dot_general(a, b, dims, preferred_element_type=F32)  2.34 us
  transfers between devices with their start and end apart: 30, of which 13 were waited for; matrix products, arithmetic and copies ran while one was open for 9% of the time, Pallas kernels for 21%

profile of v6, /device:TPU:0, one launch (start us, length us, event | category | flops | bytes accessed | tf_op | source)
XLA Modules:
  0.0 112.2 jit_solution(1206621354686652725)
XLA Ops:
  0.7 1.1 copy-done.1
  1.8 0.7 shard_map.119
  2.6 3.1 %collective-permute-start = (bf16[32,2944]{1,0:T(8,128)(2,1)S(1)}, bf16[32,2944]{1,0:T(8,128)(2,1)S(1)}, u32[]{:S(2)}, u32[]{:S(2)}) collective-permute-start(bf16[32,2944]{1,0:T(8,128)(2,1)S(1)} %slice.201), channel_id=1, source_target_pairs={{0,8},{1,9},{2,10},{3,11},{4,12},{5,13},{6,14},{7,15},{8,16},{9,17... | collective-permute-start | bytes 565256 | tf_op jit(solution)/shard_map/ppermute | solution.py:315
  5.6 2.6 %collective-permute-start.1 = (bf16[32,2944]{1,0:T(8,128)(2,1)S(1)}, bf16[32,2944]{1,0:T(8,128)(2,1)S(1)}, u32[]{:S(2)}, u32[]{:S(2)}) collective-permute-start(bf16[32,2944]{1,0:T(8,128)(2,1)S(1)} %slice.201), channel_id=1, source_target_pairs={{0,16},{1,17},{2,18},{3,19},{4,20},{5,21},{6,22},{7,23},{8,24},{9,... | collective-permute-start | bytes 565256 | tf_op jit(solution)/shard_map/ppermute | solution.py:315
  8.2 1.3 %collective-permute-start.2 = (bf16[32,2944]{1,0:T(8,128)(2,1)S(1)}, bf16[32,2944]{1,0:T(8,128)(2,1)}, u32[]{:S(2)}, u32[]{:S(2)}) collective-permute-start(bf16[32,2944]{1,0:T(8,128)(2,1)S(1)} %slice.201), channel_id=1, source_target_pairs={{0,24},{1,25},{2,26},{3,27},{4,28},{5,29},{6,30},{7,31},{8,0},{9,1... | collective-permute-start | bytes 565256 | tf_op jit(solution)/shard_map/ppermute | solution.py:315
  9.6 1.6 %collective-permute-start.3 = (bf16[8,2944]{1,0:T(8,128)(2,1)S(1)}, bf16[8,2944]{1,0:T(8,128)(2,1)S(1)}, u32[]{:S(2)}, u32[]{:S(2)}) collective-permute-start(bf16[8,2944]{1,0:T(8,128)(2,1)S(1)} %get-tuple-element.150), channel_id=1, source_target_pairs={{0,1},{1,0},{2,6},{3,7},{4,5},{5,4},{6,2},{7,3},{8,9},{9,8},{10,14... | collective-permute-start | bytes 141320 | tf_op jit(solution)/shard_map/ppermute | solution.py:315
  11.1 0.7 multiply_add_fusion.1
  12.2 0.7 convolution_convert_fusion.1
  12.9 0.8 collective-permute-done.3
  13.8 1.6 %collective-permute-start.5 = (bf16[1,1,32,640]{3,2,1,0:T(8,128)(2,1)S(1)}, bf16[1,1,32,640]{3,2,1,0:T(8,128)(2,1)S(1)}, u32[]{:S(2)}, u32[]{:S(2)}) collective-permute-start(bf16[1,1,32,640]{3,2,1,0:T(8,128)(2,1)S(1)} %slice_select_fusion.1), channel_id=1, source_target_pairs={{0,1},{1,0},{2,3},{3,2},{4,5},{5,4},{6,7},{7,6},{8,9},{9,8},{10,11... | collective-permute-start | bytes 122888 | tf_op jit(solution)/shard_map/ppermute | solution.py:244
  15.4 1.6 %collective-permute-start.4 = (bf16[2,8,2944]{2,1,0:T(8,128)(2,1)S(1)}, bf16[2,8,2944]{2,1,0:T(8,128)(2,1)S(1)}, u32[]{:S(2)}, u32[]{:S(2)}) collective-permute-start(bf16[2,8,2944]{2,1,0:T(8,128)(2,1)S(1)} %pad_maximum_fusion.11), channel_id=1, source_target_pairs={{0,4},{1,5},{2,3},{3,2},{4,0},{5,1},{6,7},{7,6},{8,12},{9,13},{10,... | collective-permute-start | bytes 282632 | tf_op jit(solution)/shard_map/ppermute | solution.py:315
  16.9 0.9 collective-permute-done.5
  18.0 2.0 %collective-permute-done.4 = bf16[2,8,2944]{2,1,0:T(8,128)(2,1)S(1)} collective-permute-done((bf16[2,8,2944]{2,1,0:T(8,128)(2,1)S(1)}, bf16[2,8,2944]{2,1,0:T(8,128)(2,1)S(1)}, u32[]{:S(2)}, u32[]{:S(2)}) %collective-permute-start.4) | collective-permute-done | bytes 94240 | tf_op jit(solution)/shard_map/ppermute | solution.py:315
  20.6 1.0 fusion.35
  21.6 1.5 %collective-permute-start.6 = (bf16[64,2944]{1,0:T(8,128)(2,1)S(1)}, bf16[64,2944]{1,0:T(8,128)(2,1)S(1)}, u32[]{:S(2)}, u32[]{:S(2)}) collective-permute-start(bf16[64,2944]{1,0:T(8,128)(2,1)S(1)} %get-tuple-element.146.own_ref), channel_id=1, source_target_pairs={{0,1},{1,0},{2,6},{3,7},{4,5},{5,4},{6,2},{7,3},{8,9},{9,8},{10,14... | collective-permute-start | bytes 1130504 | tf_op jit(solution)/shard_map/ppermute | solution.py:315
  23.4 1.2 %collective-permute-start.8 = (bf16[64,2944]{1,0:T(8,128)(2,1)S(1)}, bf16[64,2944]{1,0:T(8,128)(2,1)S(1)}, u32[]{:S(2)}, u32[]{:S(2)}) collective-permute-start(bf16[64,2944]{1,0:T(8,128)(2,1)S(1)} %get-tuple-element.144.own_ref), channel_id=1, source_target_pairs={{0,1},{1,0},{2,6},{3,7},{4,5},{5,4},{6,2},{7,3},{8,9},{9,8},{10,14... | collective-permute-start | bytes 1130504 | tf_op jit(solution)/shard_map/ppermute | solution.py:315
  24.9 4.6 %collective-permute-start.11 = (bf16[2,2,8,2944]{3,2,1,0:T(8,128)(2,1)S(1)}, bf16[2,2,8,2944]{3,2,1,0:T(8,128)(2,1)S(1)}, u32[]{:S(2)}, u32[]{:S(2)}) collective-permute-start(bf16[2,2,8,2944]{3,2,1,0:T(8,128)(2,1)S(1)} %copy_select_fusion.1), channel_id=1, source_target_pairs={{0,8},{1,9},{2,10},{3,11},{4,12},{5,13},{6,14},{7,15},{8,16},{9,17... | collective-permute-start | bytes 565256 | tf_op jit(solution)/shard_map/ppermute | solution.py:315
  29.5 1.5 %collective-permute-start.12 = (bf16[2,2,8,2944]{3,2,1,0:T(8,128)(2,1)S(1)}, bf16[2,2,8,2944]{3,2,1,0:T(8,128)(2,1)S(1)}, u32[]{:S(2)}, u32[]{:S(2)}) collective-permute-start(bf16[2,2,8,2944]{3,2,1,0:T(8,128)(2,1)S(1)} %copy_select_fusion.1), channel_id=1, source_target_pairs={{0,16},{1,17},{2,18},{3,19},{4,20},{5,21},{6,22},{7,23},{8,24},{9,... | collective-permute-start | bytes 565256 | tf_op jit(solution)/shard_map/ppermute | solution.py:315
  31.1 0.8 collective-permute-start.13
  32.2 1.1 collective-permute-done.8.near_ref
  33.3 1.5 %collective-permute-start.7 = (bf16[2,64,2944]{2,1,0:T(8,128)(2,1)S(1)}, bf16[2,64,2944]{2,1,0:T(8,128)(2,1)S(1)}, u32[]{:S(2)}, u32[]{:S(2)}) collective-permute-start(bf16[2,64,2944]{2,1,0:T(8,128)(2,1)S(1)} %pad_maximum_fusion.3), channel_id=1, source_target_pairs={{0,4},{1,5},{2,3},{3,2},{4,0},{5,1},{6,7},{7,6},{8,12},{9,13},{10,... | collective-permute-start | bytes 2261000 | tf_op jit(solution)/shard_map/ppermute | solution.py:315
  34.9 0.8 collective-permute-start.15
  35.9 0.8 fusion.27
  36.7 0.9 fusion.2
  37.6 6.3 %collective-permute-done.12 = bf16[2,2,8,2944]{3,2,1,0:T(8,128)(2,1)S(1)} collective-permute-done((bf16[2,2,8,2944]{3,2,1,0:T(8,128)(2,1)S(1)}, bf16[2,2,8,2944]{3,2,1,0:T(8,128)(2,1)S(1)}, u32[]{:S(2)}, u32[]{:S(2)}) %collective-permute-start.12) | collective-permute-done | bytes 188448 | tf_op jit(solution)/shard_map/ppermute | solution.py:315
  43.8 1.1 %collective-permute-done.7.far_ref = bf16[2,64,2944]{2,1,0:T(8,128)(2,1)S(1)} collective-permute-done((bf16[2,64,2944]{2,1,0:T(8,128)(2,1)S(1)}, bf16[2,64,2944]{2,1,0:T(8,128)(2,1)S(1)}, u32[]{:S(2)}, u32[]{:S(2)}) %collective-permute-start.7) | collective-permute-done | bytes 753696 | tf_op jit(solution)/shard_map/ppermute | solution.py:315
  45.2 7.6 %shard_map.120 = (bf16[192,5760]{1,0:T(8,128)(2,1)S(1)}, bf16[192,1024]{1,0:T(8,128)(2,1)S(1)}, bf16[1024,192]{1,0:T(8,128)(2,1)S(1)}, bf16[2,64,2944]{2,1,0:T(8...) custom-call(s32[2]{0:T(128)S(1)} %pad_add_fusion.3.place_ref, ...), custom_call_target="tpu_custom_call" | custom-call | flops 30000001024 | bytes 1048576 | tf_op jit(solution)/shard_map/pallas_call | solution.py:207
  52.9 1.6 %collective-permute-start.14 = (bf16[2,64,2944]{2,1,0:T(8,128)(2,1)S(1)}, bf16[2,64,2944]{2,1,0:T(8,128)(2,1)S(1)}, u32[]{:S(2)}, u32[]{:S(2)}) collective-permute-start(bf16[2,64,2944]{2,1,0:T(8,128)(2,1)S(1)} %get-tuple-element.89), channel_id=1, source_target_pairs={{0,4},{1,5},{2,3},{3,2},{4,0},{5,1},{6,7},{7,6},{8,12},{9,13},{10,... | collective-permute-start | bytes 2261000 | tf_op jit(solution)/shard_map/ppermute | solution.py:315
  54.6 4.7 %collective-permute-start.16 = (bf16[2,2,2,8,2944]{4,3,2,1,0:T(8,128)(2,1)S(1)}, bf16[2,2,2,8,2944]{4,3,2,1,0:T(8,128)(2,1)S(1)}, u32[]{:S(2)}, u32[]{:S(2)}) collective-permute-start(bf16[2,2,2,8,2944]{4,3,2,1,0:T(8,128)(2,1)S(1)} %maximum_select_fusion), channel_id=1, source_target_pairs={{0,8},{1,9},{2,10},{3,11},{4,12},{5,13},{6,14},{7,15},{8,0},{9,1},... | collective-permute-start | bytes 1130504 | tf_op jit(solution)/shard_map/ppermute | solution.py:315
  59.3 6.6 %shard_map.121 = (bf16[128,5760]{1,0:T(8,128)(2,1)S(1)}, bf16[128,1024]{1,0:T(8,128)(2,1)S(1)}, bf16[1024,128]{1,0:T(8,128)(2,1)S(1)}, bf16[2,64,2944]{2,1,0:T(8,128)(2,1)S(1)}, bf16[2,64,2944]{2,1,0:T(8,128)(2,1)S(1)}) custom-call(s32[2]{0:T(128)S(1)} %pad_add_fusion.3.place_ref, bf16[64,2944]{1,0:T(8,128)(2,1)S(1)} %get-tuple-element.144.own_ref, ...), custom_call_target="tpu_custom_call" | custom-call | flops 30000001024 | bytes 1048576 | tf_op jit(solution)/shard_map/pallas_call | solution.py:207
  66.7 1.5 %collective-permute-start.17 = (bf16[64,2944]{1,0:T(8,128)(2,1)S(1)}, bf16[64,2944]{1,0:T(8,128)(2,1)S(1)}, u32[]{:S(2)}, u32[]{:S(2)}) collective-permute-start(bf16[64,2944]{1,0:T(8,128)(2,1)S(1)} %fusion.9), channel_id=1, source_target_pairs={{0,1},{1,0},{2,6},{3,7},{4,5},{5,4},{6,2},{7,3},{8,9},{9,8},{10,14... | collective-permute-start | bytes 1130504 | tf_op jit(solution)/shard_map/ppermute | solution.py:315
  69.2 1.6 %collective-permute-start.21 = (bf16[2,2,8,2944]{3,2,1,0:T(8,128)(2,1)S(1)}, bf16[2,2,8,2944]{3,2,1,0:T(8,128)(2,1)S(1)}, u32[]{:S(2)}, u32[]{:S(2)}) collective-permute-start(bf16[2,2,8,2944]{3,2,1,0:T(8,128)(2,1)S(1)} %fusion.12), channel_id=1, source_target_pairs={{0,16},{1,17},{2,18},{3,19},{4,20},{5,21},{6,22},{7,23},{8,24},{9,... | collective-permute-start | bytes 565256 | tf_op jit(solution)/shard_map/ppermute | solution.py:315
  70.8 8.6 %collective-permute-done.19 = bf16[2,1,32,320]{3,2,1,0:T(8,128)(2,1)S(1)} collective-permute-done((bf16[2,1,32,320]{3,2,1,0:T(8,128)(2,1)S(1)}, bf16[2,1,32,320]{3,2,1,0:T(8,128)(2,1)S(1)}, u32[]{:S(2)}, u32[]{:S(2)}) %collective-permute-start.19) | collective-permute-done | bytes 40992 | tf_op jit(solution)/shard_map/ppermute | solution.py:244
  80.5 0.8 pad_maximum_fusion
  81.6 3.5 %shard_map.122 = f32[512,640]{1,0:T(8,128)S(1)} custom-call(bf16[192,5760]{1,0:T(8,128)(2,1)S(1)} %get-tuple-element.95.refs_0_, bf16[128,5760]{1,0:T(8,128)(2,1)S(1)} %get-tuple-element.96.refs_1_, bf16[3,576,192]{2,1,0:T(8,128)(2,1)S(1)} %slice_bitcast_fusion.refs_2_, bf16[3,576,128]{2,1,0:T(8,128)(2,1)S(1)} %slice_bitcast_fusion.2.refs_3_), custom_call_target="tpu_custom_call" | custom-call | flops 20000000000 | bytes 1048576 | tf_op jit(solution)/shard_map/pallas_call | solution.py:207
  85.7 0.8 collective-permute-start.22
  86.6 1.1 collective-permute-start.24
  87.7 1.6 %collective-permute-start.25 = (bf16[2,8,2944]{2,1,0:T(8,128)(2,1)S(1)}, bf16[2,8,2944]{2,1,0:T(8,128)(2,1)S(1)}, u32[]{:S(2)}, u32[]{:S(2)}) collective-permute-start(bf16[2,8,2944]{2,1,0:T(8,128)(2,1)S(1)} %fusion.17), channel_id=1, source_target_pairs={{0,4},{1,5},{2,3},{3,2},{4,0},{5,1},{6,7},{7,6},{8,12},{9,13},{10,... | collective-permute-start | bytes 282632 | tf_op jit(solution)/shard_map/ppermute | solution.py:315
  89.3 3.5 %shard_map.123 = f32[512,640]{1,0:T(8,128)S(1)} custom-call(bf16[192,5760]{1,0:T(8,128)(2,1)S(1)} %get-tuple-element.95.refs_0_, bf16[128,5760]{1,0:T(8,128)(2,1)S(1)} %get-tuple-element.96.refs_1_, bf16[3,576,192]{2,1,0:T(8,128)(2,1)S(1)} %slice_bitcast_fusion.1.refs_2_, bf16[3,576,128]{2,1,0:T(8,128)(2,1)S(1)} %slice_bitcast_fusion.3.refs_3_), custom_call_target="tpu_custom_call" | custom-call | flops 20000000000 | bytes 1048576 | tf_op jit(solution)/shard_map/pallas_call | solution.py:207
  93.5 0.9 collective-permute-start.23
  95.7 1.8 %collective-permute-start.28 = (bf16[2,16,2944]{2,1,0:T(8,128)(2,1)S(1)}, bf16[2,16,2944]{2,1,0:T(8,128)(2,1)S(1)}, u32[]{:S(2)}, u32[]{:S(2)}) collective-permute-start(bf16[2,16,2944]{2,1,0:T(8,128)(2,1)S(1)} %maximum_select_fusion.2), channel_id=1, source_target_pairs={{0,8},{1,9},{2,10},{3,11},{4,12},{5,13},{6,14},{7,15},{8,0},{9,1},... | collective-permute-start | bytes 565256 | tf_op jit(solution)/shard_map/ppermute | solution.py:315
  97.5 1.6 %convolution_convert_fusion = bf16[512,640]{1,0:T(8,128)(2,1)} fusion(bf16[320,512]{1,0:T(8,128)(2,1)S(1)} %collective-permute-done.20, bf16[320,512]{1,0:T(8,128)(2,1)S(1)} %slice.249, pred[320,640]{1,0:T(32,128)(4,1)S(1)} %get-tuple-element.163, pred[320,640]{1,0:T(32,128)(4,1)S(1)} %get-tuple-element.164), kind=kOutput, calls=%fused_computation.8 | convolution fusion | flops 421478400 | bytes 1720320 | tf_op jit(solution)/shard_map/dot_general | solution.py:22
  99.1 4.0 %collective-permute-done.28 = bf16[2,16,2944]{2,1,0:T(8,128)(2,1)S(1)} collective-permute-done((bf16[2,16,2944]{2,1,0:T(8,128)(2,1)S(1)}, bf16[2,16,2944]{2,1,0:T(8,128)(2,1)S(1)}, u32[]{:S(2)}, u32[]{:S(2)}) %collective-permute-start.28) | collective-permute-done | bytes 188448 | tf_op jit(solution)/shard_map/ppermute | solution.py:315
  103.1 1.7 %collective-permute-start.29 = (bf16[16,2944]{1,0:T(8,128)(2,1)S(1)}, bf16[16,2944]{1,0:T(8,128)(2,1)S(1)}, u32[]{:S(2)}, u32[]{:S(2)}) collective-permute-start(bf16[16,2944]{1,0:T(8,128)(2,1)S(1)} %fusion.14), channel_id=1, source_target_pairs={{0,16},{1,17},{2,18},{3,19},{4,20},{5,21},{6,22},{7,23},{8,24},{9,... | collective-permute-start | bytes 282632 | tf_op jit(solution)/shard_map/ppermute | solution.py:315
  104.9 1.0 add_convert_fusion
  106.5 2.0 %shard_map.124 = (f32[9,40,320]{2,1,0:T(8,128)}, f32[9,40,320]{2,1,0:T(8,128)}, f32[9,40,320]{2,1,0:T(8,128)}) custom-call(s32[2]{0:T(128)S(1)} %pad_add_fusion.3.place_ref, f32[9,40,320]{2,1,0:T(8,128)S(1)} %bitcast.107, f32[9,40,320]{2,1,0:T(8,128)S(1)} %bitcast.111, f32[9,40,320]{2,1,0:T(8,128)S(1)} %bitcast.113, ...), custom_call_target="tpu_custom_call" | custom-call | bytes 1048576 | tf_op jit(solution)/shard_map/pallas_call | solution.py:207
  108.5 2.1 %collective-permute-done.29.refs_2_ = bf16[16,2944]{1,0:T(8,128)(2,1)S(1)} collective-permute-done((bf16[16,2944]{1,0:T(8,128)(2,1)S(1)}, bf16[16,2944]{1,0:T(8,128)(2,1)S(1)}, u32[]{:S(2)}, u32[]{:S(2)}) %collective-permute-start.29) | collective-permute-done | bytes 94240 | tf_op jit(solution)/shard_map/ppermute | solution.py:315
  110.5 1.6 %shard_map.125 = (f32[9,40,320]{2,1,0:T(8,128)}, f32[9,40,320]{2,1,0:T(8,128)}, f32[9,40,320]{2,1,0:T(8,128)}) custom-call(s32[2]{0:T(128)S(1)} %pad_add_fusion.3.place_ref, f32[9,40,320]{2,1,0:T(8,128)S(1)} %bitcast.108, f32[9,40,320]{2,1,0:T(8,128)S(1)} %bitcast.112, ...), custom_call_target="tpu_custom_call", output_to_operand_aliasing={{0}: (7, {}), {1}: (8, {}), {2}: (9, {})} | custom-call | tf_op jit(solution)/shard_map/pallas_call | solution.py:486
  (99 shorter events, 8.9 us)
Async XLA Ops:
  0.6 11.5 %copy-start = (bf16[1,16,32,640]{3,2,1,0:T(8,128)(2,1)S(1)}, bf16[1,16,32,640]{3,2,1,0:T(8,128)(2,1)}, u32[]{:S(2)}) copy-start(bf16[1,16,32,640]{3,2,1,0:T(8,128)(2,1)} %param.9) | copy-start | bytes 1966084
  0.7 1.1 copy-start.1
  2.6 17.5 %collective-permute-start = (bf16[32,2944]{1,0:T(8,128)(2,1)S(1)}, bf16[32,2944]{1,0:T(8,128)(2,1)S(1)}, u32[]{:S(2)}, u32[]{:S(2)}) collective-permute-start(bf16[32,2944]{1,0:T(8,128)(2,1)S(1)} %slice.201), channel_id=1, source_target_pairs={{0,8},{1,9},{2,10},{3,11},{4,12},{5,13},{6,14},{7,15},{8,16},{9,17... | collective-permute-start | bytes 565256 | tf_op jit(solution)/shard_map/ppermute | solution.py:315
  5.6 14.9 %collective-permute-start.1 = (bf16[32,2944]{1,0:T(8,128)(2,1)S(1)}, bf16[32,2944]{1,0:T(8,128)(2,1)S(1)}, u32[]{:S(2)}, u32[]{:S(2)}) collective-permute-start(bf16[32,2944]{1,0:T(8,128)(2,1)S(1)} %slice.201), channel_id=1, source_target_pairs={{0,16},{1,17},{2,18},{3,19},{4,20},{5,21},{6,22},{7,23},{8,24},{9,... | collective-permute-start | bytes 565256 | tf_op jit(solution)/shard_map/ppermute | solution.py:315
  8.2 12.3 %collective-permute-start.2 = (bf16[32,2944]{1,0:T(8,128)(2,1)S(1)}, bf16[32,2944]{1,0:T(8,128)(2,1)}, u32[]{:S(2)}, u32[]{:S(2)}) collective-permute-start(bf16[32,2944]{1,0:T(8,128)(2,1)S(1)} %slice.201), channel_id=1, source_target_pairs={{0,24},{1,25},{2,26},{3,27},{4,28},{5,29},{6,30},{7,31},{8,0},{9,1... | collective-permute-start | bytes 565256 | tf_op jit(solution)/shard_map/ppermute | solution.py:315
  9.6 4.1 %collective-permute-start.3 = (bf16[8,2944]{1,0:T(8,128)(2,1)S(1)}, bf16[8,2944]{1,0:T(8,128)(2,1)S(1)}, u32[]{:S(2)}, u32[]{:S(2)}) collective-permute-start(bf16[8,2944]{1,0:T(8,128)(2,1)S(1)} %get-tuple-element.150), channel_id=1, source_target_pairs={{0,1},{1,0},{2,6},{3,7},{4,5},{5,4},{6,2},{7,3},{8,9},{9,8},{10,14... | collective-permute-start | bytes 141320 | tf_op jit(solution)/shard_map/ppermute | solution.py:315
  12.2 1.6 %copy-start.5 = (bf16[1,16,32,640]{3,2,1,0:T(8,128)(2,1)S(1)}, bf16[1,16,32,640]{3,2,1,0:T(8,128)(2,1)}, u32[]{:S(2)}) copy-start(bf16[1,16,32,640]{3,2,1,0:T(8,128)(2,1)} %param.8) | copy-start | bytes 1966084
  13.8 4.1 %collective-permute-start.5 = (bf16[1,1,32,640]{3,2,1,0:T(8,128)(2,1)S(1)}, bf16[1,1,32,640]{3,2,1,0:T(8,128)(2,1)S(1)}, u32[]{:S(2)}, u32[]{:S(2)}) collective-permute-start(bf16[1,1,32,640]{3,2,1,0:T(8,128)(2,1)S(1)} %slice_select_fusion.1), channel_id=1, source_target_pairs={{0,1},{1,0},{2,3},{3,2},{4,5},{5,4},{6,7},{7,6},{8,9},{9,8},{10,11... | collective-permute-start | bytes 122888 | tf_op jit(solution)/shard_map/ppermute | solution.py:244
  15.4 4.6 %collective-permute-start.4 = (bf16[2,8,2944]{2,1,0:T(8,128)(2,1)S(1)}, bf16[2,8,2944]{2,1,0:T(8,128)(2,1)S(1)}, u32[]{:S(2)}, u32[]{:S(2)}) collective-permute-start(bf16[2,8,2944]{2,1,0:T(8,128)(2,1)S(1)} %pad_maximum_fusion.11), channel_id=1, source_target_pairs={{0,4},{1,5},{2,3},{3,2},{4,0},{5,1},{6,7},{7,6},{8,12},{9,13},{10,... | collective-permute-start | bytes 282632 | tf_op jit(solution)/shard_map/ppermute | solution.py:315
  21.6 10.3 %collective-permute-start.6 = (bf16[64,2944]{1,0:T(8,128)(2,1)S(1)}, bf16[64,2944]{1,0:T(8,128)(2,1)S(1)}, u32[]{:S(2)}, u32[]{:S(2)}) collective-permute-start(bf16[64,2944]{1,0:T(8,128)(2,1)S(1)} %get-tuple-element.146.own_ref), channel_id=1, source_target_pairs={{0,1},{1,0},{2,6},{3,7},{4,5},{5,4},{6,2},{7,3},{8,9},{9,8},{10,14... | collective-permute-start | bytes 1130504 | tf_op jit(solution)/shard_map/ppermute | solution.py:315
  23.2 1.7 %collective-permute-start.10 = (bf16[320,512]{1,0:T(8,128)(2,1)S(1)}, bf16[320,512]{1,0:T(8,128)(2,1)S(1)}, u32[]{:S(2)}, u32[]{:S(2)}) collective-permute-start(bf16[320,512]{1,0:T(8,128)(2,1)S(1)} %get-tuple-element.136), channel_id=1, source_target_pairs={{0,2},{1,3},{2,0},{3,1},{4,6},{5,7},{6,4},{7,5},{8,10},{9,11},{10,... | collective-permute-start | bytes 983048 | tf_op jit(solution)/shard_map/ppermute | solution.py:315
  23.4 10.0 %collective-permute-start.8 = (bf16[64,2944]{1,0:T(8,128)(2,1)S(1)}, bf16[64,2944]{1,0:T(8,128)(2,1)S(1)}, u32[]{:S(2)}, u32[]{:S(2)}) collective-permute-start(bf16[64,2944]{1,0:T(8,128)(2,1)S(1)} %get-tuple-element.144.own_ref), channel_id=1, source_target_pairs={{0,1},{1,0},{2,6},{3,7},{4,5},{5,4},{6,2},{7,3},{8,9},{9,8},{10,14... | collective-permute-start | bytes 1130504 | tf_op jit(solution)/shard_map/ppermute | solution.py:315
  24.9 12.6 %collective-permute-start.11 = (bf16[2,2,8,2944]{3,2,1,0:T(8,128)(2,1)S(1)}, bf16[2,2,8,2944]{3,2,1,0:T(8,128)(2,1)S(1)}, u32[]{:S(2)}, u32[]{:S(2)}) collective-permute-start(bf16[2,2,8,2944]{3,2,1,0:T(8,128)(2,1)S(1)} %copy_select_fusion.1), channel_id=1, source_target_pairs={{0,8},{1,9},{2,10},{3,11},{4,12},{5,13},{6,14},{7,15},{8,16},{9,17... | collective-permute-start | bytes 565256 | tf_op jit(solution)/shard_map/ppermute | solution.py:315
  29.5 14.3 %collective-permute-start.12 = (bf16[2,2,8,2944]{3,2,1,0:T(8,128)(2,1)S(1)}, bf16[2,2,8,2944]{3,2,1,0:T(8,128)(2,1)S(1)}, u32[]{:S(2)}, u32[]{:S(2)}) collective-permute-start(bf16[2,2,8,2944]{3,2,1,0:T(8,128)(2,1)S(1)} %copy_select_fusion.1), channel_id=1, source_target_pairs={{0,16},{1,17},{2,18},{3,19},{4,20},{5,21},{6,22},{7,23},{8,24},{9,... | collective-permute-start | bytes 565256 | tf_op jit(solution)/shard_map/ppermute | solution.py:315
  31.1 12.8 %collective-permute-start.13 = (bf16[2,2,8,2944]{3,2,1,0:T(8,128)(2,1)S(1)}, bf16[2,2,8,2944]{3,2,1,0:T(8,128)(2,1)S(1)}, u32[]{:S(2)}, u32[]{:S(2)}) collective-permute-start(bf16[2,2,8,2944]{3,2,1,0:T(8,128)(2,1)S(1)} %copy_select_fusion.1), channel_id=1, source_target_pairs={{0,24},{1,25},{2,26},{3,27},{4,28},{5,29},{6,30},{7,31},{8,0},{9,1... | collective-permute-start | bytes 565256 | tf_op jit(solution)/shard_map/ppermute | solution.py:315
  32.0 2.9 %collective-permute-start.9 = (bf16[1,18,32,640]{3,2,1,0:T(8,128)(2,1)S(1)}, bf16[1,18,32,640]{3,2,1,0:T(8,128)(2,1)S(1)}, u32[]{:S(2)}, u32[]{:S(2)}) collective-permute-start(bf16[1,18,32,640]{3,2,1,0:T(8,128)(2,1)S(1)} %pad_maximum_fusion.6), channel_id=1, source_target_pairs={{0,2},{1,3},{2,0},{3,1},{4,6},{5,7},{6,4},{7,5},{8,10},{9,11},{10,... | collective-permute-start | bytes 2211848 | tf_op jit(solution)/shard_map/ppermute | solution.py:315
  33.3 11.6 %collective-permute-start.7 = (bf16[2,64,2944]{2,1,0:T(8,128)(2,1)S(1)}, bf16[2,64,2944]{2,1,0:T(8,128)(2,1)S(1)}, u32[]{:S(2)}, u32[]{:S(2)}) collective-permute-start(bf16[2,64,2944]{2,1,0:T(8,128)(2,1)S(1)} %pad_maximum_fusion.3), channel_id=1, source_target_pairs={{0,4},{1,5},{2,3},{3,2},{4,0},{5,1},{6,7},{7,6},{8,12},{9,13},{10,... | collective-permute-start | bytes 2261000 | tf_op jit(solution)/shard_map/ppermute | solution.py:315
  34.9 24.3 %collective-permute-start.15 = (bf16[2,64,2944]{2,1,0:T(8,128)(2,1)S(1)}, bf16[2,64,2944]{2,1,0:T(8,128)(2,1)S(1)}, u32[]{:S(2)}, u32[]{:S(2)}) collective-permute-start(bf16[2,64,2944]{2,1,0:T(8,128)(2,1)S(1)} %pad_maximum_fusion.5), channel_id=1, source_target_pairs={{0,4},{1,5},{2,3},{3,2},{4,0},{5,1},{6,7},{7,6},{8,12},{9,13},{10,... | collective-permute-start | bytes 2261000 | tf_op jit(solution)/shard_map/ppermute | solution.py:315
  52.9 13.8 %collective-permute-start.14 = (bf16[2,64,2944]{2,1,0:T(8,128)(2,1)S(1)}, bf16[2,64,2944]{2,1,0:T(8,128)(2,1)S(1)}, u32[]{:S(2)}, u32[]{:S(2)}) collective-permute-start(bf16[2,64,2944]{2,1,0:T(8,128)(2,1)S(1)} %get-tuple-element.89), channel_id=1, source_target_pairs={{0,4},{1,5},{2,3},{3,2},{4,0},{5,1},{6,7},{7,6},{8,12},{9,13},{10,... | collective-permute-start | bytes 2261000 | tf_op jit(solution)/shard_map/ppermute | solution.py:315
  54.6 12.0 %collective-permute-start.16 = (bf16[2,2,2,8,2944]{4,3,2,1,0:T(8,128)(2,1)S(1)}, bf16[2,2,2,8,2944]{4,3,2,1,0:T(8,128)(2,1)S(1)}, u32[]{:S(2)}, u32[]{:S(2)}) collective-permute-start(bf16[2,2,2,8,2944]{4,3,2,1,0:T(8,128)(2,1)S(1)} %maximum_select_fusion), channel_id=1, source_target_pairs={{0,8},{1,9},{2,10},{3,11},{4,12},{5,13},{6,14},{7,15},{8,0},{9,1},... | collective-permute-start | bytes 1130504 | tf_op jit(solution)/shard_map/ppermute | solution.py:315
  65.9 19.3 %collective-permute-start.18 = (bf16[2,64,2944]{2,1,0:T(8,128)(2,1)S(1)}, bf16[2,64,2944]{2,1,0:T(8,128)(2,1)S(1)}, u32[]{:S(2)}, u32[]{:S(2)}) collective-permute-start(bf16[2,64,2944]{2,1,0:T(8,128)(2,1)S(1)} %get-tuple-element.91), channel_id=1, source_target_pairs={{0,4},{1,5},{2,3},{3,2},{4,0},{5,1},{6,7},{7,6},{8,12},{9,13},{10,... | collective-permute-start | bytes 2261000 | tf_op jit(solution)/shard_map/ppermute | solution.py:315
  66.5 18.6 %collective-permute-start.20 = (bf16[320,512]{1,0:T(8,128)(2,1)S(1)}, bf16[320,512]{1,0:T(8,128)(2,1)S(1)}, u32[]{:S(2)}, u32[]{:S(2)}) collective-permute-start(bf16[320,512]{1,0:T(8,128)(2,1)S(1)} %slice.272), channel_id=1, source_target_pairs={{0,2},{1,3},{2,0},{3,1},{4,6},{5,7},{6,4},{7,5},{8,10},{9,11},{10,... | collective-permute-start | bytes 983048 | tf_op jit(solution)/shard_map/ppermute | solution.py:315
  66.7 18.5 %collective-permute-start.17 = (bf16[64,2944]{1,0:T(8,128)(2,1)S(1)}, bf16[64,2944]{1,0:T(8,128)(2,1)S(1)}, u32[]{:S(2)}, u32[]{:S(2)}) collective-permute-start(bf16[64,2944]{1,0:T(8,128)(2,1)S(1)} %fusion.9), channel_id=1, source_target_pairs={{0,1},{1,0},{2,6},{3,7},{4,5},{5,4},{6,2},{7,3},{8,9},{9,8},{10,14... | collective-permute-start | bytes 1130504 | tf_op jit(solution)/shard_map/ppermute | solution.py:315
  68.6 10.8 %collective-permute-start.19 = (bf16[2,1,32,320]{3,2,1,0:T(8,128)(2,1)S(1)}, bf16[2,1,32,320]{3,2,1,0:T(8,128)(2,1)S(1)}, u32[]{:S(2)}, u32[]{:S(2)}) collective-permute-start(bf16[2,1,32,320]{3,2,1,0:T(8,128)(2,1)S(1)} %slice_select_fusion), channel_id=1, source_target_pairs={{0,1},{1,0},{2,3},{3,2},{4,5},{5,4},{6,7},{7,6},{8,9},{9,8},{10,11... | collective-permute-start | bytes 122888 | tf_op jit(solution)/shard_map/ppermute | solution.py:244
  69.2 15.9 %collective-permute-start.21 = (bf16[2,2,8,2944]{3,2,1,0:T(8,128)(2,1)S(1)}, bf16[2,2,8,2944]{3,2,1,0:T(8,128)(2,1)S(1)}, u32[]{:S(2)}, u32[]{:S(2)}) collective-permute-start(bf16[2,2,8,2944]{3,2,1,0:T(8,128)(2,1)S(1)} %fusion.12), channel_id=1, source_target_pairs={{0,16},{1,17},{2,18},{3,19},{4,20},{5,21},{6,22},{7,23},{8,24},{9,... | collective-permute-start | bytes 565256 | tf_op jit(solution)/shard_map/ppermute | solution.py:315
  85.7 7.8 %collective-permute-start.22 = (bf16[2,16,2944]{2,1,0:T(8,128)(2,1)S(1)}, bf16[2,16,2944]{2,1,0:T(8,128)(2,1)S(1)}, u32[]{:S(2)}, u32[]{:S(2)}) collective-permute-start(bf16[2,16,2944]{2,1,0:T(8,128)(2,1)S(1)} %maximum_select_fusion.1), channel_id=1, source_target_pairs={{0,8},{1,9},{2,10},{3,11},{4,12},{5,13},{6,14},{7,15},{8,0},{9,1},... | collective-permute-start | bytes 565256 | tf_op jit(solution)/shard_map/ppermute | solution.py:315
  86.6 8.3 %collective-permute-start.24 = (bf16[64,2944]{1,0:T(8,128)(2,1)S(1)}, bf16[64,2944]{1,0:T(8,128)(2,1)S(1)}, u32[]{:S(2)}, u32[]{:S(2)}) collective-permute-start(bf16[64,2944]{1,0:T(8,128)(2,1)S(1)} %fusion.10), channel_id=1, source_target_pairs={{0,1},{1,0},{2,6},{3,7},{4,5},{5,4},{6,2},{7,3},{8,9},{9,8},{10,14... | collective-permute-start | bytes 1130504 | tf_op jit(solution)/shard_map/ppermute | solution.py:315
  87.7 5.7 %collective-permute-start.25 = (bf16[2,8,2944]{2,1,0:T(8,128)(2,1)S(1)}, bf16[2,8,2944]{2,1,0:T(8,128)(2,1)S(1)}, u32[]{:S(2)}, u32[]{:S(2)}) collective-permute-start(bf16[2,8,2944]{2,1,0:T(8,128)(2,1)S(1)} %fusion.17), channel_id=1, source_target_pairs={{0,4},{1,5},{2,3},{3,2},{4,0},{5,1},{6,7},{7,6},{8,12},{9,13},{10,... | collective-permute-start | bytes 282632 | tf_op jit(solution)/shard_map/ppermute | solution.py:315
  93.5 12.3 %collective-permute-start.23 = (bf16[16,2944]{1,0:T(8,128)(2,1)S(1)}, bf16[16,2944]{1,0:T(8,128)(2,1)S(1)}, u32[]{:S(2)}, u32[]{:S(2)}) collective-permute-start(bf16[16,2944]{1,0:T(8,128)(2,1)S(1)} %fusion.15), channel_id=1, source_target_pairs={{0,16},{1,17},{2,18},{3,19},{4,20},{5,21},{6,22},{7,23},{8,24},{9,... | collective-permute-start | bytes 282632 | tf_op jit(solution)/shard_map/ppermute | solution.py:315
  94.9 4.2 %collective-permute-start.26 = (bf16[8,2944]{1,0:T(8,128)(2,1)S(1)}, bf16[8,2944]{1,0:T(8,128)(2,1)S(1)}, u32[]{:S(2)}, u32[]{:S(2)}) collective-permute-start(bf16[8,2944]{1,0:T(8,128)(2,1)S(1)} %fusion.18), channel_id=1, source_target_pairs={{0,1},{1,0},{2,6},{3,7},{4,5},{5,4},{6,2},{7,3},{8,9},{9,8},{10,14... | collective-permute-start | bytes 141320 | tf_op jit(solution)/shard_map/ppermute | solution.py:315
  95.4 9.5 %collective-permute-start.27 = (f32[512,640]{1,0:T(8,128)S(1)}, f32[512,640]{1,0:T(8,128)S(1)}, u32[]{:S(2)}, u32[]{:S(2)}) collective-permute-start(f32[512,640]{1,0:T(8,128)S(1)} %shard_map.122), channel_id=1, source_target_pairs={{0,2},{1,3},{2,0},{3,1},{4,6},{5,7},{6,4},{7,5},{8,10},{9,11},{10,... | collective-permute-start | bytes 3932168 | tf_op jit(solution)/shard_map/ppermute | solution.py:315
  95.7 7.5 %collective-permute-start.28 = (bf16[2,16,2944]{2,1,0:T(8,128)(2,1)S(1)}, bf16[2,16,2944]{2,1,0:T(8,128)(2,1)S(1)}, u32[]{:S(2)}, u32[]{:S(2)}) collective-permute-start(bf16[2,16,2944]{2,1,0:T(8,128)(2,1)S(1)} %maximum_select_fusion.2), channel_id=1, source_target_pairs={{0,8},{1,9},{2,10},{3,11},{4,12},{5,13},{6,14},{7,15},{8,0},{9,1},... | collective-permute-start | bytes 565256 | tf_op jit(solution)/shard_map/ppermute | solution.py:315
  103.1 7.4 %collective-permute-start.29 = (bf16[16,2944]{1,0:T(8,128)(2,1)S(1)}, bf16[16,2944]{1,0:T(8,128)(2,1)S(1)}, u32[]{:S(2)}, u32[]{:S(2)}) collective-permute-start(bf16[16,2944]{1,0:T(8,128)(2,1)S(1)} %fusion.14), channel_id=1, source_target_pairs={{0,16},{1,17},{2,18},{3,19},{4,20},{5,21},{6,22},{7,23},{8,24},{9,... | collective-permute-start | bytes 282632 | tf_op jit(solution)/shard_map/ppermute | solution.py:315
  104.8 1.1 copy-start.2
  104.9 1.4 %copy-start.3 = (f32[9,320,40]{1,2,0:T(8,128)S(1)}, f32[9,320,40]{1,2,0:T(8,128)}, u32[]{:S(2)}) copy-start(f32[9,320,40]{1,2,0:T(8,128)} %param.11) | copy-start | bytes 1382404
  104.9 1.6 %copy-start.4 = (f32[9,320,40]{1,2,0:T(8,128)S(1)}, f32[9,320,40]{1,2,0:T(8,128)}, u32[]{:S(2)}) copy-start(f32[9,320,40]{1,2,0:T(8,128)} %param.12) | copy-start | bytes 1382404
